TPU v7x, 768 devices: a whole 4x8x12 slice. The times are simulated.
768 devices in a mesh: blk: 96 (over y_lo, z, core), grp: 8 (over y_hi, x).
Axes of the slice: x: 4, y: 8 (y_hi: 2, y_lo: 4; y = y_hi * 4 + y_lo), z: 12, core: 2. Of those that a mesh axis runs over, the one named last changes fastest.
Arguments:
- three_index: bfloat16 [23552, 24576], P('grp', 'blk'), may hold values from -0.359375 to 0.359375
- occ_energy: float32 [384], P('blk'), may hold values from -2 to -0.3
- vir_energy: float32 [64], replicated, may hold values from 0.2 to 3
- aux_count: int32 [8], replicated, may hold values from 1 to 2944, 22528 in all
- occ_count: int32 [96], replicated, may hold values from 1 to 4, 192 in all
Outputs:
- gamma: bfloat16 [23552, 24576], P('grp', 'blk')
Inputs may be any that keep to these rules, and one draw needn't show every extreme that they name: `aux_count`: the 8 counts sum to 22528; the largest is exactly 2944. `occ_count`: the 96 counts sum to 192; the largest is exactly 4.
All inputs are finite; a program needn't handle non-finite values.
Results may differ from a plain program's by a relative error of at most 0.018.
Values may be sent and summed in bfloat16 or wider, within the bound.
No kernel may reach another device: no remote copies, remote signals or barrier semaphores. Data moves between devices by JAX's collectives and lax.ppermute only.
A program may use at most 32 MiB of HBM per device.

v0:
```python
import jax
import jax.numpy as jnp
from jax import lax
from jax.sharding import PartitionSpec as P

contract_first = (((0,), (0,)), ((), ()))
contract_last = (((1,), (1,)), ((), ()))


def from_behind(value, axis, steps):
    count = lax.axis_size(axis)
    pairs = [(source, (source + steps) % count) for source in range(count)]
    return lax.ppermute(value, axis, pairs)


def slab_columns(slab_energy, slab_total, vir_energy):
    columns = slab_energy.shape[0] * vir_energy.shape[0]
    col_gap = (slab_energy[:, None] - vir_energy[None, :]).reshape(columns)
    col_live = jnp.repeat(jnp.arange(slab_energy.shape[0]) < slab_total, vir_energy.shape[0])
    return (col_gap, col_live)


def divide_block(pair_block, gap_rows, gap_cols, live_rows, live_cols):
    quotient = pair_block / (gap_rows[:, None] + gap_cols[None, :])
    return jnp.where(live_rows[:, None] & live_cols[None, :], quotient, 0.0).astype(jnp.bfloat16)


def amplitudes(resident, visitor, gap_rows, gap_cols, live_rows, live_cols):
    partial_pair = lax.dot_general(
        resident, visitor, contract_first, preferred_element_type=jnp.float32
    )
    summed = lax.psum(partial_pair.astype(jnp.bfloat16), "grp").astype(jnp.float32)
    return divide_block(summed, gap_rows, gap_cols, live_rows, live_cols)


def per_device(three_index, occ_energy, vir_energy, aux_count, occ_count):
    slot_count = three_index.shape[0]
    cycle_size = lax.axis_size("blk")
    position = lax.axis_index("blk")
    aux_live = jnp.arange(slot_count) < aux_count[lax.axis_index("grp")]
    resident = jnp.where(aux_live[:, None], three_index, jnp.zeros((), jnp.bfloat16))
    gap_home, live_home = slab_columns(occ_energy, occ_count[position], vir_energy)
    amplitude = amplitudes(resident, resident, gap_home, gap_home, live_home, live_home)
    accumulated = lax.dot_general(
        resident, amplitude, contract_last, preferred_element_type=jnp.float32
    )
    slab_block, slab_energy = (resident, occ_energy)
    for offset in (1, 2):
        slab_block, slab_energy = (
            from_behind(slab_block, "blk", -1),
            from_behind(slab_energy.astype(jnp.bfloat16), "blk", -1).astype(slab_energy.dtype),
        )
        col_gap, col_live = slab_columns(
            slab_energy, occ_count[(position + offset) % cycle_size], vir_energy
        )
        amplitude = amplitudes(resident, slab_block, gap_home, col_gap, live_home, col_live)
        accumulated = accumulated + lax.dot_general(
            slab_block, amplitude, contract_last, preferred_element_type=jnp.float32
        )
        returned = jnp.dot(resident, amplitude, preferred_element_type=jnp.float32).astype(
            jnp.bfloat16
        )
        arrived = from_behind(returned, "blk", offset)
        accumulated = accumulated + arrived.astype(jnp.float32)
    return accumulated.astype(jnp.bfloat16)


def solution(mesh):
    in_specs = (P("grp", "blk"), P("blk"), P(), P(), P())
    out_specs = P("grp", "blk")
    return jax.shard_map(
        per_device, mesh=mesh, in_specs=in_specs, out_specs=out_specs, check_vma=False
    )
```

profile of v0, /device:TPU:1, one launch (start us, length us, event | category | flops | bytes accessed | tf_op | source)
XLA Modules:
  0.0 254.0 jit_solution(15697799780906908950)
XLA Ops:
  6.5 0.0 all-reduce.3.cloned.1.call-start
  6.5 1.2 dynamic_slice.12
  7.8 0.7 iota_compare_fusion
  8.4 0.0 copy-start.4
  8.4 0.0 copy-start.3
  8.5 2.6 %broadcast_select_fusion = bf16[2944,256]{1,0:T(8,128)(2,1)S(1)} fusion(bf16[2944,256]{1,0:T(8,128)(2,1)} %param.5, pred[2944]{0:T(1024)(128)(4,1)S(1)} %iota_compare_fusion), kind=kLoop, calls=%fused_computation.7 | loop fusion | flops 753664 | bytes 3017600 | tf_op jit(solution)/shard_map/jit(_where)/select_n | solution.py:41
  11.1 12.4 %collective-permute-start = (bf16[2944,256]{1,0:T(8,128)(2,1)S(1)}, bf16[2944,256]{1,0:T(8,128)(2,1)}, u32[]{:S(2)}, u32[]{:S(2)}) collective-permute-start(bf16[2944,256]{1,0:T(8,128)(2,1)S(1)} %broadcast_select_fusion), channel_id=1, source_target_pairs={{0,760},{8,0},{16,8},{24,16},{32,24},{40,32},{48,40},{56,48},{64,5... | collective-permute-start | bytes 4521992 | tf_op jit(solution)/shard_map/ppermute | solution.py:13
  23.5 10.5 %collective-permute-done = bf16[2944,256]{1,0:T(8,128)(2,1)} collective-permute-done((bf16[2944,256]{1,0:T(8,128)(2,1)S(1)}, bf16[2944,256]{1,0:T(8,128)(2,1)}, u32[]{:S(2)}, u32[]{:S(2)}) %collective-permute-start) | collective-permute-done | bytes 1507360 | tf_op jit(solution)/shard_map/ppermute | solution.py:13
  34.0 14.8 %collective-permute-start.3 = (bf16[2944,256]{1,0:T(8,128)(2,1)}, bf16[2944,256]{1,0:T(8,128)(2,1)S(1)}, u32[]{:S(2)}, u32[]{:S(2)}) collective-permute-start(bf16[2944,256]{1,0:T(8,128)(2,1)} %collective-permute-done), channel_id=1, source_target_pairs={{0,760},{8,0},{16,8},{24,16},{32,24},{40,32},{48,40},{56,48},{64,5... | collective-permute-start | bytes 4521992 | tf_op jit(solution)/shard_map/ppermute | solution.py:13
  48.8 0.0 copy-done.4
  48.8 7.8 %collective-permute-start.1 = (bf16[4]{0:T(256)(128)(2,1)S(1)}, bf16[4]{0:T(256)(128)(2,1)S(1)}, u32[]{:S(2)}, u32[]{:S(2)}) collective-permute-start(bf16[4]{0:T(256)(128)(2,1)S(1)} %convert_element_type.57), channel_id=1, source_target_pairs={{0,760},{8,0},{16,8},{24,16},{32,24},{40,32},{48,40},{56,48},{64,5... | collective-permute-start | bytes 32 | tf_op jit(solution)/shard_map/ppermute | solution.py:13
  56.7 0.0 copy-done.3
  56.7 0.7 fusion.10
  57.4 1.3 convolution_convert_fusion.4
  58.7 2.6 %convolution_convert_fusion.3 = bf16[256,256]{1,0:T(8,128)(2,1)} fusion(bf16[2944,256]{1,0:T(8,128)(2,1)S(1)} %broadcast_select_fusion, bf16[2944,256]{1,0:T(8,128)(2,1)} %collective-permute-done), kind=kOutput, calls=%fused_computation.9 | convolution fusion | flops 385941504 | bytes 3145728 | tf_op jit(solution)/shard_map/dot_general | solution.py:29
  61.3 0.0 copy-start.5
  61.3 0.0 collective-permute-done.3
  61.3 1.3 convolution_convert_fusion.2
  62.6 0.0 all-reduce.3.cloned.1.call-update
  62.6 0.5 iota_compare_fusion.3
  63.2 0.1 broadcast_in_dim.36
  63.3 0.1 and.49
  63.4 0.7 iota_compare_fusion.2
  64.1 0.1 broadcast_in_dim.38
  64.1 0.1 and.54
  64.2 0.0 collective-permute-done.1
  64.2 12.8 %collective-permute-start.4 = (bf16[4]{0:T(256)(128)(2,1)S(1)}, bf16[4]{0:T(256)(128)(2,1)S(1)}, u32[]{:S(2)}, u32[]{:S(2)}) collective-permute-start(bf16[4]{0:T(256)(128)(2,1)S(1)} %collective-permute-done.1), channel_id=1, source_target_pairs={{0,760},{8,0},{16,8},{24,16},{32,24},{40,32},{48,40},{56,48},{64,5... | collective-permute-start | bytes 32 | tf_op jit(solution)/shard_map/ppermute | solution.py:13
  77.1 0.8 collective-permute-done.4
  77.8 0.0 copy-done.5
  77.8 0.1 broadcast_subtract_fusion
  77.9 0.1 sub.63
  78.0 0.1 sub.66
  78.1 101.9 %all-reduce.3.cloned.1.call-done = (bf16[256,256]{1,0:T(8,128)(2,1)}, bf16[256,256]{1,0:T(8,128)(2,1)}, bf16[256,256]{1,0:T(8,128)(2,1)}) async-done(((bf16[256,256]{1,0:T(8,128)(2,1)}, bf16[256,256]{1,0:T(8,128)(2,1)}, bf16[256,256]{1,0:T(8,128)(2,1)}), (bf16[256,256]{1,0:T(8,128)(2,1)}, bf16[256,256]{1,0:T(8,128)(2,1)}, bf16[256,256]{1,0:T(8,128)(2,1)})) %all-reduce.3.cloned.1.call-update) | async-done | bytes 393232 | tf_op jit(solution)/shard_map/psum | solution.py:32
  180.0 0.0 copy-start
  180.0 2.7 %convolution_convert_fusion.1 = bf16[2944,256]{1,0:T(8,128)(2,1)} fusion(bf16[2944,256]{1,0:T(8,128)(2,1)S(1)} %broadcast_select_fusion, bf16[256,256]{1,0:T(8,128)(2,1)} %get-tuple-element.6, f32[256]{0:T(256)S(1)} %sub.66, f32[256]{0:T(256)S(1)} %sub.63, pred[256]{0:T(512)(128)(4,1)S(1)} %and.54, pred[256]{0:T(512)(128)(4,1)S(1)} %and.49), kind=kOutput, calls=%fused_computation.6 | convolution fusion | flops 387022848 | bytes 3148288 | tf_op jit(solution)/shard_map/dot_general | solution.py:60
  182.7 9.0 %collective-permute-start.2 = (bf16[2944,256]{1,0:T(8,128)(2,1)}, bf16[2944,256]{1,0:T(8,128)(2,1)}, u32[]{:S(2)}, u32[]{:S(2)}) collective-permute-start(bf16[2944,256]{1,0:T(8,128)(2,1)} %convolution_convert_fusion.1), channel_id=1, source_target_pairs={{0,8},{8,16},{16,24},{24,32},{32,40},{40,48},{48,56},{56,64},{64,7... | collective-permute-start | bytes 4521992 | tf_op jit(solution)/shard_map/ppermute | solution.py:13
  191.7 0.7 iota_compare_fusion.1
  192.4 0.1 broadcast_in_dim.39
  192.4 0.1 and.58
  192.5 0.1 sub.69
  192.6 0.0 copy-done
  192.6 0.0 copy-start.2
  192.6 0.7 convolution_convert_fusion
  193.3 3.3 %collective-permute-start.5 = (bf16[2944,256]{1,0:T(8,128)(2,1)S(1)}, bf16[2944,256]{1,0:T(8,128)(2,1)S(1)}, u32[]{:S(2)}, u32[]{:S(2)}) collective-permute-start(bf16[2944,256]{1,0:T(8,128)(2,1)S(1)} %convolution_convert_fusion), channel_id=1, source_target_pairs={{0,16},{8,24},{16,32},{24,40},{32,48},{40,56},{48,64},{56,72},{64,... | collective-permute-start | bytes 4521992 | tf_op jit(solution)/shard_map/ppermute | solution.py:13
  196.6 0.0 copy-done.2
  196.6 0.0 copy-start.1
  196.6 0.7 fusion.3
  197.2 23.6 %collective-permute-done.2 = bf16[2944,256]{1,0:T(8,128)(2,1)} collective-permute-done((bf16[2944,256]{1,0:T(8,128)(2,1)}, bf16[2944,256]{1,0:T(8,128)(2,1)}, u32[]{:S(2)}, u32[]{:S(2)}) %collective-permute-start.2) | collective-permute-done | bytes 1507360 | tf_op jit(solution)/shard_map/ppermute | solution.py:13
  220.8 0.0 copy-done.1
  220.8 2.6 %fusion.1 = f32[2944,256]{1,0:T(8,128)S(1)} fusion(f32[2944,256]{1,0:T(8,128)S(1)} %fusion.3, bf16[2944,256]{1,0:T(8,128)(2,1)} %collective-permute-done, bf16[2944,256]{1,0:T(8,128)(2,1)} %collective-permute-done.2, bf16[256,256]{1,0:T(8,128)(2,1)S(1)} %copy-done.1, f32[256]{0:T(256)S(1)} %sub.66, f32[256]{0:T(256)S(1)} %sub.63, ...), kind=kOutput, calls=%fused_computation.3 | convolution fusion | flops 388530176 | bytes 9177600 | tf_op jit(solution)/shard_map/dot_general | solution.py:57
  223.4 21.8 %collective-permute-done.5 = bf16[2944,256]{1,0:T(8,128)(2,1)S(1)} collective-permute-done((bf16[2944,256]{1,0:T(8,128)(2,1)S(1)}, bf16[2944,256]{1,0:T(8,128)(2,1)S(1)}, u32[]{:S(2)}, u32[]{:S(2)}) %collective-permute-start.5) | collective-permute-done | bytes 1507360 | tf_op jit(solution)/shard_map/ppermute | solution.py:13
  245.3 1.9 fusion.2
  (3 shorter events, 0.0 us)
Async XLA Ops:
  6.5 173.4 %all-reduce.3.cloned.1.call-start = ((), (), s32[]{:S(2)}) async-start(), calls=%async_computation | async-start | bytes 786432 | tf_op jit(solution)/shard_map/psum | solution.py:32
  8.4 40.4 %copy-start.4 = (f32[4]{0:T(128)S(1)}, f32[4]{0:T(128)}, u32[]{:S(2)}) copy-start(f32[4]{0:T(128)} %param.6) | copy-start | bytes 52
  8.4 48.3 %copy-start.3 = (s32[96]{0:T(128)S(1)}, s32[96]{0:T(128)}, u32[]{:S(2)}) copy-start(s32[96]{0:T(128)} %param.9) | copy-start | bytes 1156
  11.1 22.9 %collective-permute-start = (bf16[2944,256]{1,0:T(8,128)(2,1)S(1)}, bf16[2944,256]{1,0:T(8,128)(2,1)}, u32[]{:S(2)}, u32[]{:S(2)}) collective-permute-start(bf16[2944,256]{1,0:T(8,128)(2,1)S(1)} %broadcast_select_fusion), channel_id=1, source_target_pairs={{0,760},{8,0},{16,8},{24,16},{32,24},{40,32},{48,40},{56,48},{64,5... | collective-permute-start | bytes 4521992 | tf_op jit(solution)/shard_map/ppermute | solution.py:13
  34.0 27.3 %collective-permute-start.3 = (bf16[2944,256]{1,0:T(8,128)(2,1)}, bf16[2944,256]{1,0:T(8,128)(2,1)S(1)}, u32[]{:S(2)}, u32[]{:S(2)}) collective-permute-start(bf16[2944,256]{1,0:T(8,128)(2,1)} %collective-permute-done), channel_id=1, source_target_pairs={{0,760},{8,0},{16,8},{24,16},{32,24},{40,32},{48,40},{56,48},{64,5... | collective-permute-start | bytes 4521992 | tf_op jit(solution)/shard_map/ppermute | solution.py:13
  48.8 15.4 %collective-permute-start.1 = (bf16[4]{0:T(256)(128)(2,1)S(1)}, bf16[4]{0:T(256)(128)(2,1)S(1)}, u32[]{:S(2)}, u32[]{:S(2)}) collective-permute-start(bf16[4]{0:T(256)(128)(2,1)S(1)} %convert_element_type.57), channel_id=1, source_target_pairs={{0,760},{8,0},{16,8},{24,16},{32,24},{40,32},{48,40},{56,48},{64,5... | collective-permute-start | bytes 32 | tf_op jit(solution)/shard_map/ppermute | solution.py:13
  61.3 16.5 %copy-start.5 = (f32[64]{0:T(128)S(1)}, f32[64]{0:T(128)}, u32[]{:S(2)}) copy-start(f32[64]{0:T(128)} %param.7) | copy-start | bytes 772
  64.2 13.6 %collective-permute-start.4 = (bf16[4]{0:T(256)(128)(2,1)S(1)}, bf16[4]{0:T(256)(128)(2,1)S(1)}, u32[]{:S(2)}, u32[]{:S(2)}) collective-permute-start(bf16[4]{0:T(256)(128)(2,1)S(1)} %collective-permute-done.1), channel_id=1, source_target_pairs={{0,760},{8,0},{16,8},{24,16},{32,24},{40,32},{48,40},{56,48},{64,5... | collective-permute-start | bytes 32 | tf_op jit(solution)/shard_map/ppermute | solution.py:13
  180.0 12.6 %copy-start = (bf16[256,256]{1,0:T(8,128)(2,1)S(1)}, bf16[256,256]{1,0:T(8,128)(2,1)}, u32[]{:S(2)}) copy-start(bf16[256,256]{1,0:T(8,128)(2,1)} %get-tuple-element.7) | copy-start | bytes 393220
  182.7 38.1 %collective-permute-start.2 = (bf16[2944,256]{1,0:T(8,128)(2,1)}, bf16[2944,256]{1,0:T(8,128)(2,1)}, u32[]{:S(2)}, u32[]{:S(2)}) collective-permute-start(bf16[2944,256]{1,0:T(8,128)(2,1)} %convolution_convert_fusion.1), channel_id=1, source_target_pairs={{0,8},{8,16},{16,24},{24,32},{32,40},{40,48},{48,56},{56,64},{64,7... | collective-permute-start | bytes 4521992 | tf_op jit(solution)/shard_map/ppermute | solution.py:13
  192.6 3.9 %copy-start.2 = (bf16[256,256]{1,0:T(8,128)(2,1)S(1)}, bf16[256,256]{1,0:T(8,128)(2,1)}, u32[]{:S(2)}) copy-start(bf16[256,256]{1,0:T(8,128)(2,1)} %get-tuple-element.5) | copy-start | bytes 393220
  193.3 52.0 %collective-permute-start.5 = (bf16[2944,256]{1,0:T(8,128)(2,1)S(1)}, bf16[2944,256]{1,0:T(8,128)(2,1)S(1)}, u32[]{:S(2)}, u32[]{:S(2)}) collective-permute-start(bf16[2944,256]{1,0:T(8,128)(2,1)S(1)} %convolution_convert_fusion), channel_id=1, source_target_pairs={{0,16},{8,24},{16,32},{24,40},{32,48},{40,56},{48,64},{56,72},{64,... | collective-permute-start | bytes 4521992 | tf_op jit(solution)/shard_map/ppermute | solution.py:13
  196.6 24.2 %copy-start.1 = (bf16[256,256]{1,0:T(8,128)(2,1)S(1)}, bf16[256,256]{1,0:T(8,128)(2,1)}, u32[]{:S(2)}) copy-start(bf16[256,256]{1,0:T(8,128)(2,1)} %get-tuple-element.6) | copy-start | bytes 393220
Sparse Core Ops, SparseCore 0:
  62.8 117.1 all-reduce.2
where the time goes:
time: 254 us
  waiting for transfers between devices  159 us (63%)
  starting transfers between devices  60.1 us (24%)
  matrix products  13.7 us (5%)
  between operations  13.6 us (5%)
  other arithmetic  5.31 us (2%)
  local copies, waits for them, and re-layouts  2.67 us (1%)
    psum x1, waiting for transfers between devices, amplitudes(): lax.psum(partial_pair.astype(jnp.bfloat16), 'grp').astype(jnp.float32)  102 us
    ppermute x6, starting transfers between devices, from_behind(): return lax.ppermute(value, axis, pairs)  60.1 us
    ppermute x6, waiting for transfers between devices, from_behind(): return lax.ppermute(value, axis, pairs)  56.6 us
    dot_general x3, matrix products, amplitudes(): lax.dot_general(resident, visitor, contract_first, preferred_element_type...  5.21 us
  transfers between devices with their start and end apart: 7, of which 5 were waited for; matrix products, arithmetic and copies ran while one was open for 5% of the time, Pallas kernels for 0%

commit v1 on v0

v1 whole, which is shorter than its diff:
```python
import jax
import jax.numpy as jnp
from jax import lax
from jax.experimental import pallas as pl
from jax.experimental.pallas import tpu as pltpu
from jax.sharding import PartitionSpec as P


BF = jnp.bfloat16
F32 = jnp.float32
first = (((0,), (0,)), ((), ()))
last = (((1,), (1,)), ((), ()))


def dot0(a, b):
    return lax.dot_general(a, b, first, preferred_element_type=F32)


def keep_rows(block, start, count):
    row = lax.broadcasted_iota(jnp.int32, block.shape, 0) + start
    return jnp.where(row < count, block, jnp.zeros((), block.dtype))


def near_kernel(sc, o_ref, p_ref, out_ref, acc):
    step = pl.program_id(0)
    tile = o_ref.shape[0]

    @pl.when(step == 0)
    def _():
        acc[...] = jnp.zeros_like(acc)

    own = keep_rows(o_ref[...], step * tile, sc[0])
    acc[0] += dot0(own, own)
    acc[1] += dot0(p_ref[...], own)

    @pl.when(step == pl.num_programs(0) - 1)
    def _():
        for j in range(2):
            out_ref[:, j] = acc[j].reshape(out_ref.shape[0], *out_ref.shape[2:]).astype(BF)


def far_kernel(half, sc, n_ref, m_ref, o0_ref, o1_ref, p0_ref, p1_ref, out_ref, acc):
    step = pl.program_id(0)
    tile = n_ref.shape[0]

    @pl.when(step == 0)
    def _():
        acc[...] = jnp.zeros_like(acc)

    own0 = keep_rows(o0_ref[...], step * tile, sc[0])
    own1 = keep_rows(o1_ref[...], half + step * tile, sc[0])
    acc[0] += dot0(n_ref[...], own0)
    acc[1] += dot0(own1, m_ref[...])

    @pl.when(sc[1] == 0)
    def _():
        acc[2] += dot0(n_ref[...], keep_rows(p0_ref[...], step * tile, sc[0]))

    @pl.when(sc[1] == 1)
    def _():
        acc[2] += dot0(keep_rows(p1_ref[...], half + step * tile, sc[0]), m_ref[...])

    @pl.when(step == pl.num_programs(0) - 1)
    def _():
        for j in range(3):
            out_ref[:, j] = acc[j].reshape(out_ref.shape[0], *out_ref.shape[2:]).astype(BF)


def three_terms(value):
    hi = value.astype(BF)
    rest = value - hi.astype(F32)
    mid = rest.astype(BF)
    low = (rest - mid.astype(F32)).astype(BF)
    return hi.astype(F32), mid.astype(F32), low.astype(F32)


def divide(pair, gap_rows, gap_cols, row_live, col_count, vir_count):
    col = lax.broadcasted_iota(jnp.int32, pair.shape, 1)
    keep = (col < col_count * vir_count) & row_live
    return jnp.where(keep, pair / (gap_rows + gap_cols), 0.0).astype(BF)


def near_amplitude_kernel(nv, sc, parts_ref, gaps_ref, vir_ref, out_ref, head_ref):
    total = jnp.sum(parts_ref[...].astype(F32), axis=0)
    vir = vir_ref[...]
    for j in range(2):
        rows = gaps_ref[2 + j:3 + j, :] - vir
        amp = divide(total[j], rows, gaps_ref[0:1, :], sc[2] < sc[3 + j], sc[3], nv)
        for g in range(out_ref.shape[0]):
            out_ref[g, j] = amp
    rows = []
    for j in range(4):
        rows += three_terms(gaps_ref[j:j + 1, :])
    rows.append(jnp.zeros((4, gaps_ref.shape[1]), F32))
    head_ref[...] = jnp.concatenate(rows, axis=0).astype(BF)


def pack_kernel(parts_ref, head_ref, sum_ref, up_ref, down_ref, swap_ref):
    total = jnp.sum(parts_ref[...].astype(F32), axis=0)
    sum_ref[...] = total[:2]
    extra = total[2].astype(BF)
    size = extra.shape[0]
    swap_ref[...] = extra
    for j, ref in ((0, up_ref), (1, down_ref)):
        ref[0:size, :] = total[j].astype(BF)
        ref[size:2 * size, :] = extra
        ref[2 * size:, :] = head_ref[...]


def far_amplitude_kernel(nv, sc, sum_ref, above_ref, below_ref, swap_ref, gaps_ref, vir_ref, out_ref):
    vir = vir_ref[...]
    size = vir.shape[0]
    own_gap = gaps_ref[0:1, :]
    own_rows = gaps_ref[2:3, :] - vir
    copies = range(out_ref.shape[0])

    def head(ref, row):
        block = ref[2 * size:, :].astype(F32)
        return block[3 * row:3 * row + 1] + block[3 * row + 1:3 * row + 2] + block[3 * row + 2:3 * row + 3]

    amp = divide(
        sum_ref[0] + above_ref[0:size, :].astype(F32), head(above_ref, 2) - vir, own_gap,
        sc[2] < sc[5], sc[3], nv,
    )
    for g in copies:
        out_ref[g, 0] = amp
    amp = divide(
        sum_ref[1] + below_ref[0:size, :].astype(F32), own_rows, head(below_ref, 0),
        sc[2] < sc[3], sc[6], nv,
    )
    for g in copies:
        out_ref[g, 1] = amp
    other = swap_ref[...].astype(F32)

    @pl.when(sc[1] == 0)
    def _():
        amp = divide(
            other + below_ref[size:2 * size, :].astype(F32), own_rows, head(below_ref, 1),
            sc[2] < sc[3], sc[7], nv,
        )
        for g in copies:
            out_ref[g, 2] = amp

    @pl.when(sc[1] == 1)
    def _():
        amp = divide(
            other + above_ref[size:2 * size, :].astype(F32), head(above_ref, 3) - vir, own_gap,
            sc[2] < sc[7], sc[3], nv,
        )
        for g in copies:
            out_ref[g, 2] = amp


def gamma_kernel(sc, near_ref, far_ref, o_ref, p_ref, n0_ref, n1_ref, m0_ref, m1_ref, x_ref, out_ref, acc):
    step = pl.program_id(0)
    tile = o_ref.shape[0]
    columns = o_ref.shape[1]

    def amp(ref, j):
        return ref[:, j].reshape(columns, columns)

    def times(block, matrix):
        return jnp.dot(block, matrix, preferred_element_type=F32)

    def times_t(block, matrix):
        return lax.dot_general(block, matrix, last, preferred_element_type=F32)

    acc[...] = times(o_ref[...], amp(near_ref, 0)) + times(p_ref[...], amp(near_ref, 1))
    lower = step < pl.num_programs(0) // 2

    @pl.when(lower)
    def _():
        acc[...] += times(n0_ref[...], amp(far_ref, 0)) + times_t(m0_ref[...], amp(far_ref, 1))

    @pl.when(jnp.logical_not(lower))
    def _():
        acc[...] += times(n1_ref[...], amp(far_ref, 0)) + times_t(m1_ref[...], amp(far_ref, 1))

    @pl.when(sc[1] == 0)
    def _():
        acc[...] += times_t(x_ref[...], amp(far_ref, 2))

    @pl.when(sc[1] == 1)
    def _():
        acc[...] += times(x_ref[...], amp(far_ref, 2))

    out_ref[...] = keep_rows(acc[...], step * tile, sc[0]).astype(out_ref.dtype)


def per_device(three_index, occ_energy, vir_energy, aux_count, occ_count):
    rows, cols = three_index.shape
    half = rows // 2
    nv = vir_energy.shape[0]
    slabs = lax.axis_size("blk")
    owners = lax.axis_size("grp")
    piece = cols // owners
    r = lax.axis_index("blk")
    g = lax.axis_index("grp")
    parity = r % 2

    def shift(value, steps):
        return lax.ppermute(value, "blk", [(i, (i + steps) % slabs) for i in range(slabs)])

    def swap(value):
        return lax.ppermute(value, "blk", [(i, i ^ 1) for i in range(slabs)])

    own = three_index
    n0 = shift(own[:half], -2)
    m1 = shift(own[half:], 2)
    partner = swap(own)
    n1 = shift(own[half:], -2)
    m0 = shift(own[:half], 2)

    partner_energy = swap(occ_energy)
    slot = (g * piece) // nv
    fifth = (r + jnp.where(parity == 0, -1, 1)) % slabs
    sc = jnp.stack([
        aux_count[g], parity, slot, occ_count[r], occ_count[r ^ 1],
        occ_count[(r + 2) % slabs], occ_count[(r - 2) % slabs], occ_count[fifth],
    ]).astype(jnp.int32)
    energies = jnp.stack([occ_energy, partner_energy])
    gap = (energies[:, :, None] - vir_energy[None, None, :]).reshape(2, cols)
    mine = jnp.broadcast_to(lax.dynamic_slice_in_dim(energies, slot, 1, 1), (2, cols))
    gaps = jnp.concatenate([gap, mine, jnp.zeros((4, cols), F32)], axis=0)
    vir = jnp.broadcast_to(
        lax.dynamic_slice_in_dim(vir_energy, (g * piece) % nv, piece, 0)[:, None], (piece, cols)
    )

    smem = pl.BlockSpec(memory_space=pltpu.SMEM)
    tiles = 4
    tile = rows // tiles
    ht = tiles // 2

    def whole(shape):
        return pl.BlockSpec(shape, lambda i: (0,) * len(shape))

    row_tile = pl.BlockSpec((tile, cols), lambda i: (i, 0))
    parts = (owners, 2, piece, cols)
    near = pl.pallas_call(
        near_kernel,
        grid=(tiles,),
        in_specs=[smem, row_tile, row_tile],
        out_specs=whole(parts),
        out_shape=jax.ShapeDtypeStruct(parts, BF),
        scratch_shapes=[pltpu.VMEM((2, cols, cols), F32)],
        cost_estimate=pl.CostEstimate(flops=4 * rows * cols * cols, bytes_accessed=4 * rows * cols, transcendentals=0),
        name="near",
    )(sc, own, partner)
    near = lax.all_to_all(near, "grp", 0, 0)
    vm = pl.BlockSpec(memory_space=pltpu.VMEM)
    near, head = pl.pallas_call(
        lambda *refs: near_amplitude_kernel(nv, *refs),
        in_specs=[smem, vm, vm, vm],
        out_specs=[vm, vm],
        out_shape=[jax.ShapeDtypeStruct(parts, BF), jax.ShapeDtypeStruct((16, cols), BF)],
        name="near_amplitude",
    )(sc, near, gaps, vir)
    near = lax.all_to_all(near, "grp", 0, 0)

    low_tile = pl.BlockSpec((tile, cols), lambda i: (i, 0))
    high_tile = pl.BlockSpec((tile, cols), lambda i: (i + ht, 0))
    parts3 = (owners, 3, piece, cols)
    far = pl.pallas_call(
        lambda *refs: far_kernel(half, *refs),
        grid=(ht,),
        in_specs=[smem, low_tile, low_tile, low_tile, high_tile, low_tile, high_tile],
        out_specs=whole(parts3),
        out_shape=jax.ShapeDtypeStruct(parts3, BF),
        scratch_shapes=[pltpu.VMEM((3, cols, cols), F32)],
        cost_estimate=pl.CostEstimate(flops=3 * rows * cols * cols, bytes_accessed=6 * rows * cols, transcendentals=0),
        name="far",
    )(sc, n0, m1, own, own, partner, partner)
    far = lax.all_to_all(far, "grp", 0, 0)
    message = jax.ShapeDtypeStruct((2 * piece + 16, cols), BF)
    sums, up, down, extra = pl.pallas_call(
        pack_kernel,
        in_specs=[vm, vm],
        out_specs=[vm] * 4,
        out_shape=[
            jax.ShapeDtypeStruct((2, piece, cols), F32), message, message,
            jax.ShapeDtypeStruct((piece, cols), BF),
        ],
        name="pack",
    )(far, head)
    below = shift(up, 2)
    above = shift(down, -2)
    extra = swap(extra)
    far = pl.pallas_call(
        lambda *refs: far_amplitude_kernel(nv, *refs),
        in_specs=[smem] + [vm] * 6,
        out_specs=vm,
        out_shape=jax.ShapeDtypeStruct(parts3, BF),
        name="far_amplitude",
    )(sc, sums, above, below, extra, gaps, vir)
    far = lax.all_to_all(far, "grp", 0, 0)

    fifth_block = swap(jnp.where(
        parity == 0, jnp.concatenate([n0, n1], axis=0), jnp.concatenate([m0, m1], axis=0)
    ))
    front = pl.BlockSpec((tile, cols), lambda i: (jnp.minimum(i, ht - 1), 0))
    back = pl.BlockSpec((tile, cols), lambda i: (jnp.maximum(i - ht, 0), 0))
    return pl.pallas_call(
        gamma_kernel,
        grid=(tiles,),
        in_specs=[smem, whole(parts), whole(parts3), row_tile, row_tile, front, back, front, back, row_tile],
        out_specs=row_tile,
        out_shape=jax.ShapeDtypeStruct((rows, cols), three_index.dtype),
        scratch_shapes=[pltpu.VMEM((tile, cols), F32)],
        cost_estimate=pl.CostEstimate(flops=10 * rows * cols * cols, bytes_accessed=14 * rows * cols, transcendentals=0),
        name="gamma",
    )(sc, near, far, own, partner, n0, n1, m0, m1, fifth_block)


def solution(mesh):
    in_specs = (P("grp", "blk"), P("blk"), P(), P(), P())
    out_specs = P("grp", "blk")
    return jax.shard_map(
        per_device, mesh=mesh, in_specs=in_specs, out_specs=out_specs, check_vma=False
    )
```

time: 254 us -> 140 us (0.55)
  the two profiles are of different devices: /device:TPU:1 before, /device:TPU:2 now
where the time goes in v1:
time: 140 us; the launch traced here: 139 us
  starting transfers between devices  72.6 us (52%)
  waiting for transfers between devices  26.7 us (19%)
  Pallas kernels  21.4 us (15%)
  local copies, waits for them, and re-layouts  13.5 us (10%)
  other arithmetic  3.95 us (3%)
    ppermute x6, starting transfers between devices, shift(): lax.ppermute(value, 'blk', [(i, (i + steps) % slabs) for i in range(slabs)])  35.7 us
    all_to_all x2, starting transfers between devices, per_device(): near = lax.all_to_all(near, 'grp', 0, 0)  14.7 us
    all_to_all x2, starting transfers between devices, per_device(): far = lax.all_to_all(far, 'grp', 0, 0)  14.4 us
    all_to_all x2, waiting for transfers between devices, per_device(): far = lax.all_to_all(far, 'grp', 0, 0)  13.3 us
    pallas_call x1, Pallas kernels, per_device(): pl.pallas_call(gamma_kernel, grid=(tiles,), in_specs=[smem, whole(parts),...  7.91 us
    ppermute x4, starting transfers between devices, swap(): return lax.ppermute(value, 'blk', [(i, i ^ 1) for i in range(slabs)])  7.78 us
    all_to_all x2, waiting for transfers between devices, per_device(): near = lax.all_to_all(near, 'grp', 0, 0)  6.46 us
    ppermute x6, waiting for transfers between devices, shift(): lax.ppermute(value, 'blk', [(i, (i + steps) % slabs) for i in range(slabs)])  4.8 us
  transfers between devices with their start and end apart: 14, of which 6 were waited for; matrix products, arithmetic and copies ran while one was open for 9% of the time, Pallas kernels for 10%

profile of v1, /device:TPU:2, one launch (start us, length us, event | category | flops | bytes accessed | tf_op | source)
XLA Modules:
  0.0 138.5 jit_solution(8797736500157315543)
XLA Ops:
  0.0 0.0 copy-start.14
  0.0 2.0 %collective-permute-start = (bf16[2944,256]{1,0:T(8,128)(2,1)}, bf16[2944,256]{1,0:T(8,128)(2,1)S(1)}, u32[]{:S(2)}, u32[]{:S(2)}) collective-permute-start(bf16[2944,256]{1,0:T(8,128)(2,1)} %o_ref.3), channel_id=1, source_target_pairs={{0,8},{8,0},{16,24},{24,16},{32,40},{40,32},{48,56},{56,48},{64,72... | collective-permute-start | bytes 4521992 | tf_op jit(solution)/shard_map/ppermute | solution.py:205
  2.1 2.6 %fusion = (bf16[1472,256]{1,0:T(8,128)(2,1)}, bf16[1472,256]{1,0:T(8,128)(2,1)}) fusion(bf16[2944,256]{1,0:T(8,128)(2,1)} %o_ref.3), kind=kLoop, calls=%fused_computation.5 | loop fusion | bytes 3014656 | tf_op jit(solution)/shard_map/slice | solution.py:209
  4.7 4.3 %collective-permute-start.3 = (bf16[1472,256]{1,0:T(8,128)(2,1)}, bf16[1472,256]{1,0:T(8,128)(2,1)S(1)}, u32[]{:S(2)}, u32[]{:S(2)}) collective-permute-start(bf16[1472,256]{1,0:T(8,128)(2,1)} %get-tuple-element.17), channel_id=1, source_target_pairs={{0,16},{8,24},{16,32},{24,40},{32,48},{40,56},{48,64},{56,72},{64,... | collective-permute-start | bytes 2261000 | tf_op jit(solution)/shard_map/ppermute | solution.py:202
  8.9 15.3 %collective-permute-start.2 = (bf16[1472,256]{1,0:T(8,128)(2,1)}, bf16[1472,256]{1,0:T(8,128)(2,1)S(1)}, u32[]{:S(2)}, u32[]{:S(2)}) collective-permute-start(bf16[1472,256]{1,0:T(8,128)(2,1)} %get-tuple-element.18), channel_id=1, source_target_pairs={{0,752},{8,760},{16,0},{24,8},{32,16},{40,24},{48,32},{56,40},{64,... | collective-permute-start | bytes 2261000 | tf_op jit(solution)/shard_map/ppermute | solution.py:202
  24.2 3.9 %collective-permute-start.7 = (bf16[1472,256]{1,0:T(8,128)(2,1)}, bf16[1472,256]{1,0:T(8,128)(2,1)}, u32[]{:S(2)}, u32[]{:S(2)}) collective-permute-start(bf16[1472,256]{1,0:T(8,128)(2,1)} %get-tuple-element.17), channel_id=1, source_target_pairs={{0,752},{8,760},{16,0},{24,8},{32,16},{40,24},{48,32},{56,40},{64,... | collective-permute-start | bytes 2261000 | tf_op jit(solution)/shard_map/ppermute | solution.py:202
  28.1 1.9 %collective-permute-start.8 = (bf16[1472,256]{1,0:T(8,128)(2,1)}, bf16[1472,256]{1,0:T(8,128)(2,1)}, u32[]{:S(2)}, u32[]{:S(2)}) collective-permute-start(bf16[1472,256]{1,0:T(8,128)(2,1)} %get-tuple-element.18), channel_id=1, source_target_pairs={{0,16},{8,24},{16,32},{24,40},{32,48},{40,56},{48,64},{56,72},{64,... | collective-permute-start | bytes 2261000 | tf_op jit(solution)/shard_map/ppermute | solution.py:202
  30.2 0.0 copy-done.14
  30.2 0.6 dynamic_slice.24
  30.8 0.0 copy-done.11
  30.8 0.6 fusion.1
  31.4 4.0 %stack.20.sc.refs_0_ = s32[8]{0:T(128)} concatenate(s32[1]{0:T(128)} %dynamic_slice.24, s32[1]{0:T(128)} %bitcast, s32[1]{0:T(128)} %bitcast.1, s32[1]{0:T(128)} %get-tuple-element.22, s32[1]{0:T(128)} %get-tuple-element.21, s32[1]{0:T(128)} %get-tuple-element.20, s32[1]{0:T(128)} %get-tuple-element.23, s32[1]{0:T(128)} %get-tuple-element.19), dimensions={0} | concatenate | bytes 64 | tf_op jit(solution)/shard_map/stack | solution.py:217
  35.4 0.0 collective-permute-done.p_ref.refs_5_.refs_6_
  35.4 1.2 copy-done
  36.6 4.3 %near.1 = bf16[8,2,32,256]{3,2,1,0:T(8,128)(2,1)} custom-call(s32[8]{0:T(128)} %stack.20.sc.refs_0_, bf16[2944,256]{1,0:T(8,128)(2,1)} %o_ref.3, bf16[2944,256]{1,0:T(8,128)(2,1)} %copy-done), custom_call_target="tpu_custom_call" | custom-call | flops 771751936 | bytes 3014656 | tf_op jit(solution)/shard_map/near/pallas_call | solution.py:239
  40.9 7.4 %all-to-all-start = ((bf16[8,2,32,256]{3,2,1,0:T(8,128)(2,1)}), bf16[8,2,32,256]{3,2,1,0:T(8,128)(2,1)S(1)}, u32[]{:S(2)}, u32[]{:S(2)}) async-start(bf16[8,2,32,256]{3,2,1,0:T(8,128)(2,1)} %near.1), calls=%async_computation | async-start | bytes 524288 | tf_op jit(solution)/shard_map/all_to_all | solution.py:249
  48.3 0.0 copy-done.13
  48.3 1.9 %collective-permute-start.1 = (f32[4]{0:T(128)S(1)}, f32[4]{0:T(128)S(1)}, u32[]{:S(2)}, u32[]{:S(2)}) collective-permute-start(f32[4]{0:T(128)S(1)} %copy-done.13), channel_id=1, source_target_pairs={{0,8},{8,0},{16,24},{24,16},{32,40},{40,32},{48,56},{56,48},{64,72... | collective-permute-start | bytes 56 | tf_op jit(solution)/shard_map/ppermute | solution.py:205
  50.3 0.0 copy-done.12
  50.3 0.1 dynamic_slice.31
  50.4 0.1 sub.32
  50.4 0.1 pad.6.clone
  50.5 0.8 collective-permute-done.1
  51.3 0.2 dynamic-slice_reduce_fusion
  51.5 0.1 pad.5.clone
  51.6 0.1 sub.29
  51.7 0.1 sub.30
  51.8 0.0 collective-permute-done.3.refs_2_.m1_ref
  51.8 0.0 collective-permute-done.2.refs_1_.n0_ref
  51.8 0.9 copy-done.1
  52.7 0.9 copy-done.2
  53.5 4.0 %far.1 = bf16[8,3,32,256]{3,2,1,0:T(8,128)(2,1)} custom-call(s32[8]{0:T(128)} %stack.20.sc.refs_0_, bf16[1472,256]{1,0:T(8,128)(2,1)} %copy-done.2, bf16[1472,256]{1,0:T(8,128)(2,1)} %copy-done.1, bf16[2944,256]{1,0:T(8,128)(2,1)} %o_ref.3, bf16[2944,256]{1,0:T(8,128)(2,1)} %o_ref.3, bf16[2944,256]{1,0:T(8,128)(2,1)} %copy-done, bf16[2944,256]{1,0:T(8,128)(2,1)} %copy-done), custom_call_target="tpu_custom_call" | custom-call | flops 578813952 | bytes 4521984 | tf_op jit(solution)/shard_map/far/pallas_call | solution.py:263
  57.5 6.5 %all-to-all-done.refs_1_ = bf16[8,2,32,256]{3,2,1,0:T(8,128)(2,1)S(1)} async-done(((bf16[8,2,32,256]{3,2,1,0:T(8,128)(2,1)}), bf16[8,2,32,256]{3,2,1,0:T(8,128)(2,1)S(1)}, u32[]{:S(2)}, u32[]{:S(2)}) %all-to-all-start) | async-done | bytes 262176 | tf_op jit(solution)/shard_map/all_to_all | solution.py:249
  64.0 4.8 %all-to-all-start.2 = ((bf16[8,3,32,256]{3,2,1,0:T(8,128)(2,1)}), bf16[8,3,32,256]{3,2,1,0:T(8,128)(2,1)S(1)}, u32[]{:S(2)}, u32[]{:S(2)}) async-start(bf16[8,3,32,256]{3,2,1,0:T(8,128)(2,1)} %far.1), calls=%async_computation.2 | async-start | bytes 786432 | tf_op jit(solution)/shard_map/all_to_all | solution.py:273
  68.8 0.0 collective-permute-done.7.n1_ref
  68.8 0.0 collective-permute-done.8.m0_ref
  68.8 3.3 %maximum_select_fusion = bf16[2944,256]{1,0:T(8,128)(2,1)} fusion(bf16[1472,256]{1,0:T(8,128)(2,1)} %collective-permute-done.7.n1_ref, bf16[1472,256]{1,0:T(8,128)(2,1)} %copy-done.2, bf16[1472,256]{1,0:T(8,128)(2,1)} %copy-done.1, bf16[1472,256]{1,0:T(8,128)(2,1)} %collective-permute-done.8.m0_ref, pred[]{:T(512)S(6)} %eq.10), kind=kLoop, calls=%fused_computation | loop fusion | flops 6782976 | bytes 4521985 | tf_op jit(solution)/shard_map/jit(_where)/select_n | solution.py:297
  72.1 0.0 copy-done.7
  72.1 1.9 %collective-permute-start.9 = (bf16[2944,256]{1,0:T(8,128)(2,1)}, bf16[2944,256]{1,0:T(8,128)(2,1)S(1)}, u32[]{:S(2)}, u32[]{:S(2)}) collective-permute-start(bf16[2944,256]{1,0:T(8,128)(2,1)} %maximum_select_fusion), channel_id=1, source_target_pairs={{0,8},{8,0},{16,24},{24,16},{32,40},{40,32},{48,56},{56,48},{64,72... | collective-permute-start | bytes 4521992 | tf_op jit(solution)/shard_map/ppermute | solution.py:205
  74.0 0.7 maximum_maximum_fusion.refs_2_.refs_5_
  74.7 0.7 broadcast_in_dim.21.refs_3_.refs_6_
  75.4 1.7 %near_amplitude.1 = (bf16[8,2,32,256]{3,2,1,0:T(8,128)(2,1)}, bf16[16,256]{1,0:T(8,128)(2,1)}) custom-call(s32[8]{0:T(128)} %stack.20.sc.refs_0_, bf16[8,2,32,256]{3,2,1,0:T(8,128)(2,1)} %copy-done.7, f32[8,256]{1,0:T(8,128)} %maximum_maximum_fusion.refs_2_.refs_5_, f32[32,256]{1,0:T(8,128)} %broadcast_in_dim.21.refs_3_.refs_6_), custom_call_target="tpu_custom_call" | custom-call | tf_op jit(solution)/shard_map/near_amplitude/pallas_call | solution.py:251
  77.1 2.3 %all-to-all-done.2.parts_ref = bf16[8,3,32,256]{3,2,1,0:T(8,128)(2,1)S(1)} async-done(((bf16[8,3,32,256]{3,2,1,0:T(8,128)(2,1)}), bf16[8,3,32,256]{3,2,1,0:T(8,128)(2,1)S(1)}, u32[]{:S(2)}, u32[]{:S(2)}) %all-to-all-start.2) | async-done | bytes 393248 | tf_op jit(solution)/shard_map/all_to_all | solution.py:273
  79.4 7.3 %all-to-all-start.1 = ((bf16[8,2,32,256]{3,2,1,0:T(8,128)(2,1)}), bf16[8,2,32,256]{3,2,1,0:T(8,128)(2,1)S(1)}, u32[]{:S(2)}, u32[]{:S(2)}) async-start(bf16[8,2,32,256]{3,2,1,0:T(8,128)(2,1)} %get-tuple-element.11), calls=%async_computation.1 | async-start | bytes 524288 | tf_op jit(solution)/shard_map/all_to_all | solution.py:258
  86.8 0.0 copy-done.4
  86.8 1.7 %pack.1 = (f32[2,32,256]{2,1,0:T(8,128)}, bf16[80,256]{1,0:T(8,128)(2,1)}, bf16[80,256]{1,0:T(8,128)(2,1)}, bf16[32,256]{1,0:T(8,128)(2,1)}) custom-call(bf16[8,3,32,256]{3,2,1,0:T(8,128)(2,1)} %copy-done.4, bf16[16,256]{1,0:T(8,128)(2,1)} %get-tuple-element.12.head_ref), custom_call_target="tpu_custom_call" | custom-call | tf_op jit(solution)/shard_map/pack/pallas_call | solution.py:275
  88.5 8.4 %collective-permute-start.4 = (bf16[80,256]{1,0:T(8,128)(2,1)}, bf16[80,256]{1,0:T(8,128)(2,1)S(1)}, u32[]{:S(2)}, u32[]{:S(2)}) collective-permute-start(bf16[80,256]{1,0:T(8,128)(2,1)} %get-tuple-element.14), channel_id=1, source_target_pairs={{0,752},{8,760},{16,0},{24,8},{32,16},{40,24},{48,32},{56,40},{64,... | collective-permute-start | bytes 122888 | tf_op jit(solution)/shard_map/ppermute | solution.py:202
  96.9 1.9 %collective-permute-start.5 = (bf16[80,256]{1,0:T(8,128)(2,1)}, bf16[80,256]{1,0:T(8,128)(2,1)S(1)}, u32[]{:S(2)}, u32[]{:S(2)}) collective-permute-start(bf16[80,256]{1,0:T(8,128)(2,1)} %get-tuple-element.15), channel_id=1, source_target_pairs={{0,16},{8,24},{16,32},{24,40},{32,48},{40,56},{48,64},{56,72},{64,... | collective-permute-start | bytes 122888 | tf_op jit(solution)/shard_map/ppermute | solution.py:202
  98.8 1.9 %collective-permute-start.6 = (bf16[32,256]{1,0:T(8,128)(2,1)}, bf16[32,256]{1,0:T(8,128)(2,1)S(1)}, u32[]{:S(2)}, u32[]{:S(2)}) collective-permute-start(bf16[32,256]{1,0:T(8,128)(2,1)} %get-tuple-element.16), channel_id=1, source_target_pairs={{0,8},{8,0},{16,24},{24,16},{32,40},{40,32},{48,56},{56,48},{64,72... | collective-permute-start | bytes 49160 | tf_op jit(solution)/shard_map/ppermute | solution.py:205
  100.7 1.4 collective-permute-done.6.refs_4_
  102.1 0.0 collective-permute-done.4.refs_2_
  102.1 4.8 %collective-permute-done.5.refs_3_ = bf16[80,256]{1,0:T(8,128)(2,1)S(1)} collective-permute-done((bf16[80,256]{1,0:T(8,128)(2,1)}, bf16[80,256]{1,0:T(8,128)(2,1)S(1)}, u32[]{:S(2)}, u32[]{:S(2)}) %collective-permute-start.5) | collective-permute-done | bytes 40992 | tf_op jit(solution)/shard_map/ppermute | solution.py:202
  106.9 0.0 copy-done.10
  106.9 0.0 copy-done.8
  106.9 0.6 copy-done.9
  107.5 1.7 %far_amplitude.1 = bf16[8,3,32,256]{3,2,1,0:T(8,128)(2,1)} custom-call(s32[8]{0:T(128)} %stack.20.sc.refs_0_, f32[2,32,256]{2,1,0:T(8,128)} %get-tuple-element.13.refs_1_, bf16[80,256]{1,0:T(8,128)(2,1)} %copy-done.8, bf16[80,256]{1,0:T(8,128)(2,1)} %copy-done.9, bf16[32,256]{1,0:T(8,128)(2,1)} %copy-done.10, f32[8,256]{1,0:T(8,128)} %maximum_maximum_fusion.refs_2_.refs_5_, ...), custom_call_target="tpu_custom_call" | custom-call | tf_op jit(solution)/shard_map/far_amplitude/pallas_call | solution.py:288
  109.3 0.0 all-to-all-done.1.near_ref
  109.3 9.6 %all-to-all-start.3 = ((bf16[8,3,32,256]{3,2,1,0:T(8,128)(2,1)}), bf16[8,3,32,256]{3,2,1,0:T(8,128)(2,1)S(1)}, u32[]{:S(2)}, u32[]{:S(2)}) async-start(bf16[8,3,32,256]{3,2,1,0:T(8,128)(2,1)} %far_amplitude.1), calls=%async_computation.3 | async-start | bytes 786432 | tf_op jit(solution)/shard_map/all_to_all | solution.py:295
  118.9 0.0 collective-permute-done.9.x_ref
  118.9 11.0 %all-to-all-done.3.far_ref = bf16[8,3,32,256]{3,2,1,0:T(8,128)(2,1)S(1)} async-done(((bf16[8,3,32,256]{3,2,1,0:T(8,128)(2,1)}), bf16[8,3,32,256]{3,2,1,0:T(8,128)(2,1)S(1)}, u32[]{:S(2)}, u32[]{:S(2)}) %all-to-all-start.3) | async-done | bytes 393248 | tf_op jit(solution)/shard_map/all_to_all | solution.py:295
  129.8 0.0 copy-done.6
  129.8 0.0 copy-done.5
  129.9 0.8 copy-done.3
  130.6 7.9 %gamma.1 = bf16[2944,256]{1,0:T(8,128)(2,1)} custom-call(s32[8]{0:T(128)} %stack.20.sc.refs_0_, bf16[8,2,32,256]{3,2,1,0:T(8,128)(2,1)} %copy-done.6, bf16[8,3,32,256]{3,2,1,0:T(8,128)(2,1)} %copy-done.3, bf16[2944,256]{1,0:T(8,128)(2,1)} %o_ref.3, bf16[2944,256]{1,0:T(8,128)(2,1)} %copy-done, bf16[1472,256]{1,0:T(8,128)(2,1)} %copy-done.2, ...), custom_call_target="tpu_custom_call" | custom-call | flops 1929379840 | bytes 10551296 | tf_op jit(solution)/shard_map/gamma/pallas_call | solution.py:302
  (18 shorter events, 0.0 us)
Async XLA Ops:
  0.0 30.2 %copy-start.14 = (s32[8]{0:T(128)S(1)}, s32[8]{0:T(128)}, u32[]{:S(2)}) copy-start(s32[8]{0:T(128)} %param.8) | copy-start | bytes 100
  0.0 30.8 %copy-start.11 = (s32[96]{0:T(128)S(1)}, s32[96]{0:T(128)}, u32[]{:S(2)}) copy-start(s32[96]{0:T(128)} %param.9) | copy-start | bytes 1156
  0.0 35.4 %collective-permute-start = (bf16[2944,256]{1,0:T(8,128)(2,1)}, bf16[2944,256]{1,0:T(8,128)(2,1)S(1)}, u32[]{:S(2)}, u32[]{:S(2)}) collective-permute-start(bf16[2944,256]{1,0:T(8,128)(2,1)} %o_ref.3), channel_id=1, source_target_pairs={{0,8},{8,0},{16,24},{24,16},{32,40},{40,32},{48,56},{56,48},{64,72... | collective-permute-start | bytes 4521992 | tf_op jit(solution)/shard_map/ppermute | solution.py:205
  4.7 47.1 %collective-permute-start.3 = (bf16[1472,256]{1,0:T(8,128)(2,1)}, bf16[1472,256]{1,0:T(8,128)(2,1)S(1)}, u32[]{:S(2)}, u32[]{:S(2)}) collective-permute-start(bf16[1472,256]{1,0:T(8,128)(2,1)} %get-tuple-element.17), channel_id=1, source_target_pairs={{0,16},{8,24},{16,32},{24,40},{32,48},{40,56},{48,64},{56,72},{64,... | collective-permute-start | bytes 2261000 | tf_op jit(solution)/shard_map/ppermute | solution.py:202
  8.9 42.8 %collective-permute-start.2 = (bf16[1472,256]{1,0:T(8,128)(2,1)}, bf16[1472,256]{1,0:T(8,128)(2,1)S(1)}, u32[]{:S(2)}, u32[]{:S(2)}) collective-permute-start(bf16[1472,256]{1,0:T(8,128)(2,1)} %get-tuple-element.18), channel_id=1, source_target_pairs={{0,752},{8,760},{16,0},{24,8},{32,16},{40,24},{48,32},{56,40},{64,... | collective-permute-start | bytes 2261000 | tf_op jit(solution)/shard_map/ppermute | solution.py:202
  24.2 44.6 %collective-permute-start.7 = (bf16[1472,256]{1,0:T(8,128)(2,1)}, bf16[1472,256]{1,0:T(8,128)(2,1)}, u32[]{:S(2)}, u32[]{:S(2)}) collective-permute-start(bf16[1472,256]{1,0:T(8,128)(2,1)} %get-tuple-element.17), channel_id=1, source_target_pairs={{0,752},{8,760},{16,0},{24,8},{32,16},{40,24},{48,32},{56,40},{64,... | collective-permute-start | bytes 2261000 | tf_op jit(solution)/shard_map/ppermute | solution.py:202
  28.1 40.7 %collective-permute-start.8 = (bf16[1472,256]{1,0:T(8,128)(2,1)}, bf16[1472,256]{1,0:T(8,128)(2,1)}, u32[]{:S(2)}, u32[]{:S(2)}) collective-permute-start(bf16[1472,256]{1,0:T(8,128)(2,1)} %get-tuple-element.18), channel_id=1, source_target_pairs={{0,16},{8,24},{16,32},{24,40},{32,48},{40,56},{48,64},{56,72},{64,... | collective-permute-start | bytes 2261000 | tf_op jit(solution)/shard_map/ppermute | solution.py:202
  35.4 12.9 %copy-start.13 = (f32[4]{0:T(128)S(1)}, f32[4]{0:T(128)}, u32[]{:S(2)}) copy-start(f32[4]{0:T(128)} %param.6) | copy-start | bytes 52
  35.4 14.9 %copy-start.12 = (f32[64]{0:T(128)S(1)}, f32[64]{0:T(128)}, u32[]{:S(2)}) copy-start(f32[64]{0:T(128)} %param.7) | copy-start | bytes 772
  35.4 1.2 copy-start
  40.9 23.1 %all-to-all-start = ((bf16[8,2,32,256]{3,2,1,0:T(8,128)(2,1)}), bf16[8,2,32,256]{3,2,1,0:T(8,128)(2,1)S(1)}, u32[]{:S(2)}, u32[]{:S(2)}) async-start(bf16[8,2,32,256]{3,2,1,0:T(8,128)(2,1)} %near.1), calls=%async_computation | async-start | bytes 524288 | tf_op jit(solution)/shard_map/all_to_all | solution.py:249
  48.3 3.0 %collective-permute-start.1 = (f32[4]{0:T(128)S(1)}, f32[4]{0:T(128)S(1)}, u32[]{:S(2)}, u32[]{:S(2)}) collective-permute-start(f32[4]{0:T(128)S(1)} %copy-done.13), channel_id=1, source_target_pairs={{0,8},{8,0},{16,24},{24,16},{32,40},{40,32},{48,56},{56,48},{64,72... | collective-permute-start | bytes 56 | tf_op jit(solution)/shard_map/ppermute | solution.py:205
  51.8 0.9 copy-start.1
  52.7 0.9 copy-start.2
  64.0 8.1 %copy-start.7 = (bf16[8,2,32,256]{3,2,1,0:T(8,128)(2,1)}, bf16[8,2,32,256]{3,2,1,0:T(8,128)(2,1)S(1)}, u32[]{:S(2)}) copy-start(bf16[8,2,32,256]{3,2,1,0:T(8,128)(2,1)S(1)} %all-to-all-done.refs_1_) | copy-start | bytes 786436
  64.0 15.4 %all-to-all-start.2 = ((bf16[8,3,32,256]{3,2,1,0:T(8,128)(2,1)}), bf16[8,3,32,256]{3,2,1,0:T(8,128)(2,1)S(1)}, u32[]{:S(2)}, u32[]{:S(2)}) async-start(bf16[8,3,32,256]{3,2,1,0:T(8,128)(2,1)} %far.1), calls=%async_computation.2 | async-start | bytes 786432 | tf_op jit(solution)/shard_map/all_to_all | solution.py:273
  72.1 46.8 %collective-permute-start.9 = (bf16[2944,256]{1,0:T(8,128)(2,1)}, bf16[2944,256]{1,0:T(8,128)(2,1)S(1)}, u32[]{:S(2)}, u32[]{:S(2)}) collective-permute-start(bf16[2944,256]{1,0:T(8,128)(2,1)} %maximum_select_fusion), channel_id=1, source_target_pairs={{0,8},{8,0},{16,24},{24,16},{32,40},{40,32},{48,56},{56,48},{64,72... | collective-permute-start | bytes 4521992 | tf_op jit(solution)/shard_map/ppermute | solution.py:205
  79.4 7.3 %copy-start.4 = (bf16[8,3,32,256]{3,2,1,0:T(8,128)(2,1)}, bf16[8,3,32,256]{3,2,1,0:T(8,128)(2,1)S(1)}, u32[]{:S(2)}) copy-start(bf16[8,3,32,256]{3,2,1,0:T(8,128)(2,1)S(1)} %all-to-all-done.2.parts_ref) | copy-start | bytes 1179652
  79.4 29.8 %all-to-all-start.1 = ((bf16[8,2,32,256]{3,2,1,0:T(8,128)(2,1)}), bf16[8,2,32,256]{3,2,1,0:T(8,128)(2,1)S(1)}, u32[]{:S(2)}, u32[]{:S(2)}) async-start(bf16[8,2,32,256]{3,2,1,0:T(8,128)(2,1)} %get-tuple-element.11), calls=%async_computation.1 | async-start | bytes 524288 | tf_op jit(solution)/shard_map/all_to_all | solution.py:258
  88.5 13.6 %collective-permute-start.4 = (bf16[80,256]{1,0:T(8,128)(2,1)}, bf16[80,256]{1,0:T(8,128)(2,1)S(1)}, u32[]{:S(2)}, u32[]{:S(2)}) collective-permute-start(bf16[80,256]{1,0:T(8,128)(2,1)} %get-tuple-element.14), channel_id=1, source_target_pairs={{0,752},{8,760},{16,0},{24,8},{32,16},{40,24},{48,32},{56,40},{64,... | collective-permute-start | bytes 122888 | tf_op jit(solution)/shard_map/ppermute | solution.py:202
  96.9 10.0 %collective-permute-start.5 = (bf16[80,256]{1,0:T(8,128)(2,1)}, bf16[80,256]{1,0:T(8,128)(2,1)S(1)}, u32[]{:S(2)}, u32[]{:S(2)}) collective-permute-start(bf16[80,256]{1,0:T(8,128)(2,1)} %get-tuple-element.15), channel_id=1, source_target_pairs={{0,16},{8,24},{16,32},{24,40},{32,48},{40,56},{48,64},{56,72},{64,... | collective-permute-start | bytes 122888 | tf_op jit(solution)/shard_map/ppermute | solution.py:202
  98.8 3.3 %collective-permute-start.6 = (bf16[32,256]{1,0:T(8,128)(2,1)}, bf16[32,256]{1,0:T(8,128)(2,1)S(1)}, u32[]{:S(2)}, u32[]{:S(2)}) collective-permute-start(bf16[32,256]{1,0:T(8,128)(2,1)} %get-tuple-element.16), channel_id=1, source_target_pairs={{0,8},{8,0},{16,24},{24,16},{32,40},{40,32},{48,56},{56,48},{64,72... | collective-permute-start | bytes 49160 | tf_op jit(solution)/shard_map/ppermute | solution.py:205
  102.1 4.8 %copy-start.10 = (bf16[32,256]{1,0:T(8,128)(2,1)}, bf16[32,256]{1,0:T(8,128)(2,1)S(1)}, u32[]{:S(2)}) copy-start(bf16[32,256]{1,0:T(8,128)(2,1)S(1)} %collective-permute-done.6.refs_4_) | copy-start | bytes 49156
  102.1 4.8 %copy-start.8 = (bf16[80,256]{1,0:T(8,128)(2,1)}, bf16[80,256]{1,0:T(8,128)(2,1)S(1)}, u32[]{:S(2)}) copy-start(bf16[80,256]{1,0:T(8,128)(2,1)S(1)} %collective-permute-done.4.refs_2_) | copy-start | bytes 122884
  106.9 0.6 copy-start.9
  109.3 20.6 %copy-start.6 = (bf16[8,2,32,256]{3,2,1,0:T(8,128)(2,1)}, bf16[8,2,32,256]{3,2,1,0:T(8,128)(2,1)S(1)}, u32[]{:S(2)}) copy-start(bf16[8,2,32,256]{3,2,1,0:T(8,128)(2,1)S(1)} %all-to-all-done.1.near_ref) | copy-start | bytes 786436
  109.3 20.6 %all-to-all-start.3 = ((bf16[8,3,32,256]{3,2,1,0:T(8,128)(2,1)}), bf16[8,3,32,256]{3,2,1,0:T(8,128)(2,1)S(1)}, u32[]{:S(2)}, u32[]{:S(2)}) async-start(bf16[8,3,32,256]{3,2,1,0:T(8,128)(2,1)} %far_amplitude.1), calls=%async_computation.3 | async-start | bytes 786432 | tf_op jit(solution)/shard_map/all_to_all | solution.py:295
  118.9 11.0 %copy-start.5 = (bf16[2944,256]{1,0:T(8,128)(2,1)}, bf16[2944,256]{1,0:T(8,128)(2,1)S(1)}, u32[]{:S(2)}) copy-start(bf16[2944,256]{1,0:T(8,128)(2,1)S(1)} %collective-permute-done.9.x_ref) | copy-start | bytes 4521988
  129.8 0.8 copy-start.3

commit v2 on v0

v2 whole, which is shorter than its diff:
```python
import jax
import jax.numpy as jnp
from jax import lax
from jax.experimental import pallas as pl
from jax.experimental.pallas import tpu as pltpu
from jax.sharding import PartitionSpec as P


BF = jnp.bfloat16
F32 = jnp.float32
VM = pl.BlockSpec(memory_space=pltpu.VMEM)
SM = pl.BlockSpec(memory_space=pltpu.SMEM)
ANY = pl.BlockSpec(memory_space=pl.ANY)


def mm(a, b):
    return jnp.dot(a, b, preferred_element_type=F32)


def keep_rows(block, start, count):
    row = lax.broadcasted_iota(jnp.int32, block.shape, 0) + start
    return jnp.where(row < count, block, jnp.zeros((), block.dtype))


def fetch(pairs, sems):
    copies = [pltpu.make_async_copy(src, dst, sems.at[j]) for j, (src, dst) in enumerate(pairs)]
    for copy in copies:
        copy.start()
    return copies


def place():
    r = lax.axis_index("blk")
    return r, lax.rem(r, 2), lax.axis_index("grp")


def at(count_ref, index):
    slabs = count_ref.shape[0]
    return count_ref[lax.rem(index + slabs, slabs)]


def three_terms(value):
    hi = value.astype(BF)
    rest = value - hi.astype(F32)
    mid = rest.astype(BF)
    low = (rest - mid.astype(F32)).astype(BF)
    return [hi.astype(F32), mid.astype(F32), low.astype(F32)]


def prep_kernel(
    aux_ref, energy_ref, other_ref, vir_ref, vir_rows_ref, own_ref, p_ref,
    o0t_ref, o1t_ref, pt_ref, near_ref, gaps_ref, head_ref,
):
    _, parity, g = place()
    rows, cols = own_ref.shape
    half = rows // 2
    owners, _, piece, _ = near_ref.shape
    nv = vir_ref.shape[1]
    count = aux_ref[g]
    o0t_ref[...] = keep_rows(own_ref[:half, :], 0, count).T
    o1t_ref[...] = keep_rows(own_ref[half:, :], half, count).T

    @pl.when(parity == 0)
    def _():
        pt_ref[...] = keep_rows(p_ref[:half, :], 0, count).T

    @pl.when(parity == 1)
    def _():
        pt_ref[...] = keep_rows(p_ref[half:, :], half, count).T

    for j, ref in enumerate((own_ref, p_ref)):
        pair = mm(o0t_ref[...], ref[:half, :]) + mm(o1t_ref[...], ref[half:, :])
        near_ref[:, j] = pair.reshape(owners, piece, cols).astype(BF)

    slots = cols // nv
    slot = (g * piece) // nv
    lane = lax.broadcasted_iota(jnp.int32, (1, cols), 1)
    vir = jnp.concatenate([vir_ref[...]] * slots, axis=1)
    rows_out = []
    for ref in (energy_ref, other_ref):
        level = jnp.zeros((1, cols), F32)
        for k in range(slots):
            level = jnp.where(lane // nv == k, ref[k], level)
        rows_out.append(level - vir)
    for ref in (energy_ref, other_ref):
        rows_out.append(jnp.broadcast_to(ref[slot], (1, cols)))
    terms = []
    for row in rows_out:
        terms += three_terms(row)
    zero = jnp.zeros((4, cols), F32)
    head_ref[...] = jnp.concatenate(terms + [zero], axis=0).astype(BF)
    start = pl.multiple_of(lax.rem(g * piece, nv), piece)
    gaps_ref[0:8, :] = jnp.concatenate(rows_out + [zero], axis=0)
    gaps_ref[8:, :] = vir_rows_ref[pl.ds(start, piece), :]


def far_kernel(n_ref, m_ref, o0t_ref, o1t_ref, pt_ref, near_ref, out_ref, n_buf, m_buf, o0_buf, o1_buf, p_buf, sems):
    _, parity, _ = place()
    owners, _, piece, cols = out_ref.shape
    copies = fetch(
        [(n_ref, n_buf), (o0t_ref, o0_buf), (m_ref, m_buf), (o1t_ref, o1_buf), (pt_ref, p_buf)], sems
    )

    def put(j, pair):
        out_ref[:, j] = pair.reshape(owners, piece, cols).astype(BF)

    out_ref[:, 0:2] = near_ref[...]
    copies[0].wait()
    copies[1].wait()
    put(2, mm(o0_buf[...], n_buf[...]).T)
    copies[2].wait()
    copies[3].wait()
    put(3, mm(o1_buf[...], m_buf[...]))
    copies[4].wait()

    @pl.when(parity == 0)
    def _():
        put(4, mm(p_buf[...], n_buf[...]).T)

    @pl.when(parity == 1)
    def _():
        put(4, mm(p_buf[...], m_buf[...]))


def pack_kernel(parts_ref, head_ref, sum_ref, up_ref, down_ref, swap_ref, buf, sems):
    fetch([(parts_ref, buf)], sems)[0].wait()
    total = jnp.sum(buf[...].astype(F32), axis=0)
    sum_ref[...] = total[:4]
    extra = total[4].astype(BF)
    size = extra.shape[0]
    swap_ref[...] = extra
    for j, ref in ((2, up_ref), (3, down_ref)):
        ref[0:size, :] = total[j].astype(BF)
        ref[size:2 * size, :] = extra
        ref[2 * size:, :] = head_ref[...]


def amplitude_kernel(
    nv, count_ref, sum_ref, gaps_ref, above_ref, below_ref, swap_ref, out_ref, above, below, swapped, sems
):
    r, parity, g = place()
    size, cols = swapped.shape
    slot = (g * size) // nv
    copies = fetch([(above_ref, above), (below_ref, below), (swap_ref, swapped)], sems)
    vir = gaps_ref[8:, :]
    own_gap = gaps_ref[0:1, :]
    own_rows = gaps_ref[2:3, :] - vir
    own_count = count_ref[r]
    lane = lax.broadcasted_iota(jnp.int32, (size, cols), 1)

    def put(j, pair, gap_rows, gap_cols, row_count, col_count):
        keep = (lane < col_count * nv) & (slot < row_count)
        amp = jnp.where(keep, pair / (gap_rows + gap_cols), 0.0).astype(BF)
        for owner in range(out_ref.shape[0]):
            out_ref[owner, j] = amp

    put(0, sum_ref[0], own_rows, own_gap, own_count, own_count)
    put(1, sum_ref[1], own_rows, gaps_ref[1:2, :], own_count, count_ref[r + 1 - 2 * parity])
    for copy in copies:
        copy.wait()

    def head(ref, row):
        block = ref[2 * size:, :].astype(F32)
        return block[3 * row:3 * row + 1] + block[3 * row + 1:3 * row + 2] + block[3 * row + 2:3 * row + 3]

    put(
        2, sum_ref[2] + above[0:size, :].astype(F32), head(above, 2) - vir, own_gap,
        at(count_ref, r + 2), own_count,
    )
    put(
        3, sum_ref[3] + below[0:size, :].astype(F32), own_rows, head(below, 0),
        own_count, at(count_ref, r - 2),
    )

    @pl.when(parity == 0)
    def _():
        put(
            4, swapped[...].astype(F32) + below[size:2 * size, :].astype(F32), own_rows, head(below, 1),
            own_count, at(count_ref, r - 1),
        )

    @pl.when(parity == 1)
    def _():
        put(
            4, swapped[...].astype(F32) + above[size:2 * size, :].astype(F32), head(above, 3) - vir, own_gap,
            at(count_ref, r + 1), own_count,
        )


def gamma_kernel(
    aux_ref, amps_ref, o_ref, p_ref, n0_ref, n1_ref, m0_ref, m1_ref, x_ref, out_ref, buf, weights, sems
):
    step = pl.program_id(0)
    tile, cols = o_ref.shape
    _, parity, g = place()

    @pl.when(step == 0)
    def _():
        fetch([(amps_ref, buf)], sems)[0].wait()

        def put(j, turned):
            matrix = buf[:, j].reshape(cols, cols)
            weights[j * cols:(j + 1) * cols, :] = matrix.T if turned else matrix

        put(0, False)
        put(1, True)
        put(2, False)
        put(3, True)

        @pl.when(parity == 0)
        def _():
            put(4, True)

        @pl.when(parity == 1)
        def _():
            put(4, False)

    def finish(n_ref, m_ref):
        blocks = jnp.concatenate([o_ref[...], p_ref[...], n_ref[...], m_ref[...], x_ref[...]], axis=1)
        total = mm(blocks, weights[...])
        out_ref[...] = keep_rows(total, step * tile, aux_ref[g]).astype(out_ref.dtype)

    lower = step < pl.num_programs(0) // 2

    @pl.when(lower)
    def _():
        finish(n0_ref, m0_ref)

    @pl.when(jnp.logical_not(lower))
    def _():
        finish(n1_ref, m1_ref)


def cost(flops, size):
    return pl.CostEstimate(flops=flops, bytes_accessed=size, transcendentals=0)


def per_device(three_index, occ_energy, vir_energy, aux_count, occ_count):
    rows, cols = three_index.shape
    half = rows // 2
    nv = vir_energy.shape[0]
    slabs = lax.axis_size("blk")
    owners = lax.axis_size("grp")
    piece = cols // owners
    dma = pltpu.SemaphoreType.DMA

    def shift(value, steps):
        return lax.ppermute(value, "blk", [(i, (i + steps) % slabs) for i in range(slabs)])

    def swap(value):
        return lax.ppermute(value, "blk", [(i, i ^ 1) for i in range(slabs)])

    def shape(*dims, dtype=BF):
        return jax.ShapeDtypeStruct(dims, dtype)

    own = three_index
    lower, upper = own[:half], own[half:]
    n0 = shift(lower, -2)
    m1 = shift(upper, 2)
    partner = swap(own)
    n1 = shift(upper, -2)
    m0 = shift(lower, 2)
    partner_energy = swap(occ_energy)

    o0t, o1t, pt, near, gaps, head = pl.pallas_call(
        prep_kernel,
        in_specs=[SM, SM, SM, VM, VM, VM, VM],
        out_specs=[VM] * 6,
        out_shape=[
            shape(cols, half), shape(cols, half), shape(cols, half), shape(owners, 2, piece, cols),
            shape(8 + piece, cols, dtype=F32), shape(16, cols),
        ],
        cost_estimate=cost(4 * rows * cols * cols, 8 * rows * cols),
        compiler_params=pltpu.CompilerParams(vmem_limit_bytes=16 << 20),
        name="prep",
    )(
        aux_count, occ_energy, partner_energy, vir_energy[None, :],
        jnp.broadcast_to(vir_energy[:, None], (nv, cols)), own, partner,
    )

    parts = shape(owners, 5, piece, cols)
    partial_sums = pl.pallas_call(
        far_kernel,
        in_specs=[ANY] * 5 + [VM],
        out_specs=VM,
        out_shape=parts,
        scratch_shapes=[
            pltpu.VMEM((half, cols), BF), pltpu.VMEM((half, cols), BF), pltpu.VMEM((cols, half), BF),
            pltpu.VMEM((cols, half), BF), pltpu.VMEM((cols, half), BF), dma((5,)),
        ],
        cost_estimate=cost(3 * rows * cols * cols, 5 * rows * cols),
        compiler_params=pltpu.CompilerParams(vmem_limit_bytes=10 << 20),
        name="far",
    )(n0, m1, o0t, o1t, pt, near)
    pieces = lax.all_to_all(partial_sums, "grp", 0, 0)
    message = shape(2 * piece + 16, cols)
    sums, up, down, extra = pl.pallas_call(
        pack_kernel,
        in_specs=[ANY, VM],
        out_specs=[VM] * 4,
        out_shape=[shape(4, piece, cols, dtype=F32), message, message, shape(piece, cols)],
        scratch_shapes=[pltpu.VMEM(parts.shape, BF), dma((1,))],
        cost_estimate=cost(cols * cols, 4 * cols * cols),
        compiler_params=pltpu.CompilerParams(vmem_limit_bytes=6 << 20),
        name="pack",
    )(pieces, head)
    below = shift(up, 2)
    above = shift(down, -2)
    extra = swap(extra)
    amps = pl.pallas_call(
        lambda *refs: amplitude_kernel(nv, *refs),
        in_specs=[SM, VM, VM, ANY, ANY, ANY],
        out_specs=VM,
        out_shape=parts,
        scratch_shapes=[
            pltpu.VMEM(message.shape, BF), pltpu.VMEM(message.shape, BF), pltpu.VMEM((piece, cols), BF), dma((3,)),
        ],
        cost_estimate=cost(cols * cols, 8 * cols * cols),
        compiler_params=pltpu.CompilerParams(vmem_limit_bytes=6 << 20),
        name="amplitude",
    )(occ_count, sums, gaps, above, below, extra)
    amps = lax.all_to_all(amps, "grp", 0, 0)

    parity = lax.axis_index("blk") % 2
    fifth = swap(jnp.where(
        parity == 0, jnp.concatenate([n0, n1], axis=0), jnp.concatenate([m0, m1], axis=0)
    ))

    tiles = 4
    tile = rows // tiles
    ht = tiles // 2
    row_tile = pl.BlockSpec((tile, cols), lambda i: (i, 0))
    front = pl.BlockSpec((tile, cols), lambda i: (jnp.minimum(i, ht - 1), 0))
    back = pl.BlockSpec((tile, cols), lambda i: (jnp.maximum(i - ht, 0), 0))
    return pl.pallas_call(
        gamma_kernel,
        grid=(tiles,),
        in_specs=[SM, ANY, row_tile, row_tile, front, back, front, back, row_tile],
        out_specs=row_tile,
        out_shape=jax.ShapeDtypeStruct((rows, cols), three_index.dtype),
        scratch_shapes=[pltpu.VMEM(parts.shape, BF), pltpu.VMEM((5 * cols, cols), BF), dma((1,))],
        cost_estimate=cost(10 * rows * cols * cols, 14 * rows * cols),
        compiler_params=pltpu.CompilerParams(vmem_limit_bytes=16 << 20),
        name="gamma",
    )(aux_count, amps, own, partner, n0, n1, m0, m1, fifth)


def solution(mesh):
    in_specs = (P("grp", "blk"), P("blk"), P(), P(), P())
    out_specs = P("grp", "blk")
    return jax.shard_map(
        per_device, mesh=mesh, in_specs=in_specs, out_specs=out_specs, check_vma=False
    )
```

time: 254 us -> 126 us (0.50)
  the two profiles are of different devices: /device:TPU:1 before, /device:TPU:8 now
where the time goes in v2:
time: 126 us; the launch traced here: 125 us
  starting transfers between devices  53.3 us (42%)
  waiting for transfers between devices  49.2 us (39%)
  Pallas kernels  13.5 us (11%)
  local copies, waits for them, and re-layouts  5.77 us (5%)
  other arithmetic  2.81 us (2%)
    ppermute x6, starting transfers between devices, shift(): lax.ppermute(value, 'blk', [(i, (i + steps) % slabs) for i in range(slabs)])  30.2 us
    all_to_all x1, waiting for transfers between devices, per_device(): amps = lax.all_to_all(amps, 'grp', 0, 0)  18.2 us
    all_to_all x1, waiting for transfers between devices, per_device(): pieces = lax.all_to_all(partial_sums, 'grp', 0, 0)  16.5 us
    ppermute x6, waiting for transfers between devices, shift(): lax.ppermute(value, 'blk', [(i, (i + steps) % slabs) for i in range(slabs)])  12.2 us
    all_to_all x1, starting transfers between devices, per_device(): pieces = lax.all_to_all(partial_sums, 'grp', 0, 0)  9.56 us
    ppermute x4, starting transfers between devices, swap(): return lax.ppermute(value, 'blk', [(i, i ^ 1) for i in range(slabs)])  7.8 us
    pallas_call x1, Pallas kernels, per_device(): pl.pallas_call(gamma_kernel, grid=(tiles,), in_specs=[SM, ANY, row_tile,...  6.72 us
    all_to_all x1, starting transfers between devices, per_device(): amps = lax.all_to_all(amps, 'grp', 0, 0)  5.8 us
  transfers between devices with their start and end apart: 12, of which 8 were waited for; matrix products, arithmetic and copies ran while one was open for 4% of the time, Pallas kernels for 5%

profile of v2, /device:TPU:8, one launch (start us, length us, event | category | flops | bytes accessed | tf_op | source)
XLA Modules:
  0.0 124.8 jit_solution(1411686513676722577)
XLA Ops:
  0.0 0.0 copy-start
  0.0 0.0 copy-start.8
  0.0 0.0 copy-start.6
  0.0 0.0 copy-start.5
  0.0 2.1 %collective-permute-start.3 = (bf16[2944,256]{1,0:T(8,128)(2,1)}, bf16[2944,256]{1,0:T(8,128)(2,1)S(1)}, u32[]{:S(2)}, u32[]{:S(2)}) collective-permute-start(bf16[2944,256]{1,0:T(8,128)(2,1)} %o_ref.1), channel_id=1, source_target_pairs={{0,8},{8,0},{16,24},{24,16},{32,40},{40,32},{48,56},{56,48},{64,72... | collective-permute-start | bytes 4521992 | tf_op jit(solution)/shard_map/ppermute | solution.py:251
  2.1 2.6 %fusion = (bf16[1472,256]{1,0:T(8,128)(2,1)}, bf16[1472,256]{1,0:T(8,128)(2,1)}) fusion(bf16[2944,256]{1,0:T(8,128)(2,1)} %o_ref.1), kind=kLoop, calls=%fused_computation.1 | loop fusion | bytes 3014656 | tf_op jit(solution)/shard_map/slice | solution.py:257
  4.7 14.5 %collective-permute-start = (bf16[1472,256]{1,0:T(8,128)(2,1)}, bf16[1472,256]{1,0:T(8,128)(2,1)S(1)}, u32[]{:S(2)}, u32[]{:S(2)}) collective-permute-start(bf16[1472,256]{1,0:T(8,128)(2,1)} %get-tuple-element.26), channel_id=1, source_target_pairs={{0,752},{8,760},{16,0},{24,8},{32,16},{40,24},{48,32},{56,40},{64,... | collective-permute-start | bytes 2261000 | tf_op jit(solution)/shard_map/ppermute | solution.py:248
  19.1 1.9 %collective-permute-start.1 = (bf16[1472,256]{1,0:T(8,128)(2,1)}, bf16[1472,256]{1,0:T(8,128)(2,1)S(1)}, u32[]{:S(2)}, u32[]{:S(2)}) collective-permute-start(bf16[1472,256]{1,0:T(8,128)(2,1)} %get-tuple-element.25), channel_id=1, source_target_pairs={{0,16},{8,24},{16,32},{24,40},{32,48},{40,56},{48,64},{56,72},{64,... | collective-permute-start | bytes 2261000 | tf_op jit(solution)/shard_map/ppermute | solution.py:248
  21.1 6.0 %collective-permute-start.7 = (bf16[1472,256]{1,0:T(8,128)(2,1)}, bf16[1472,256]{1,0:T(8,128)(2,1)}, u32[]{:S(2)}, u32[]{:S(2)}) collective-permute-start(bf16[1472,256]{1,0:T(8,128)(2,1)} %get-tuple-element.25), channel_id=1, source_target_pairs={{0,752},{8,760},{16,0},{24,8},{32,16},{40,24},{48,32},{56,40},{64,... | collective-permute-start | bytes 2261000 | tf_op jit(solution)/shard_map/ppermute | solution.py:248
  27.1 0.0 copy-done.8
  27.1 1.9 %collective-permute-start.2 = (f32[4]{0:T(128)S(1)}, f32[4]{0:T(128)S(1)}, u32[]{:S(2)}, u32[]{:S(2)}) collective-permute-start(f32[4]{0:T(128)S(1)} %copy-done.8), channel_id=1, source_target_pairs={{0,8},{8,0},{16,24},{24,16},{32,40},{40,32},{48,56},{56,48},{64,72... | collective-permute-start | bytes 56 | tf_op jit(solution)/shard_map/ppermute | solution.py:251
  29.1 1.1 collective-permute-done.2.other_ref
  30.1 1.9 %collective-permute-start.8 = (bf16[1472,256]{1,0:T(8,128)(2,1)}, bf16[1472,256]{1,0:T(8,128)(2,1)}, u32[]{:S(2)}, u32[]{:S(2)}) collective-permute-start(bf16[1472,256]{1,0:T(8,128)(2,1)} %get-tuple-element.26), channel_id=1, source_target_pairs={{0,16},{8,24},{16,32},{24,40},{32,48},{40,56},{48,64},{56,72},{64,... | collective-permute-start | bytes 2261000 | tf_op jit(solution)/shard_map/ppermute | solution.py:248
  32.1 0.0 collective-permute-done.3.p_ref
  32.1 0.0 copy-start.1
  32.1 0.0 copy-done.5
  32.1 0.1 broadcast_in_dim.10.vir_rows_ref
  32.2 0.0 copy-done
  32.2 0.0 copy-done.6
  32.2 2.3 %prep.1 = (bf16[256,1472]{1,0:T(8,128)(2,1)S(1)}, bf16[256,1472]{1,0:T(8,128)(2,1)S(1)}, bf16[256,1472]{1,0:T(8,128)(2,1)S(1)}, bf16[8,2,32,256]{3,2,1,0:T(8,128...) custom-call(s32[8]{0:T(128)S(1)} %copy-done.6, f32[4]{0:T(128)S(1)} %copy-done.8, ...), custom_call_target="tpu_custom_call" | custom-call | flops 771751936 | bytes 6029312 | tf_op jit(solution)/shard_map/prep/pallas_call | solution.py:265
  34.5 0.0 copy-done.1
  34.5 2.1 %collective-permute-done.n_ref.n0_ref = bf16[1472,256]{1,0:T(8,128)(2,1)S(1)} collective-permute-done((bf16[1472,256]{1,0:T(8,128)(2,1)}, bf16[1472,256]{1,0:T(8,128)(2,1)S(1)}, u32[]{:S(2)}, u32[]{:S(2)}) %collective-permute-start) | collective-permute-done | bytes 753696 | tf_op jit(solution)/shard_map/ppermute | solution.py:248
  36.6 6.4 %collective-permute-done.1.m_ref.m1_ref = bf16[1472,256]{1,0:T(8,128)(2,1)S(1)} collective-permute-done((bf16[1472,256]{1,0:T(8,128)(2,1)}, bf16[1472,256]{1,0:T(8,128)(2,1)S(1)}, u32[]{:S(2)}, u32[]{:S(2)}) %collective-permute-start.1) | collective-permute-done | bytes 753696 | tf_op jit(solution)/shard_map/ppermute | solution.py:248
  43.0 2.5 %far.1 = bf16[8,5,32,256]{3,2,1,0:T(8,128)(2,1)S(1)} custom-call(bf16[1472,256]{1,0:T(8,128)(2,1)S(1)} %collective-permute-done.n_ref.n0_ref, bf16[1472,256]{1,0:T(8,128)(2,1)S(1)} %collective-permute-done.1.m_ref.m1_ref, bf16[256,1472]{1,0:T(8,128)(2,1)S(1)} %get-tuple-element.15.o0t_ref, bf16[256,1472]{1,0:T(8,128)(2,1)S(1)} %get-tuple-element.16.o1t_ref, ...), custom_call_target="tpu_custom_call" | custom-call | flops 578813952 | bytes 3768320 | tf_op jit(solution)/shard_map/far/pallas_call | solution.py:282
  45.5 0.0 copy-start.3
  45.6 0.8 copy-done.3
  46.4 9.6 %all-to-all-start = ((bf16[8,5,32,256]{3,2,1,0:T(8,128)(2,1)}), bf16[8,5,32,256]{3,2,1,0:T(8,128)(2,1)}, u32[]{:S(2)}, u32[]{:S(2)}) async-start(bf16[8,5,32,256]{3,2,1,0:T(8,128)(2,1)} %copy-done.3), calls=%async_computation | async-start | bytes 1310720 | tf_op jit(solution)/shard_map/all_to_all | solution.py:295
  56.0 0.0 copy-start.7
  56.0 0.0 collective-permute-done.7.n1_ref
  56.0 2.6 %collective-permute-done.8.m0_ref = bf16[1472,256]{1,0:T(8,128)(2,1)} collective-permute-done((bf16[1472,256]{1,0:T(8,128)(2,1)}, bf16[1472,256]{1,0:T(8,128)(2,1)}, u32[]{:S(2)}, u32[]{:S(2)}) %collective-permute-start.8) | collective-permute-done | bytes 753696 | tf_op jit(solution)/shard_map/ppermute | solution.py:248
  58.6 2.8 %maximum_select_fusion = bf16[2944,256]{1,0:T(8,128)(2,1)} fusion(bf16[1472,256]{1,0:T(8,128)(2,1)} %collective-permute-done.7.n1_ref, bf16[1472,256]{1,0:T(8,128)(2,1)S(1)} %collective-permute-done.n_ref.n0_ref, bf16[1472,256]{1,0:T(8,128)(2,1)S(1)} %collective-permute-done.1.m_ref.m1_ref, bf16[1472,256]{1,0:T(8,128)(2,1)} %collective-permute-done.8.m0_ref, ...), kind=kLoop, calls=%fused_computation | loop fusion | flops 6782976 | bytes 4521985 | tf_op jit(solution)/shard_map/jit(_where)/select_n | solution.py:325
  61.4 1.9 %collective-permute-start.9 = (bf16[2944,256]{1,0:T(8,128)(2,1)}, bf16[2944,256]{1,0:T(8,128)(2,1)}, u32[]{:S(2)}, u32[]{:S(2)}) collective-permute-start(bf16[2944,256]{1,0:T(8,128)(2,1)} %maximum_select_fusion), channel_id=1, source_target_pairs={{0,8},{8,0},{16,24},{24,16},{32,40},{40,32},{48,56},{56,48},{64,72... | collective-permute-start | bytes 4521992 | tf_op jit(solution)/shard_map/ppermute | solution.py:251
  63.4 16.5 %all-to-all-done.parts_ref = bf16[8,5,32,256]{3,2,1,0:T(8,128)(2,1)} async-done(((bf16[8,5,32,256]{3,2,1,0:T(8,128)(2,1)}), bf16[8,5,32,256]{3,2,1,0:T(8,128)(2,1)}, u32[]{:S(2)}, u32[]{:S(2)}) %all-to-all-start) | async-done | bytes 655392 | tf_op jit(solution)/shard_map/all_to_all | solution.py:295
  79.9 1.2 pack.1
  81.1 1.9 %collective-permute-start.4 = (bf16[80,256]{1,0:T(8,128)(2,1)S(1)}, bf16[80,256]{1,0:T(8,128)(2,1)S(1)}, u32[]{:S(2)}, u32[]{:S(2)}) collective-permute-start(bf16[80,256]{1,0:T(8,128)(2,1)S(1)} %get-tuple-element.22), channel_id=1, source_target_pairs={{0,752},{8,760},{16,0},{24,8},{32,16},{40,24},{48,32},{56,40},{64,... | collective-permute-start | bytes 122888 | tf_op jit(solution)/shard_map/ppermute | solution.py:248
  83.0 3.9 %collective-permute-start.5 = (bf16[80,256]{1,0:T(8,128)(2,1)S(1)}, bf16[80,256]{1,0:T(8,128)(2,1)S(1)}, u32[]{:S(2)}, u32[]{:S(2)}) collective-permute-start(bf16[80,256]{1,0:T(8,128)(2,1)S(1)} %get-tuple-element.23), channel_id=1, source_target_pairs={{0,16},{8,24},{16,32},{24,40},{32,48},{40,56},{48,64},{56,72},{64,... | collective-permute-start | bytes 122888 | tf_op jit(solution)/shard_map/ppermute | solution.py:248
  86.9 1.9 %collective-permute-start.6 = (bf16[32,256]{1,0:T(8,128)(2,1)S(1)}, bf16[32,256]{1,0:T(8,128)(2,1)S(1)}, u32[]{:S(2)}, u32[]{:S(2)}) collective-permute-start(bf16[32,256]{1,0:T(8,128)(2,1)S(1)} %get-tuple-element.24), channel_id=1, source_target_pairs={{0,8},{8,0},{16,24},{24,16},{32,40},{40,32},{48,56},{56,48},{64,72... | collective-permute-start | bytes 49160 | tf_op jit(solution)/shard_map/ppermute | solution.py:251
  88.8 1.1 collective-permute-done.6.refs_5_
  90.0 0.0 collective-permute-done.4.refs_3_
  90.0 1.0 collective-permute-done.5.refs_4_
  91.0 0.0 copy-done.7
  91.0 0.8 amplitude.1
  91.8 0.0 copy-start.4
  91.8 0.8 copy-done.4
  92.6 5.8 %all-to-all-start.1 = ((bf16[8,5,32,256]{3,2,1,0:T(8,128)(2,1)}), bf16[8,5,32,256]{3,2,1,0:T(8,128)(2,1)}, u32[]{:S(2)}, u32[]{:S(2)}) async-start(bf16[8,5,32,256]{3,2,1,0:T(8,128)(2,1)} %copy-done.4), calls=%async_computation.1 | async-start | bytes 1310720 | tf_op jit(solution)/shard_map/all_to_all | solution.py:322
  98.4 0.0 collective-permute-done.9.x_ref
  98.5 18.2 %all-to-all-done.1.amps_ref = bf16[8,5,32,256]{3,2,1,0:T(8,128)(2,1)} async-done(((bf16[8,5,32,256]{3,2,1,0:T(8,128)(2,1)}), bf16[8,5,32,256]{3,2,1,0:T(8,128)(2,1)}, u32[]{:S(2)}, u32[]{:S(2)}) %all-to-all-start.1) | async-done | bytes 655392 | tf_op jit(solution)/shard_map/all_to_all | solution.py:322
  116.7 0.0 copy-start.2
  116.7 1.4 %copy-done.2 = bf16[2944,256]{1,0:T(8,128)(2,1)S(1)} copy-done((bf16[2944,256]{1,0:T(8,128)(2,1)S(1)}, bf16[2944,256]{1,0:T(8,128)(2,1)}, u32[]{:S(2)}) %copy-start.2) | copy-done | bytes 1507352
  118.0 6.7 %gamma.1 = bf16[2944,256]{1,0:T(8,128)(2,1)} custom-call(s32[8]{0:T(128)S(1)} %copy-done.6, bf16[8,5,32,256]{3,2,1,0:T(8,128)(2,1)} %all-to-all-done.1.amps_ref, bf16[2944,256]{1,0:T(8,128)(2,1)S(1)} %copy-done, bf16[2944,256]{1,0:T(8,128)(2,1)S(1)} %copy-done.2, bf16[1472,256]{1,0:T(8,128)(2,1)S(1)} %collective-permute-done.n_ref.n0_ref, ...), custom_call_target="tpu_custom_call" | custom-call | flops 1929379840 | bytes 10551296 | tf_op jit(solution)/shard_map/gamma/pallas_call | solution.py:335
Async XLA Ops:
  0.0 32.2 %copy-start = (bf16[2944,256]{1,0:T(8,128)(2,1)S(1)}, bf16[2944,256]{1,0:T(8,128)(2,1)}, u32[]{:S(2)}) copy-start(bf16[2944,256]{1,0:T(8,128)(2,1)} %o_ref.1) | copy-start | bytes 4521988
  0.0 27.1 %copy-start.8 = (f32[4]{0:T(128)S(1)}, f32[4]{0:T(128)}, u32[]{:S(2)}) copy-start(f32[4]{0:T(128)} %energy_ref.1) | copy-start | bytes 52
  0.0 32.2 %copy-start.6 = (s32[8]{0:T(128)S(1)}, s32[8]{0:T(128)}, u32[]{:S(2)}) copy-start(s32[8]{0:T(128)} %aux_ref.3) | copy-start | bytes 100
  0.0 32.1 %copy-start.5 = (f32[64]{0:T(128)S(1)}, f32[64]{0:T(128)}, u32[]{:S(2)}) copy-start(f32[64]{0:T(128)} %param.7) | copy-start | bytes 772
  0.0 32.0 %collective-permute-start.3 = (bf16[2944,256]{1,0:T(8,128)(2,1)}, bf16[2944,256]{1,0:T(8,128)(2,1)S(1)}, u32[]{:S(2)}, u32[]{:S(2)}) collective-permute-start(bf16[2944,256]{1,0:T(8,128)(2,1)} %o_ref.1), channel_id=1, source_target_pairs={{0,8},{8,0},{16,24},{24,16},{32,40},{40,32},{48,56},{56,48},{64,72... | collective-permute-start | bytes 4521992 | tf_op jit(solution)/shard_map/ppermute | solution.py:251
  4.7 31.9 %collective-permute-start = (bf16[1472,256]{1,0:T(8,128)(2,1)}, bf16[1472,256]{1,0:T(8,128)(2,1)S(1)}, u32[]{:S(2)}, u32[]{:S(2)}) collective-permute-start(bf16[1472,256]{1,0:T(8,128)(2,1)} %get-tuple-element.26), channel_id=1, source_target_pairs={{0,752},{8,760},{16,0},{24,8},{32,16},{40,24},{48,32},{56,40},{64,... | collective-permute-start | bytes 2261000 | tf_op jit(solution)/shard_map/ppermute | solution.py:248
  19.1 23.9 %collective-permute-start.1 = (bf16[1472,256]{1,0:T(8,128)(2,1)}, bf16[1472,256]{1,0:T(8,128)(2,1)S(1)}, u32[]{:S(2)}, u32[]{:S(2)}) collective-permute-start(bf16[1472,256]{1,0:T(8,128)(2,1)} %get-tuple-element.25), channel_id=1, source_target_pairs={{0,16},{8,24},{16,32},{24,40},{32,48},{40,56},{48,64},{56,72},{64,... | collective-permute-start | bytes 2261000 | tf_op jit(solution)/shard_map/ppermute | solution.py:248
  21.1 34.9 %collective-permute-start.7 = (bf16[1472,256]{1,0:T(8,128)(2,1)}, bf16[1472,256]{1,0:T(8,128)(2,1)}, u32[]{:S(2)}, u32[]{:S(2)}) collective-permute-start(bf16[1472,256]{1,0:T(8,128)(2,1)} %get-tuple-element.25), channel_id=1, source_target_pairs={{0,752},{8,760},{16,0},{24,8},{32,16},{40,24},{48,32},{56,40},{64,... | collective-permute-start | bytes 2261000 | tf_op jit(solution)/shard_map/ppermute | solution.py:248
  27.1 3.0 %collective-permute-start.2 = (f32[4]{0:T(128)S(1)}, f32[4]{0:T(128)S(1)}, u32[]{:S(2)}, u32[]{:S(2)}) collective-permute-start(f32[4]{0:T(128)S(1)} %copy-done.8), channel_id=1, source_target_pairs={{0,8},{8,0},{16,24},{24,16},{32,40},{40,32},{48,56},{56,48},{64,72... | collective-permute-start | bytes 56 | tf_op jit(solution)/shard_map/ppermute | solution.py:251
  30.1 28.5 %collective-permute-start.8 = (bf16[1472,256]{1,0:T(8,128)(2,1)}, bf16[1472,256]{1,0:T(8,128)(2,1)}, u32[]{:S(2)}, u32[]{:S(2)}) collective-permute-start(bf16[1472,256]{1,0:T(8,128)(2,1)} %get-tuple-element.26), channel_id=1, source_target_pairs={{0,16},{8,24},{16,32},{24,40},{32,48},{40,56},{48,64},{56,72},{64,... | collective-permute-start | bytes 2261000 | tf_op jit(solution)/shard_map/ppermute | solution.py:248
  32.1 2.4 %copy-start.1 = (bf16[2944,256]{1,0:T(8,128)(2,1)}, bf16[2944,256]{1,0:T(8,128)(2,1)S(1)}, u32[]{:S(2)}) copy-start(bf16[2944,256]{1,0:T(8,128)(2,1)S(1)} %collective-permute-done.3.p_ref) | copy-start | bytes 4521988
  45.5 0.9 copy-start.3
  46.4 33.5 %all-to-all-start = ((bf16[8,5,32,256]{3,2,1,0:T(8,128)(2,1)}), bf16[8,5,32,256]{3,2,1,0:T(8,128)(2,1)}, u32[]{:S(2)}, u32[]{:S(2)}) async-start(bf16[8,5,32,256]{3,2,1,0:T(8,128)(2,1)} %copy-done.3), calls=%async_computation | async-start | bytes 1310720 | tf_op jit(solution)/shard_map/all_to_all | solution.py:295
  56.0 35.0 %copy-start.7 = (s32[96]{0:T(128)S(1)}, s32[96]{0:T(128)}, u32[]{:S(2)}) copy-start(s32[96]{0:T(128)} %refs_0_.1) | copy-start | bytes 1156
  61.4 37.0 %collective-permute-start.9 = (bf16[2944,256]{1,0:T(8,128)(2,1)}, bf16[2944,256]{1,0:T(8,128)(2,1)}, u32[]{:S(2)}, u32[]{:S(2)}) collective-permute-start(bf16[2944,256]{1,0:T(8,128)(2,1)} %maximum_select_fusion), channel_id=1, source_target_pairs={{0,8},{8,0},{16,24},{24,16},{32,40},{40,32},{48,56},{56,48},{64,72... | collective-permute-start | bytes 4521992 | tf_op jit(solution)/shard_map/ppermute | solution.py:251
  81.1 8.9 %collective-permute-start.4 = (bf16[80,256]{1,0:T(8,128)(2,1)S(1)}, bf16[80,256]{1,0:T(8,128)(2,1)S(1)}, u32[]{:S(2)}, u32[]{:S(2)}) collective-permute-start(bf16[80,256]{1,0:T(8,128)(2,1)S(1)} %get-tuple-element.22), channel_id=1, source_target_pairs={{0,752},{8,760},{16,0},{24,8},{32,16},{40,24},{48,32},{56,40},{64,... | collective-permute-start | bytes 122888 | tf_op jit(solution)/shard_map/ppermute | solution.py:248
  83.0 8.0 %collective-permute-start.5 = (bf16[80,256]{1,0:T(8,128)(2,1)S(1)}, bf16[80,256]{1,0:T(8,128)(2,1)S(1)}, u32[]{:S(2)}, u32[]{:S(2)}) collective-permute-start(bf16[80,256]{1,0:T(8,128)(2,1)S(1)} %get-tuple-element.23), channel_id=1, source_target_pairs={{0,16},{8,24},{16,32},{24,40},{32,48},{40,56},{48,64},{56,72},{64,... | collective-permute-start | bytes 122888 | tf_op jit(solution)/shard_map/ppermute | solution.py:248
  86.9 3.1 %collective-permute-start.6 = (bf16[32,256]{1,0:T(8,128)(2,1)S(1)}, bf16[32,256]{1,0:T(8,128)(2,1)S(1)}, u32[]{:S(2)}, u32[]{:S(2)}) collective-permute-start(bf16[32,256]{1,0:T(8,128)(2,1)S(1)} %get-tuple-element.24), channel_id=1, source_target_pairs={{0,8},{8,0},{16,24},{24,16},{32,40},{40,32},{48,56},{56,48},{64,72... | collective-permute-start | bytes 49160 | tf_op jit(solution)/shard_map/ppermute | solution.py:251
  91.8 0.9 copy-start.4
  92.6 24.0 %all-to-all-start.1 = ((bf16[8,5,32,256]{3,2,1,0:T(8,128)(2,1)}), bf16[8,5,32,256]{3,2,1,0:T(8,128)(2,1)}, u32[]{:S(2)}, u32[]{:S(2)}) async-start(bf16[8,5,32,256]{3,2,1,0:T(8,128)(2,1)} %copy-done.4), calls=%async_computation.1 | async-start | bytes 1310720 | tf_op jit(solution)/shard_map/all_to_all | solution.py:322
  116.7 1.4 %copy-start.2 = (bf16[2944,256]{1,0:T(8,128)(2,1)S(1)}, bf16[2944,256]{1,0:T(8,128)(2,1)}, u32[]{:S(2)}) copy-start(bf16[2944,256]{1,0:T(8,128)(2,1)} %copy-done.1) | copy-start | bytes 4521988

commit v3 on v0

v3 whole, which is shorter than its diff:
```python
import jax
import jax.numpy as jnp
from jax import lax
from jax.experimental import pallas as pl
from jax.experimental.pallas import tpu as pltpu
from jax.sharding import Mesh, PartitionSpec as P


BF = jnp.bfloat16
F32 = jnp.float32
VM = pl.BlockSpec(memory_space=pltpu.VMEM)
SM = pl.BlockSpec(memory_space=pltpu.SMEM)
ANY = pl.BlockSpec(memory_space=pl.ANY)


def mm(a, b):
    return jnp.dot(a, b, preferred_element_type=F32)


def keep_rows(block, start, count):
    row = lax.broadcasted_iota(jnp.int32, block.shape, 0) + start
    return jnp.where(row < count, block, jnp.zeros((), block.dtype))


def place():
    return lax.axis_index("ch"), lax.axis_index("core"), lax.axis_index("grp")


def piece_start(piece):
    return (lax.axis_index("core") * lax.axis_size("grp") + lax.axis_index("grp")) * piece


def at(count_ref, index):
    slabs = count_ref.shape[0]
    return count_ref[lax.rem(index + slabs, slabs)]


def three_terms(value):
    hi = value.astype(BF)
    rest = value - hi.astype(F32)
    mid = rest.astype(BF)
    low = (rest - mid.astype(F32)).astype(BF)
    return [hi.astype(F32), mid.astype(F32), low.astype(F32)]


def prep_kernel(
    aux_ref, energy_ref, other_ref, vir_ref, vir_rows_ref, own_ref, p_ref,
    o0t_ref, o1t_ref, pt_ref, near_ref, gaps_ref, head_ref,
):
    _, parity, g = place()
    rows, cols = own_ref.shape
    half = rows // 2
    members, _, piece, _ = near_ref.shape
    nv = vir_ref.shape[1]
    count = aux_ref[g]
    o0t_ref[...] = keep_rows(own_ref[:half, :], 0, count).T
    o1t_ref[...] = keep_rows(own_ref[half:, :], half, count).T

    def put(j, pair):
        near_ref[:, j] = pair.reshape(members, piece, cols).astype(BF)

    put(0, mm(o0t_ref[...], own_ref[:half, :]) + mm(o1t_ref[...], own_ref[half:, :]))

    @pl.when(parity == 0)
    def _():
        pt_ref[...] = keep_rows(p_ref[:half, :], 0, count).T
        put(1, mm(o0t_ref[...], p_ref[:half, :]))

    @pl.when(parity == 1)
    def _():
        pt_ref[...] = keep_rows(p_ref[half:, :], half, count).T
        put(1, mm(pt_ref[...], own_ref[half:, :]))

    slots = cols // nv
    first_row = piece_start(piece)
    slot = first_row // nv
    lane = lax.broadcasted_iota(jnp.int32, (1, cols), 1)
    vir = jnp.concatenate([vir_ref[...]] * slots, axis=1)
    even = parity == 0
    levels = [
        [jnp.where(even, energy_ref[k], other_ref[k]) for k in range(slots)],
        [jnp.where(even, other_ref[k], energy_ref[k]) for k in range(slots)],
    ]
    rows_out = []
    for level_of in levels:
        level = jnp.zeros((1, cols), F32)
        for k in range(slots):
            level = jnp.where(lane // nv == k, level_of[k], level)
        rows_out.append(level - vir)
    for level_of in levels:
        level = jnp.zeros((1, cols), F32)
        for k in range(slots):
            level = jnp.where(slot == k, level_of[k], level)
        rows_out.append(level)
    terms = []
    for row in rows_out:
        terms += three_terms(row)
    zero = jnp.zeros((4, cols), F32)
    head_ref[...] = jnp.concatenate(terms + [zero], axis=0).astype(BF)
    start = pl.multiple_of(lax.rem(first_row, nv), piece)
    gaps_ref[0:8, :] = jnp.concatenate(rows_out + [zero], axis=0)
    gaps_ref[8:, :] = vir_rows_ref[pl.ds(start, piece), :]


def far_kernel(n_ref, m_ref, o0t_ref, o1t_ref, pt_ref, near_ref, out_ref):
    _, parity, _ = place()
    members, _, piece, cols = out_ref.shape

    def put(j, pair):
        out_ref[:, j] = pair.reshape(members, piece, cols).astype(BF)

    out_ref[:, 0:2] = near_ref[...]
    put(2, mm(o0t_ref[...], n_ref[...]).T)
    put(3, mm(o1t_ref[...], m_ref[...]))

    @pl.when(parity == 0)
    def _():
        put(4, mm(pt_ref[...], n_ref[...]).T)

    @pl.when(parity == 1)
    def _():
        put(4, mm(pt_ref[...], m_ref[...]))


def pack_kernel(parts_ref, head_ref, sum_ref, up_ref, down_ref):
    members = parts_ref.shape[0]
    even = jnp.sum(parts_ref[:members // 2].astype(F32), axis=0)
    odd = jnp.sum(parts_ref[members // 2:].astype(F32), axis=0)
    size = head_ref.shape[0]
    pairs = [
        even[0], odd[0], even[1] + odd[1], even[2], odd[2], even[4], even[3], odd[3], odd[4],
    ]
    for j, pair in enumerate(pairs):
        sum_ref[j] = pair
    for first_pair, ref in ((3, up_ref), (6, down_ref)):
        for j in range(3):
            ref[j * size:(j + 1) * size, :] = pairs[first_pair + j].astype(BF)
        ref[3 * size:, :] = head_ref[...]


def amplitude_kernel(nv, count_ref, sum_ref, gaps_ref, above_ref, below_ref, out_ref):
    chip, _, _ = place()
    members, _, size, cols = out_ref.shape
    slot = piece_start(size) // nv
    vir = gaps_ref[8:, :]
    lane = lax.broadcasted_iota(jnp.int32, (size, cols), 1)

    def heads(ref):
        block = ref[3 * size:, :].astype(F32)
        return [block[3 * j:3 * j + 1] + block[3 * j + 1:3 * j + 2] + block[3 * j + 2:3 * j + 3] for j in range(4)]

    def slab_pair(gaps, position):
        counts = [at(count_ref, 2 * position + j) for j in range(2)]
        return [(gaps[j], gaps[2 + j] - vir, counts[j]) for j in range(2)]

    here = slab_pair([gaps_ref[j:j + 1, :] for j in range(4)], chip)
    upper = slab_pair(heads(above_ref), chip + 1)
    lower = slab_pair(heads(below_ref), chip - 1)

    def amp(pair, row_slab, col_slab):
        keep = (lane < col_slab[2] * nv) & (slot < row_slab[2])
        return jnp.where(keep, pair / (row_slab[1] + col_slab[0]), 0.0).astype(BF)

    def send(core, j, value):
        for member in range(core * members // 2, (core + 1) * members // 2):
            out_ref[member, j] = value

    def other(ref, j):
        return ref[j * size:(j + 1) * size, :].astype(F32)

    for core in range(2):
        send(core, 0, amp(sum_ref[core], here[core], here[core]))
        send(core, 2, amp(sum_ref[3 + core] + other(above_ref, core), upper[core], here[core]))
        send(core, 3, amp(sum_ref[6 + core] + other(below_ref, core), here[core], lower[core]))
    both = amp(sum_ref[2], here[0], here[1])
    send(0, 1, both)
    send(1, 1, both)
    send(0, 4, amp(sum_ref[8] + other(below_ref, 2), here[0], lower[1]))
    send(1, 4, amp(sum_ref[5] + other(above_ref, 2), upper[0], here[1]))


def gamma_kernel(
    aux_ref, amps_ref, o_ref, p_ref, n0_ref, n1_ref, m0_ref, m1_ref, x_ref, out_ref, result, weights, sems
):
    rows, cols = o_ref.shape
    half = rows // 2
    _, parity, g = place()

    def put(j, turned):
        matrix = amps_ref[:, j].reshape(cols, cols)
        weights[j * cols:(j + 1) * cols, :] = matrix.T if turned else matrix

    put(0, False)
    put(2, False)
    put(3, True)

    @pl.when(parity == 0)
    def _():
        put(1, True)
        put(4, True)

    @pl.when(parity == 1)
    def _():
        put(1, False)
        put(4, False)

    tile = rows // sems.shape[0]
    copies = []
    for j in range(sems.shape[0]):
        start = j * tile
        n_ref, m_ref, low = (n0_ref, m0_ref, start) if start < half else (n1_ref, m1_ref, start - half)
        here, there = pl.ds(start, tile), pl.ds(low, tile)
        blocks = jnp.concatenate(
            [o_ref[here, :], p_ref[here, :], n_ref[there, :], m_ref[there, :], x_ref[here, :]], axis=1
        )
        result[here, :] = keep_rows(mm(blocks, weights[...]), start, aux_ref[g]).astype(result.dtype)
        copy = pltpu.make_async_copy(result.at[here, :], out_ref.at[here, :], sems.at[j])
        copy.start()
        copies.append(copy)
    for copy in copies:
        copy.wait()


def cost(flops, size):
    return pl.CostEstimate(flops=flops, bytes_accessed=size, transcendentals=0)


def memory(mebibytes):
    return pltpu.CompilerParams(vmem_limit_bytes=mebibytes << 20)


def per_device(three_index, occ_energy, vir_energy, aux_count, occ_count):
    rows, cols = three_index.shape
    half = rows // 2
    nv = vir_energy.shape[0]
    chips = lax.axis_size("ch")
    members = 2 * lax.axis_size("grp")
    piece = cols // members

    def shift(value, steps):
        return lax.ppermute(value, "ch", [(i, (i + steps) % chips) for i in range(chips)])

    def swap(value):
        return lax.ppermute(value, "core", [(0, 1), (1, 0)])

    def exchange(value):
        return lax.all_to_all(value, ("core", "grp"), 0, 0)

    def shape(*dims, dtype=BF):
        return jax.ShapeDtypeStruct(dims, dtype)

    own = three_index
    lower, upper = own[:half], own[half:]
    n0 = shift(lower, -1)
    m1 = shift(upper, 1)
    partner = swap(own)
    n1 = shift(upper, -1)
    m0 = shift(lower, 1)
    partner_energy = swap(occ_energy)

    o0t, o1t, pt, near, gaps, head = pl.pallas_call(
        prep_kernel,
        in_specs=[SM, SM, SM, VM, VM, VM, VM],
        out_specs=[VM] * 6,
        out_shape=[
            shape(cols, half), shape(cols, half), shape(cols, half), shape(members, 2, piece, cols),
            shape(8 + piece, cols, dtype=F32), shape(16, cols),
        ],
        cost_estimate=cost(3 * rows * cols * cols, 8 * rows * cols),
        compiler_params=memory(16),
        name="prep",
    )(
        aux_count, occ_energy, partner_energy, vir_energy[None, :],
        jnp.broadcast_to(vir_energy[:, None], (nv, cols)), own, partner,
    )

    parts = shape(members, 5, piece, cols)
    partial_sums = pl.pallas_call(
        far_kernel,
        in_specs=[VM] * 6,
        out_specs=VM,
        out_shape=parts,
        cost_estimate=cost(3 * rows * cols * cols, 5 * rows * cols),
        compiler_params=memory(12),
        name="far",
    )(n0, m1, o0t, o1t, pt, near)
    pieces = exchange(partial_sums)
    message = shape(3 * piece + 16, cols)
    sums, up, down = pl.pallas_call(
        pack_kernel,
        in_specs=[VM, VM],
        out_specs=[VM] * 3,
        out_shape=[shape(9, piece, cols, dtype=F32), message, message],
        cost_estimate=cost(cols * cols, 4 * cols * cols),
        compiler_params=memory(6),
        name="pack",
    )(pieces, head)
    below = shift(up, 1)
    above = shift(down, -1)
    amps = pl.pallas_call(
        lambda *refs: amplitude_kernel(nv, *refs),
        in_specs=[SM] + [VM] * 4,
        out_specs=VM,
        out_shape=parts,
        cost_estimate=cost(cols * cols, 8 * cols * cols),
        compiler_params=memory(6),
        name="amplitude",
    )(occ_count, sums, gaps, above, below)
    amps = exchange(amps)
    fifth = swap(jnp.where(
        lax.axis_index("core") == 0, jnp.concatenate([n0, n1], axis=0), jnp.concatenate([m0, m1], axis=0)
    ))

    tiles = 8
    return pl.pallas_call(
        gamma_kernel,
        in_specs=[SM] + [VM] * 8,
        out_specs=ANY,
        out_shape=jax.ShapeDtypeStruct((rows, cols), three_index.dtype),
        scratch_shapes=[
            pltpu.VMEM((rows, cols), three_index.dtype), pltpu.VMEM((5 * cols, cols), BF),
            pltpu.SemaphoreType.DMA((tiles,)),
        ],
        cost_estimate=cost(10 * rows * cols * cols, 14 * rows * cols),
        compiler_params=memory(20),
        name="gamma",
    )(aux_count, amps, own, partner, n0, n1, m0, m1, fifth)


def solution(mesh):
    chips = mesh.shape["blk"] // 2
    cores = Mesh(mesh.devices.reshape(chips, 2, mesh.shape["grp"]), ("ch", "core", "grp"))
    blocks = P("grp", ("ch", "core"))
    return jax.shard_map(
        per_device, mesh=cores, in_specs=(blocks, P(("ch", "core")), P(), P(), P()), out_specs=blocks,
        check_vma=False,
    )
```

time: 254 us -> 128 us (0.50)
  the two profiles are of different devices: /device:TPU:1 before, /device:TPU:8 now
where the time goes in v3:
time: 128 us; the launch traced here: 127 us
  waiting for transfers between devices  58 us (45%)
  starting transfers between devices  50.1 us (39%)
  Pallas kernels  9.84 us (8%)
  local copies, waits for them, and re-layouts  5.82 us (5%)
  other arithmetic  2.82 us (2%)
    all_to_all x2, waiting for transfers between devices, exchange(): return lax.all_to_all(value, ('core', 'grp'), 0, 0)  40.1 us
    ppermute x6, starting transfers between devices, shift(): lax.ppermute(value, 'ch', [(i, (i + steps) % chips) for i in range(chips)])  30.2 us
    ppermute x6, waiting for transfers between devices, shift(): lax.ppermute(value, 'ch', [(i, (i + steps) % chips) for i in range(chips)])  16.9 us
    all_to_all x2, starting transfers between devices, exchange(): return lax.all_to_all(value, ('core', 'grp'), 0, 0)  14 us
    ppermute x3, starting transfers between devices, swap(): return lax.ppermute(value, 'core', [(0, 1), (1, 0)])  5.88 us
    pallas_call x1, Pallas kernels, per_device(): pl.pallas_call(gamma_kernel, in_specs=[SM] + [VM] * 8, out_specs=ANY, out...  5.19 us
    unnamed x18, local copies, waits for them, and re-layouts  3.14 us
    select_n x1, other arithmetic, per_device(): jnp.where(lax.axis_index('core') == 0, jnp.concatenate([n0, n1], axis=0),...  2.82 us
  transfers between devices with their start and end apart: 11, of which 7 were waited for; matrix products, arithmetic and copies ran while one was open for 4% of the time, Pallas kernels for 4%

profile of v3, /device:TPU:8, one launch (start us, length us, event | category | flops | bytes accessed | tf_op | source)
XLA Modules:
  0.0 126.8 jit_solution(13216563320605899197)
XLA Ops:
  0.0 0.0 copy-start
  0.0 0.0 copy-start.8
  0.0 0.0 copy-start.5
  0.0 0.0 copy-start.6
  0.0 2.1 %collective-permute-start.3 = (bf16[2944,256]{1,0:T(8,128)(2,1)}, bf16[2944,256]{1,0:T(8,128)(2,1)S(1)}, u32[]{:S(2)}, u32[]{:S(2)}) collective-permute-start(bf16[2944,256]{1,0:T(8,128)(2,1)} %o_ref.1), channel_id=1, source_target_pairs={{0,8},{8,0},{1,9},{9,1},{2,10},{10,2},{3,11},{11,3},{4,12},{12,4},... | collective-permute-start | bytes 4521992 | tf_op jit(solution)/shard_map/ppermute | solution.py:244
  2.1 2.6 %fusion = (bf16[1472,256]{1,0:T(8,128)(2,1)}, bf16[1472,256]{1,0:T(8,128)(2,1)}) fusion(bf16[2944,256]{1,0:T(8,128)(2,1)} %o_ref.1), kind=kLoop, calls=%fused_computation.1 | loop fusion | bytes 3014656 | tf_op jit(solution)/shard_map/slice | solution.py:253
  4.7 14.5 %collective-permute-start = (bf16[1472,256]{1,0:T(8,128)(2,1)}, bf16[1472,256]{1,0:T(8,128)(2,1)S(1)}, u32[]{:S(2)}, u32[]{:S(2)}) collective-permute-start(bf16[1472,256]{1,0:T(8,128)(2,1)} %get-tuple-element.24), channel_id=1, source_target_pairs={{0,752},{16,0},{32,16},{48,32},{64,48},{80,64},{96,80},{112,96},{1... | collective-permute-start | bytes 2261000 | tf_op jit(solution)/shard_map/ppermute | solution.py:241
  19.1 1.9 %collective-permute-start.1 = (bf16[1472,256]{1,0:T(8,128)(2,1)}, bf16[1472,256]{1,0:T(8,128)(2,1)S(1)}, u32[]{:S(2)}, u32[]{:S(2)}) collective-permute-start(bf16[1472,256]{1,0:T(8,128)(2,1)} %get-tuple-element.23), channel_id=1, source_target_pairs={{0,16},{16,32},{32,48},{48,64},{64,80},{80,96},{96,112},{112,128},... | collective-permute-start | bytes 2261000 | tf_op jit(solution)/shard_map/ppermute | solution.py:241
  21.1 6.0 %collective-permute-start.6 = (bf16[1472,256]{1,0:T(8,128)(2,1)}, bf16[1472,256]{1,0:T(8,128)(2,1)}, u32[]{:S(2)}, u32[]{:S(2)}) collective-permute-start(bf16[1472,256]{1,0:T(8,128)(2,1)} %get-tuple-element.23), channel_id=1, source_target_pairs={{0,752},{16,0},{32,16},{48,32},{64,48},{80,64},{96,80},{112,96},{1... | collective-permute-start | bytes 2261000 | tf_op jit(solution)/shard_map/ppermute | solution.py:241
  27.1 0.0 copy-done.8
  27.1 1.9 %collective-permute-start.2 = (f32[4]{0:T(128)S(1)}, f32[4]{0:T(128)S(1)}, u32[]{:S(2)}, u32[]{:S(2)}) collective-permute-start(f32[4]{0:T(128)S(1)} %copy-done.8), channel_id=1, source_target_pairs={{0,8},{8,0},{1,9},{9,1},{2,10},{10,2},{3,11},{11,3},{4,12},{12,4},... | collective-permute-start | bytes 56 | tf_op jit(solution)/shard_map/ppermute | solution.py:244
  29.1 1.1 collective-permute-done.2.other_ref
  30.1 1.9 %collective-permute-start.7 = (bf16[1472,256]{1,0:T(8,128)(2,1)}, bf16[1472,256]{1,0:T(8,128)(2,1)}, u32[]{:S(2)}, u32[]{:S(2)}) collective-permute-start(bf16[1472,256]{1,0:T(8,128)(2,1)} %get-tuple-element.24), channel_id=1, source_target_pairs={{0,16},{16,32},{32,48},{48,64},{64,80},{80,96},{96,112},{112,128},... | collective-permute-start | bytes 2261000 | tf_op jit(solution)/shard_map/ppermute | solution.py:241
  32.1 0.0 collective-permute-done.3.p_ref
  32.1 0.0 copy-done.5
  32.1 0.0 copy-start.1
  32.1 0.1 broadcast_in_dim.10.vir_rows_ref
  32.2 0.0 copy-done
  32.2 0.0 copy-done.6
  32.2 1.8 %prep.1 = (bf16[256,1472]{1,0:T(8,128)(2,1)S(1)}, bf16[256,1472]{1,0:T(8,128)(2,1)S(1)}, bf16[256,1472]{1,0:T(8,128)(2,1)S(1)}, bf16[16,2,16,256]{3,2,1,0:T(8,12...) custom-call(s32[8]{0:T(128)S(1)} %copy-done.6, f32[4]{0:T(128)S(1)} %copy-done.8, ...), custom_call_target="tpu_custom_call" | custom-call | flops 578813952 | bytes 6029312 | tf_op jit(solution)/shard_map/prep/pallas_call | solution.py:261
  34.0 0.0 copy-done.1
  34.0 2.6 %collective-permute-done.n_ref.n0_ref = bf16[1472,256]{1,0:T(8,128)(2,1)S(1)} collective-permute-done((bf16[1472,256]{1,0:T(8,128)(2,1)}, bf16[1472,256]{1,0:T(8,128)(2,1)S(1)}, u32[]{:S(2)}, u32[]{:S(2)}) %collective-permute-start) | collective-permute-done | bytes 753696 | tf_op jit(solution)/shard_map/ppermute | solution.py:241
  36.6 6.4 %collective-permute-done.1.m_ref.m1_ref = bf16[1472,256]{1,0:T(8,128)(2,1)S(1)} collective-permute-done((bf16[1472,256]{1,0:T(8,128)(2,1)}, bf16[1472,256]{1,0:T(8,128)(2,1)S(1)}, u32[]{:S(2)}, u32[]{:S(2)}) %collective-permute-start.1) | collective-permute-done | bytes 753696 | tf_op jit(solution)/shard_map/ppermute | solution.py:241
  43.0 1.1 far.1
  44.1 0.0 copy-start.3
  44.1 0.9 copy-done.3
  45.0 9.7 %all-to-all-start = ((bf16[16,5,16,256]{3,2,1,0:T(8,128)(2,1)}), bf16[16,5,16,256]{3,2,1,0:T(8,128)(2,1)}, u32[]{:S(2)}, u32[]{:S(2)}) async-start(bf16[16,5,16,256]{3,2,1,0:T(8,128)(2,1)} %copy-done.3), calls=%async_computation | async-start | bytes 1310720 | tf_op jit(solution)/shard_map/all_to_all | solution.py:247
  54.7 0.0 copy-start.7
  54.7 0.0 collective-permute-done.6.n1_ref
  54.7 3.8 %collective-permute-done.7.m0_ref = bf16[1472,256]{1,0:T(8,128)(2,1)} collective-permute-done((bf16[1472,256]{1,0:T(8,128)(2,1)}, bf16[1472,256]{1,0:T(8,128)(2,1)}, u32[]{:S(2)}, u32[]{:S(2)}) %collective-permute-start.7) | collective-permute-done | bytes 753696 | tf_op jit(solution)/shard_map/ppermute | solution.py:241
  58.6 2.8 %maximum_select_fusion = bf16[2944,256]{1,0:T(8,128)(2,1)} fusion(bf16[1472,256]{1,0:T(8,128)(2,1)} %collective-permute-done.6.n1_ref, bf16[1472,256]{1,0:T(8,128)(2,1)S(1)} %collective-permute-done.n_ref.n0_ref, bf16[1472,256]{1,0:T(8,128)(2,1)S(1)} %collective-permute-done.1.m_ref.m1_ref, bf16[1472,256]{1,0:T(8,128)(2,1)} %collective-permute-done.7.m0_ref, ...), kind=kLoop, calls=%fused_computation | loop fusion | flops 6782976 | bytes 4521985 | tf_op jit(solution)/shard_map/jit(_where)/select_n | solution.py:310
  61.4 1.9 %collective-permute-start.8 = (bf16[2944,256]{1,0:T(8,128)(2,1)}, bf16[2944,256]{1,0:T(8,128)(2,1)}, u32[]{:S(2)}, u32[]{:S(2)}) collective-permute-start(bf16[2944,256]{1,0:T(8,128)(2,1)} %maximum_select_fusion), channel_id=1, source_target_pairs={{0,8},{8,0},{1,9},{9,1},{2,10},{10,2},{3,11},{11,3},{4,12},{12,4},... | collective-permute-start | bytes 4521992 | tf_op jit(solution)/shard_map/ppermute | solution.py:244
  63.3 18.2 %all-to-all-done.parts_ref = bf16[16,5,16,256]{3,2,1,0:T(8,128)(2,1)} async-done(((bf16[16,5,16,256]{3,2,1,0:T(8,128)(2,1)}), bf16[16,5,16,256]{3,2,1,0:T(8,128)(2,1)}, u32[]{:S(2)}, u32[]{:S(2)}) %all-to-all-start) | async-done | bytes 655392 | tf_op jit(solution)/shard_map/all_to_all | solution.py:247
  81.5 1.2 pack.1
  82.7 1.9 %collective-permute-start.4 = (bf16[64,256]{1,0:T(8,128)(2,1)S(1)}, bf16[64,256]{1,0:T(8,128)(2,1)S(1)}, u32[]{:S(2)}, u32[]{:S(2)}) collective-permute-start(bf16[64,256]{1,0:T(8,128)(2,1)S(1)} %get-tuple-element.21), channel_id=1, source_target_pairs={{0,752},{16,0},{32,16},{48,32},{64,48},{80,64},{96,80},{112,96},{1... | collective-permute-start | bytes 98312 | tf_op jit(solution)/shard_map/ppermute | solution.py:241
  84.6 3.9 %collective-permute-start.5 = (bf16[64,256]{1,0:T(8,128)(2,1)S(1)}, bf16[64,256]{1,0:T(8,128)(2,1)S(1)}, u32[]{:S(2)}, u32[]{:S(2)}) collective-permute-start(bf16[64,256]{1,0:T(8,128)(2,1)S(1)} %get-tuple-element.22), channel_id=1, source_target_pairs={{0,16},{16,32},{32,48},{48,64},{64,80},{80,96},{96,112},{112,128},... | collective-permute-start | bytes 98312 | tf_op jit(solution)/shard_map/ppermute | solution.py:241
  88.6 0.0 collective-permute-done.4.refs_3_
  88.6 4.0 %collective-permute-done.5.refs_4_ = bf16[64,256]{1,0:T(8,128)(2,1)S(1)} collective-permute-done((bf16[64,256]{1,0:T(8,128)(2,1)S(1)}, bf16[64,256]{1,0:T(8,128)(2,1)S(1)}, u32[]{:S(2)}, u32[]{:S(2)}) %collective-permute-start.5) | collective-permute-done | bytes 32800 | tf_op jit(solution)/shard_map/ppermute | solution.py:241
  92.6 0.0 copy-done.7
  92.6 0.6 amplitude.1
  93.2 0.0 copy-start.4
  93.2 0.9 copy-done.4
  94.1 4.3 %all-to-all-start.1 = ((bf16[16,5,16,256]{3,2,1,0:T(8,128)(2,1)}), bf16[16,5,16,256]{3,2,1,0:T(8,128)(2,1)}, u32[]{:S(2)}, u32[]{:S(2)}) async-start(bf16[16,5,16,256]{3,2,1,0:T(8,128)(2,1)} %copy-done.4), calls=%async_computation.1 | async-start | bytes 1310720 | tf_op jit(solution)/shard_map/all_to_all | solution.py:247
  98.4 0.0 collective-permute-done.8.x_ref
  98.4 21.8 %all-to-all-done.1.amps_ref = bf16[16,5,16,256]{3,2,1,0:T(8,128)(2,1)} async-done(((bf16[16,5,16,256]{3,2,1,0:T(8,128)(2,1)}), bf16[16,5,16,256]{3,2,1,0:T(8,128)(2,1)}, u32[]{:S(2)}, u32[]{:S(2)}) %all-to-all-start.1) | async-done | bytes 655392 | tf_op jit(solution)/shard_map/all_to_all | solution.py:247
  120.2 0.0 copy-start.2
  120.2 1.4 %copy-done.2 = bf16[2944,256]{1,0:T(8,128)(2,1)S(1)} copy-done((bf16[2944,256]{1,0:T(8,128)(2,1)S(1)}, bf16[2944,256]{1,0:T(8,128)(2,1)}, u32[]{:S(2)}) %copy-start.2) | copy-done | bytes 1507352
  121.6 5.2 %gamma.1 = bf16[2944,256]{1,0:T(8,128)(2,1)} custom-call(s32[8]{0:T(128)S(1)} %copy-done.6, bf16[16,5,16,256]{3,2,1,0:T(8,128)(2,1)} %all-to-all-done.1.amps_ref, bf16[2944,256]{1,0:T(8,128)(2,1)S(1)} %copy-done, bf16[2944,256]{1,0:T(8,128)(2,1)S(1)} %copy-done.2, bf16[1472,256]{1,0:T(8,128)(2,1)S(1)} %collective-permute-done.n_ref.n0_ref, ...), custom_call_target="tpu_custom_call" | custom-call | flops 1929379840 | bytes 10551296 | tf_op jit(solution)/shard_map/gamma/pallas_call | solution.py:315
Async XLA Ops:
  0.0 32.2 %copy-start = (bf16[2944,256]{1,0:T(8,128)(2,1)S(1)}, bf16[2944,256]{1,0:T(8,128)(2,1)}, u32[]{:S(2)}) copy-start(bf16[2944,256]{1,0:T(8,128)(2,1)} %o_ref.1) | copy-start | bytes 4521988
  0.0 27.1 %copy-start.8 = (f32[4]{0:T(128)S(1)}, f32[4]{0:T(128)}, u32[]{:S(2)}) copy-start(f32[4]{0:T(128)} %energy_ref.1) | copy-start | bytes 52
  0.0 32.1 %copy-start.5 = (f32[64]{0:T(128)S(1)}, f32[64]{0:T(128)}, u32[]{:S(2)}) copy-start(f32[64]{0:T(128)} %param.7) | copy-start | bytes 772
  0.0 32.2 %copy-start.6 = (s32[8]{0:T(128)S(1)}, s32[8]{0:T(128)}, u32[]{:S(2)}) copy-start(s32[8]{0:T(128)} %aux_ref.3) | copy-start | bytes 100
  0.0 32.0 %collective-permute-start.3 = (bf16[2944,256]{1,0:T(8,128)(2,1)}, bf16[2944,256]{1,0:T(8,128)(2,1)S(1)}, u32[]{:S(2)}, u32[]{:S(2)}) collective-permute-start(bf16[2944,256]{1,0:T(8,128)(2,1)} %o_ref.1), channel_id=1, source_target_pairs={{0,8},{8,0},{1,9},{9,1},{2,10},{10,2},{3,11},{11,3},{4,12},{12,4},... | collective-permute-start | bytes 4521992 | tf_op jit(solution)/shard_map/ppermute | solution.py:244
  4.7 31.9 %collective-permute-start = (bf16[1472,256]{1,0:T(8,128)(2,1)}, bf16[1472,256]{1,0:T(8,128)(2,1)S(1)}, u32[]{:S(2)}, u32[]{:S(2)}) collective-permute-start(bf16[1472,256]{1,0:T(8,128)(2,1)} %get-tuple-element.24), channel_id=1, source_target_pairs={{0,752},{16,0},{32,16},{48,32},{64,48},{80,64},{96,80},{112,96},{1... | collective-permute-start | bytes 2261000 | tf_op jit(solution)/shard_map/ppermute | solution.py:241
  19.1 23.9 %collective-permute-start.1 = (bf16[1472,256]{1,0:T(8,128)(2,1)}, bf16[1472,256]{1,0:T(8,128)(2,1)S(1)}, u32[]{:S(2)}, u32[]{:S(2)}) collective-permute-start(bf16[1472,256]{1,0:T(8,128)(2,1)} %get-tuple-element.23), channel_id=1, source_target_pairs={{0,16},{16,32},{32,48},{48,64},{64,80},{80,96},{96,112},{112,128},... | collective-permute-start | bytes 2261000 | tf_op jit(solution)/shard_map/ppermute | solution.py:241
  21.1 33.6 %collective-permute-start.6 = (bf16[1472,256]{1,0:T(8,128)(2,1)}, bf16[1472,256]{1,0:T(8,128)(2,1)}, u32[]{:S(2)}, u32[]{:S(2)}) collective-permute-start(bf16[1472,256]{1,0:T(8,128)(2,1)} %get-tuple-element.23), channel_id=1, source_target_pairs={{0,752},{16,0},{32,16},{48,32},{64,48},{80,64},{96,80},{112,96},{1... | collective-permute-start | bytes 2261000 | tf_op jit(solution)/shard_map/ppermute | solution.py:241
  27.1 3.0 %collective-permute-start.2 = (f32[4]{0:T(128)S(1)}, f32[4]{0:T(128)S(1)}, u32[]{:S(2)}, u32[]{:S(2)}) collective-permute-start(f32[4]{0:T(128)S(1)} %copy-done.8), channel_id=1, source_target_pairs={{0,8},{8,0},{1,9},{9,1},{2,10},{10,2},{3,11},{11,3},{4,12},{12,4},... | collective-permute-start | bytes 56 | tf_op jit(solution)/shard_map/ppermute | solution.py:244
  30.1 28.4 %collective-permute-start.7 = (bf16[1472,256]{1,0:T(8,128)(2,1)}, bf16[1472,256]{1,0:T(8,128)(2,1)}, u32[]{:S(2)}, u32[]{:S(2)}) collective-permute-start(bf16[1472,256]{1,0:T(8,128)(2,1)} %get-tuple-element.24), channel_id=1, source_target_pairs={{0,16},{16,32},{32,48},{48,64},{64,80},{80,96},{96,112},{112,128},... | collective-permute-start | bytes 2261000 | tf_op jit(solution)/shard_map/ppermute | solution.py:241
  32.1 1.9 %copy-start.1 = (bf16[2944,256]{1,0:T(8,128)(2,1)}, bf16[2944,256]{1,0:T(8,128)(2,1)S(1)}, u32[]{:S(2)}) copy-start(bf16[2944,256]{1,0:T(8,128)(2,1)S(1)} %collective-permute-done.3.p_ref) | copy-start | bytes 4521988
  44.1 0.9 copy-start.3
  45.0 36.5 %all-to-all-start = ((bf16[16,5,16,256]{3,2,1,0:T(8,128)(2,1)}), bf16[16,5,16,256]{3,2,1,0:T(8,128)(2,1)}, u32[]{:S(2)}, u32[]{:S(2)}) async-start(bf16[16,5,16,256]{3,2,1,0:T(8,128)(2,1)} %copy-done.3), calls=%async_computation | async-start | bytes 1310720 | tf_op jit(solution)/shard_map/all_to_all | solution.py:247
  54.7 37.9 %copy-start.7 = (s32[96]{0:T(128)S(1)}, s32[96]{0:T(128)}, u32[]{:S(2)}) copy-start(s32[96]{0:T(128)} %refs_0_.1) | copy-start | bytes 1156
  61.4 37.0 %collective-permute-start.8 = (bf16[2944,256]{1,0:T(8,128)(2,1)}, bf16[2944,256]{1,0:T(8,128)(2,1)}, u32[]{:S(2)}, u32[]{:S(2)}) collective-permute-start(bf16[2944,256]{1,0:T(8,128)(2,1)} %maximum_select_fusion), channel_id=1, source_target_pairs={{0,8},{8,0},{1,9},{9,1},{2,10},{10,2},{3,11},{11,3},{4,12},{12,4},... | collective-permute-start | bytes 4521992 | tf_op jit(solution)/shard_map/ppermute | solution.py:244
  82.7 5.9 %collective-permute-start.4 = (bf16[64,256]{1,0:T(8,128)(2,1)S(1)}, bf16[64,256]{1,0:T(8,128)(2,1)S(1)}, u32[]{:S(2)}, u32[]{:S(2)}) collective-permute-start(bf16[64,256]{1,0:T(8,128)(2,1)S(1)} %get-tuple-element.21), channel_id=1, source_target_pairs={{0,752},{16,0},{32,16},{48,32},{64,48},{80,64},{96,80},{112,96},{1... | collective-permute-start | bytes 98312 | tf_op jit(solution)/shard_map/ppermute | solution.py:241
  84.6 7.9 %collective-permute-start.5 = (bf16[64,256]{1,0:T(8,128)(2,1)S(1)}, bf16[64,256]{1,0:T(8,128)(2,1)S(1)}, u32[]{:S(2)}, u32[]{:S(2)}) collective-permute-start(bf16[64,256]{1,0:T(8,128)(2,1)S(1)} %get-tuple-element.22), channel_id=1, source_target_pairs={{0,16},{16,32},{32,48},{48,64},{64,80},{80,96},{96,112},{112,128},... | collective-permute-start | bytes 98312 | tf_op jit(solution)/shard_map/ppermute | solution.py:241
  93.2 0.9 copy-start.4
  94.1 26.2 %all-to-all-start.1 = ((bf16[16,5,16,256]{3,2,1,0:T(8,128)(2,1)}), bf16[16,5,16,256]{3,2,1,0:T(8,128)(2,1)}, u32[]{:S(2)}, u32[]{:S(2)}) async-start(bf16[16,5,16,256]{3,2,1,0:T(8,128)(2,1)} %copy-done.4), calls=%async_computation.1 | async-start | bytes 1310720 | tf_op jit(solution)/shard_map/all_to_all | solution.py:247
  120.2 1.4 %copy-start.2 = (bf16[2944,256]{1,0:T(8,128)(2,1)S(1)}, bf16[2944,256]{1,0:T(8,128)(2,1)}, u32[]{:S(2)}) copy-start(bf16[2944,256]{1,0:T(8,128)(2,1)} %copy-done.1) | copy-start | bytes 4521988

commit v4 on v2

v4 whole, which is shorter than its diff:
```python
import jax
import jax.numpy as jnp
from jax import lax
from jax.experimental import pallas as pl
from jax.experimental.pallas import tpu as pltpu
from jax.sharding import PartitionSpec as P


BF = jnp.bfloat16
F32 = jnp.float32
VM = pl.BlockSpec(memory_space=pltpu.VMEM)
SM = pl.BlockSpec(memory_space=pltpu.SMEM)
ANY = pl.BlockSpec(memory_space=pl.ANY)


def mm(a, b):
    return jnp.dot(a, b, preferred_element_type=F32)


def keep_rows(block, start, count):
    row = lax.broadcasted_iota(jnp.int32, block.shape, 0) + start
    return jnp.where(row < count, block, jnp.zeros((), block.dtype))


def place():
    r = lax.axis_index("blk")
    return r, lax.rem(r, 2), lax.axis_index("grp")


def at(count_ref, index):
    slabs = count_ref.shape[0]
    return count_ref[lax.rem(index + slabs, slabs)]


def halves_kernel(own_ref, lower_ref, upper_ref, sems):
    half = lower_ref.shape[0]
    copies = [
        pltpu.make_async_copy(own_ref.at[j * half:(j + 1) * half], ref, sems.at[j])
        for j, ref in enumerate((lower_ref, upper_ref))
    ]
    for copy in copies:
        copy.start()
    for copy in copies:
        copy.wait()


def three_terms(value):
    hi = value.astype(BF)
    rest = value - hi.astype(F32)
    mid = rest.astype(BF)
    low = (rest - mid.astype(F32)).astype(BF)
    return [hi.astype(F32), mid.astype(F32), low.astype(F32)]


def prep_kernel(
    aux_ref, energy_ref, other_ref, vir_ref, vir_rows_ref, own_ref, p_ref,
    o0t_ref, o1t_ref, pt_ref, near_ref, gaps_ref, head_ref,
):
    _, parity, g = place()
    rows, cols = own_ref.shape
    half = rows // 2
    owners, _, piece, _ = near_ref.shape
    nv = vir_ref.shape[1]
    count = aux_ref[g]
    o0t_ref[...] = keep_rows(own_ref[:half, :], 0, count).T
    o1t_ref[...] = keep_rows(own_ref[half:, :], half, count).T

    @pl.when(parity == 0)
    def _():
        pt_ref[...] = keep_rows(p_ref[:half, :], 0, count).T

    @pl.when(parity == 1)
    def _():
        pt_ref[...] = keep_rows(p_ref[half:, :], half, count).T

    for j, ref in enumerate((own_ref, p_ref)):
        pair = mm(o0t_ref[...], ref[:half, :]) + mm(o1t_ref[...], ref[half:, :])
        near_ref[:, j] = pair.reshape(owners, piece, cols).astype(BF)

    slots = cols // nv
    slot = (g * piece) // nv
    lane = lax.broadcasted_iota(jnp.int32, (1, cols), 1)
    vir = jnp.concatenate([vir_ref[...]] * slots, axis=1)
    rows_out = []
    for ref in (energy_ref, other_ref):
        level = jnp.zeros((1, cols), F32)
        for k in range(slots):
            level = jnp.where(lane // nv == k, ref[k], level)
        rows_out.append(level - vir)
    for ref in (energy_ref, other_ref):
        rows_out.append(jnp.broadcast_to(ref[slot], (1, cols)))
    terms = []
    for row in rows_out:
        terms += three_terms(row)
    zero = jnp.zeros((4, cols), F32)
    head_ref[...] = jnp.concatenate(terms + [zero], axis=0).astype(BF)
    start = pl.multiple_of(lax.rem(g * piece, nv), piece)
    gaps_ref[0:8, :] = jnp.concatenate(rows_out + [zero], axis=0)
    gaps_ref[8:, :] = vir_rows_ref[pl.ds(start, piece), :]


def far_kernel(n_ref, m_ref, o0t_ref, o1t_ref, pt_ref, out_ref):
    _, parity, _ = place()
    owners, _, piece, cols = out_ref.shape

    def put(j, pair):
        out_ref[:, j] = pair.reshape(owners, piece, cols).astype(BF)

    put(0, mm(o0t_ref[...], n_ref[...]).T)
    put(1, mm(o1t_ref[...], m_ref[...]))

    @pl.when(parity == 0)
    def _():
        put(2, mm(pt_ref[...], n_ref[...]).T)

    @pl.when(parity == 1)
    def _():
        put(2, mm(pt_ref[...], m_ref[...]))


def pack_kernel(parts_ref, head_ref, sum_ref, up_ref, down_ref, swap_ref):
    total = jnp.sum(parts_ref[...].astype(F32), axis=0)
    sum_ref[...] = total[:2]
    extra = total[2].astype(BF)
    size = extra.shape[0]
    swap_ref[...] = extra
    for j, ref in ((0, up_ref), (1, down_ref)):
        ref[0:size, :] = total[j].astype(BF)
        ref[size:2 * size, :] = extra
        ref[2 * size:, :] = head_ref[...]


def amplitude_kernel(nv, count_ref, near_ref, sum_ref, gaps_ref, above_ref, below_ref, swap_ref, out_ref):
    r, parity, g = place()
    size, cols = swap_ref.shape
    slot = (g * size) // nv
    vir = gaps_ref[8:, :]
    own_gap = gaps_ref[0:1, :]
    own_rows = gaps_ref[2:3, :] - vir
    own_count = count_ref[r]
    lane = lax.broadcasted_iota(jnp.int32, (size, cols), 1)

    def put(j, pair, gap_rows, gap_cols, row_count, col_count):
        keep = (lane < col_count * nv) & (slot < row_count)
        amp = jnp.where(keep, pair / (gap_rows + gap_cols), 0.0).astype(BF)
        for owner in range(out_ref.shape[0]):
            out_ref[owner, j] = amp

    def head(ref, row):
        block = ref[2 * size:, :].astype(F32)
        return block[3 * row:3 * row + 1] + block[3 * row + 1:3 * row + 2] + block[3 * row + 2:3 * row + 3]

    near = jnp.sum(near_ref[...].astype(F32), axis=0)
    put(0, near[0], own_rows, own_gap, own_count, own_count)
    put(1, near[1], own_rows, gaps_ref[1:2, :], own_count, count_ref[r + 1 - 2 * parity])
    put(
        2, sum_ref[0] + above_ref[0:size, :].astype(F32), head(above_ref, 2) - vir, own_gap,
        at(count_ref, r + 2), own_count,
    )
    put(
        3, sum_ref[1] + below_ref[0:size, :].astype(F32), own_rows, head(below_ref, 0),
        own_count, at(count_ref, r - 2),
    )
    other = swap_ref[...].astype(F32)

    @pl.when(parity == 0)
    def _():
        put(
            4, other + below_ref[size:2 * size, :].astype(F32), own_rows, head(below_ref, 1),
            own_count, at(count_ref, r - 1),
        )

    @pl.when(parity == 1)
    def _():
        put(
            4, other + above_ref[size:2 * size, :].astype(F32), head(above_ref, 3) - vir, own_gap,
            at(count_ref, r + 1), own_count,
        )


def gamma_kernel(
    aux_ref, amps_ref, o_ref, p_ref, n0_ref, n1_ref, m0_ref, m1_ref, x_ref, out_ref,
    p_buf, n_buf, m_buf, result, weights, sems,
):
    rows, cols = o_ref.shape
    half = rows // 2
    _, parity, g = place()
    tiles = sems.shape[1]
    tile = rows // tiles
    starts = [j * tile for j in range(tiles)]
    fetches = {}
    for j, start in enumerate(starts):
        here = pl.ds(start, tile)
        wanted = [(p_ref.at[here, :], p_buf.at[here, :])]
        if start < half:
            wanted.append((m0_ref.at[here, :], m_buf.at[here, :]))
        else:
            low = pl.ds(start - half, tile)
            wanted.append((n1_ref.at[low, :], n_buf.at[low, :]))
        fetches[j] = [pltpu.make_async_copy(src, dst, sems.at[k, j]) for k, (src, dst) in enumerate(wanted)]
        for copy in fetches[j]:
            copy.start()

    def put(j, turned):
        matrix = amps_ref[:, j].reshape(cols, cols)
        weights[j * cols:(j + 1) * cols, :] = matrix.T if turned else matrix

    put(0, False)
    put(1, True)
    put(2, False)
    put(3, True)

    @pl.when(parity == 0)
    def _():
        put(4, True)

    @pl.when(parity == 1)
    def _():
        put(4, False)

    copies = []
    for j, start in enumerate(starts):
        n_ref, m_ref, low = (n0_ref, m_buf, start) if start < half else (n_buf, m1_ref, start - half)
        here, there = pl.ds(start, tile), pl.ds(low, tile)
        for copy in fetches[j]:
            copy.wait()
        blocks = jnp.concatenate(
            [o_ref[here, :], p_buf[here, :], n_ref[there, :], m_ref[there, :], x_ref[here, :]], axis=1
        )
        result[here, :] = keep_rows(mm(blocks, weights[...]), start, aux_ref[g]).astype(result.dtype)
        copy = pltpu.make_async_copy(result.at[here, :], out_ref.at[here, :], sems.at[2, j])
        copy.start()
        copies.append(copy)
    for copy in copies:
        copy.wait()


def cost(flops, size):
    return pl.CostEstimate(flops=flops, bytes_accessed=size, transcendentals=0)


def memory(mebibytes):
    return pltpu.CompilerParams(vmem_limit_bytes=mebibytes << 20)


def per_device(three_index, occ_energy, vir_energy, aux_count, occ_count):
    rows, cols = three_index.shape
    half = rows // 2
    nv = vir_energy.shape[0]
    slabs = lax.axis_size("blk")
    owners = lax.axis_size("grp")
    piece = cols // owners
    dma = pltpu.SemaphoreType.DMA

    def shift(value, steps):
        return lax.ppermute(value, "blk", [(i, (i + steps) % slabs) for i in range(slabs)])

    def swap(value):
        return lax.ppermute(value, "blk", [(i, i ^ 1) for i in range(slabs)])

    def shape(*dims, dtype=BF):
        return jax.ShapeDtypeStruct(dims, dtype)

    own = three_index
    lower, upper = pl.pallas_call(
        halves_kernel,
        in_specs=[ANY],
        out_specs=[VM, VM],
        out_shape=[shape(half, cols), shape(half, cols)],
        scratch_shapes=[dma((2,))],
        cost_estimate=cost(0, 4 * rows * cols),
        compiler_params=memory(8),
        name="halves",
    )(own)
    n0 = shift(lower, -2)
    m1 = shift(upper, 2)
    partner = swap(own)
    partner_energy = swap(occ_energy)

    o0t, o1t, pt, near, gaps, head = pl.pallas_call(
        prep_kernel,
        in_specs=[SM, SM, SM, VM, VM, VM, VM],
        out_specs=[VM] * 6,
        out_shape=[
            shape(cols, half), shape(cols, half), shape(cols, half), shape(owners, 2, piece, cols),
            shape(8 + piece, cols, dtype=F32), shape(16, cols),
        ],
        cost_estimate=cost(4 * rows * cols * cols, 8 * rows * cols),
        compiler_params=memory(16),
        name="prep",
    )(
        aux_count, occ_energy, partner_energy, vir_energy[None, :],
        jnp.broadcast_to(vir_energy[:, None], (nv, cols)), own, partner,
    )
    upper, lower, near = lax.optimization_barrier((upper, lower, near))
    n1 = shift(upper, -2)
    m0 = shift(lower, 2)
    near = lax.all_to_all(near, "grp", 0, 0)
    n0, m1, near = lax.optimization_barrier((n0, m1, near))
    parts = shape(owners, 3, piece, cols)
    partial_sums = pl.pallas_call(
        far_kernel,
        in_specs=[VM] * 5,
        out_specs=VM,
        out_shape=parts,
        cost_estimate=cost(3 * rows * cols * cols, 5 * rows * cols),
        compiler_params=memory(12),
        name="far",
    )(n0, m1, o0t, o1t, pt)
    pieces = lax.all_to_all(partial_sums, "grp", 0, 0)
    message = shape(2 * piece + 16, cols)
    sums, up, down, extra = pl.pallas_call(
        pack_kernel,
        in_specs=[VM, VM],
        out_specs=[VM] * 4,
        out_shape=[shape(2, piece, cols, dtype=F32), message, message, shape(piece, cols)],
        cost_estimate=cost(cols * cols, 4 * cols * cols),
        compiler_params=memory(6),
        name="pack",
    )(pieces, head)
    below = shift(up, 2)
    above = shift(down, -2)
    extra = swap(extra)
    amps = pl.pallas_call(
        lambda *refs: amplitude_kernel(nv, *refs),
        in_specs=[SM] + [VM] * 6,
        out_specs=VM,
        out_shape=shape(owners, 5, piece, cols),
        cost_estimate=cost(cols * cols, 8 * cols * cols),
        compiler_params=memory(6),
        name="amplitude",
    )(occ_count, near, sums, gaps, above, below, extra)
    amps = lax.all_to_all(amps, "grp", 0, 0)
    fifth = swap(jnp.where(
        lax.axis_index("blk") % 2 == 0, jnp.concatenate([n0, n1], axis=0), jnp.concatenate([m0, m1], axis=0)
    ))

    tiles = 4
    return pl.pallas_call(
        gamma_kernel,
        in_specs=[SM, VM, VM, ANY, VM, ANY, ANY, VM, VM],
        out_specs=ANY,
        out_shape=jax.ShapeDtypeStruct((rows, cols), three_index.dtype),
        scratch_shapes=[
            pltpu.VMEM((rows, cols), BF), pltpu.VMEM((half, cols), BF), pltpu.VMEM((half, cols), BF),
            pltpu.VMEM((rows, cols), three_index.dtype), pltpu.VMEM((5 * cols, cols), BF), dma((3, tiles)),
        ],
        cost_estimate=cost(10 * rows * cols * cols, 14 * rows * cols),
        compiler_params=memory(20),
        name="gamma",
    )(aux_count, amps, own, partner, n0, n1, m0, m1, fifth)


def solution(mesh):
    in_specs = (P("grp", "blk"), P("blk"), P(), P(), P())
    out_specs = P("grp", "blk")
    return jax.shard_map(
        per_device, mesh=mesh, in_specs=in_specs, out_specs=out_specs, check_vma=False
    )
```

time: 126 us -> 145 us (1.15)
  waiting for transfers between devices: 49.2 us -> 57.7 us
  local copies, waits for them, and re-layouts: 5.77 us -> 11.6 us
  starting transfers between devices: 53.3 us -> 56.9 us
    all_to_all x0 -> x1, waiting for transfers between devices: none -> 27.4 us  [per_device(): near = lax.all_to_all(near, 'grp', 0, 0)]
    ppermute x6, waiting for transfers between devices: 12.2 us -> 1.01 us  [shift(): lax.ppermute(value, 'blk', [(i, (i + steps) % slabs) for i in range(slabs)])]
    all_to_all x0 -> x1, starting transfers between devices: none -> 9.57 us  [per_device(): near = lax.all_to_all(near, 'grp', 0, 0)]
    unnamed x18 -> x36, local copies, waits for them, and re-layouts: 3.1 us -> 11.5 us
    all_to_all x1, waiting for transfers between devices: 16.5 us -> 8.78 us  [per_device(): pieces = lax.all_to_all(partial_sums, 'grp', 0, 0)]
    all_to_all x1, starting transfers between devices: 9.56 us -> 4.78 us  [per_device(): pieces = lax.all_to_all(partial_sums, 'grp', 0, 0)]
    slice x1 -> x0, local copies, waits for them, and re-layouts: 2.6 us -> none  [per_device(): lower, upper = (own[:half], own[half:])]
    all_to_all x1, starting transfers between devices: 5.8 us -> 4.2 us  [per_device(): amps = lax.all_to_all(amps, 'grp', 0, 0)]
  transfers between devices with their start and end apart: 12 -> 13, of which waited for: 8 -> 5; matrix products, arithmetic and copies ran while one was open for 4% -> 2% of each run, Pallas kernels for 5% -> 5%
where the time goes in v4:
time: 145 us; the launch traced here: 144 us
  waiting for transfers between devices  57.7 us (40%)
  starting transfers between devices  56.9 us (39%)
  Pallas kernels  14.7 us (10%)
  local copies, waits for them, and re-layouts  11.6 us (8%)
  other arithmetic  2.81 us (2%)
    ppermute x6, starting transfers between devices, shift(): lax.ppermute(value, 'blk', [(i, (i + steps) % slabs) for i in range(slabs)])  30.2 us
    all_to_all x1, waiting for transfers between devices, per_device(): near = lax.all_to_all(near, 'grp', 0, 0)  27.4 us
    all_to_all x1, waiting for transfers between devices, per_device(): amps = lax.all_to_all(amps, 'grp', 0, 0)  19.3 us
    unnamed x36, local copies, waits for them, and re-layouts  11.5 us
    all_to_all x1, starting transfers between devices, per_device(): near = lax.all_to_all(near, 'grp', 0, 0)  9.57 us
    all_to_all x1, waiting for transfers between devices, per_device(): pieces = lax.all_to_all(partial_sums, 'grp', 0, 0)  8.78 us
    ppermute x4, starting transfers between devices, swap(): return lax.ppermute(value, 'blk', [(i, i ^ 1) for i in range(slabs)])  8.14 us
    pallas_call x1, Pallas kernels, per_device(): pl.pallas_call(gamma_kernel, in_specs=[SM, VM, VM, ANY, VM, ANY, ANY, VM,...  8.1 us
  transfers between devices with their start and end apart: 13, of which 5 were waited for; matrix products, arithmetic and copies ran while one was open for 2% of the time, Pallas kernels for 5%

profile of v4, /device:TPU:8, one launch (start us, length us, event | category | flops | bytes accessed | tf_op | source)
XLA Modules:
  0.0 143.9 jit_solution(10203008362324324528)
XLA Ops:
  0.0 1.9 %collective-permute-start.3 = (bf16[2944,256]{1,0:T(8,128)(2,1)}, bf16[2944,256]{1,0:T(8,128)(2,1)S(1)}, u32[]{:S(2)}, u32[]{:S(2)}) collective-permute-start(bf16[2944,256]{1,0:T(8,128)(2,1)} %o_ref.1), channel_id=1, source_target_pairs={{0,8},{8,0},{16,24},{24,16},{32,40},{40,32},{48,56},{56,48},{64,72... | collective-permute-start | bytes 4521992 | tf_op jit(solution)/shard_map/ppermute | solution.py:259
  1.9 2.4 %collective-permute-start.2 = (f32[4]{0:T(128)}, f32[4]{0:T(128)S(1)}, u32[]{:S(2)}, u32[]{:S(2)}) collective-permute-start(f32[4]{0:T(128)} %energy_ref.1), channel_id=1, source_target_pairs={{0,8},{8,0},{16,24},{24,16},{32,40},{40,32},{48,56},{56,48},{64,72... | collective-permute-start | bytes 56 | tf_op jit(solution)/shard_map/ppermute | solution.py:259
  4.3 0.0 copy-start
  4.3 1.4 copy-done
  5.7 0.0 copy-start.14
  5.7 0.0 copy-start.1
  5.7 0.0 copy-start.15
  5.7 0.0 copy-start.17
  5.7 1.8 %halves.1 = (bf16[1472,256]{1,0:T(8,128)(2,1)}, bf16[1472,256]{1,0:T(8,128)(2,1)}) custom-call(bf16[2944,256]{1,0:T(8,128)(2,1)S(1)} %copy-done), custom_call_target="tpu_custom_call" | custom-call | bytes 3014656 | tf_op jit(solution)/shard_map/halves/pallas_call | solution.py:265
  7.5 14.5 %collective-permute-start = (bf16[1472,256]{1,0:T(8,128)(2,1)}, bf16[1472,256]{1,0:T(8,128)(2,1)S(1)}, u32[]{:S(2)}, u32[]{:S(2)}) collective-permute-start(bf16[1472,256]{1,0:T(8,128)(2,1)} %get-tuple-element.40), channel_id=1, source_target_pairs={{0,752},{8,760},{16,0},{24,8},{32,16},{40,24},{48,32},{56,40},{64,... | collective-permute-start | bytes 2261000 | tf_op jit(solution)/shard_map/ppermute | solution.py:256
  22.0 1.9 %collective-permute-start.1 = (bf16[1472,256]{1,0:T(8,128)(2,1)}, bf16[1472,256]{1,0:T(8,128)(2,1)S(1)}, u32[]{:S(2)}, u32[]{:S(2)}) collective-permute-start(bf16[1472,256]{1,0:T(8,128)(2,1)} %get-tuple-element.39), channel_id=1, source_target_pairs={{0,16},{8,24},{16,32},{24,40},{32,48},{40,56},{48,64},{56,72},{64,... | collective-permute-start | bytes 2261000 | tf_op jit(solution)/shard_map/ppermute | solution.py:256
  24.0 0.0 collective-permute-done.2.other_ref
  24.0 0.0 collective-permute-done.3.p_ref
  24.0 0.0 copy-start.2
  24.0 0.0 copy-done.14
  24.0 0.1 broadcast_in_dim.10.vir_rows_ref
  24.1 0.0 copy-done.1
  24.1 0.0 copy-done.15
  24.1 0.0 copy-done.17
  24.1 3.0 %prep.1 = (bf16[256,1472]{1,0:T(8,128)(2,1)S(1)}, bf16[256,1472]{1,0:T(8,128)(2,1)S(1)}, bf16[256,1472]{1,0:T(8,128)(2,1)S(1)}, bf16[8,2,32,256]{3,2,1,0:T(8,128...) custom-call(s32[8]{0:T(128)S(1)} %copy-done.15, f32[4]{0:T(128)S(1)} %copy-done.17, ...), custom_call_target="tpu_custom_call" | custom-call | flops 771751936 | bytes 6029312 | tf_op jit(solution)/shard_map/prep/pallas_call | solution.py:280
  27.1 0.0 copy-done.2
  27.1 0.0 copy-start.8
  27.1 0.9 copy-done.8
  27.9 0.0 copy-start.10
  27.9 0.9 copy-done.10
  28.8 0.0 copy-start.12
  28.8 0.9 copy-done.12
  29.8 6.0 %collective-permute-start.7 = (bf16[1472,256]{1,0:T(8,128)(2,1)}, bf16[1472,256]{1,0:T(8,128)(2,1)}, u32[]{:S(2)}, u32[]{:S(2)}) collective-permute-start(bf16[1472,256]{1,0:T(8,128)(2,1)} %get-tuple-element.39), channel_id=1, source_target_pairs={{0,752},{8,760},{16,0},{24,8},{32,16},{40,24},{48,32},{56,40},{64,... | collective-permute-start | bytes 2261000 | tf_op jit(solution)/shard_map/ppermute | solution.py:256
  35.8 1.9 %collective-permute-start.8 = (bf16[1472,256]{1,0:T(8,128)(2,1)}, bf16[1472,256]{1,0:T(8,128)(2,1)}, u32[]{:S(2)}, u32[]{:S(2)}) collective-permute-start(bf16[1472,256]{1,0:T(8,128)(2,1)} %get-tuple-element.40), channel_id=1, source_target_pairs={{0,16},{8,24},{16,32},{24,40},{32,48},{40,56},{48,64},{56,72},{64,... | collective-permute-start | bytes 2261000 | tf_op jit(solution)/shard_map/ppermute | solution.py:256
  37.7 9.6 %all-to-all-start = ((bf16[8,2,32,256]{3,2,1,0:T(8,128)(2,1)}), bf16[8,2,32,256]{3,2,1,0:T(8,128)(2,1)S(1)}, u32[]{:S(2)}, u32[]{:S(2)}) async-start(bf16[8,2,32,256]{3,2,1,0:T(8,128)(2,1)} %get-tuple-element.26), calls=%async_computation | async-start | bytes 524288 | tf_op jit(solution)/shard_map/all_to_all | solution.py:298
  47.3 0.0 collective-permute-done.n_ref.n0_ref
  47.3 0.0 collective-permute-done.1.m_ref.m1_ref
  47.3 27.4 %all-to-all-done.refs_1_ = bf16[8,2,32,256]{3,2,1,0:T(8,128)(2,1)S(1)} async-done(((bf16[8,2,32,256]{3,2,1,0:T(8,128)(2,1)}), bf16[8,2,32,256]{3,2,1,0:T(8,128)(2,1)S(1)}, u32[]{:S(2)}, u32[]{:S(2)}) %all-to-all-start) | async-done | bytes 262176 | tf_op jit(solution)/shard_map/all_to_all | solution.py:298
  74.7 0.0 copy-start.6
  74.7 1.2 copy-done.9
  76.0 1.1 copy-done.11
  77.1 1.1 copy-done.13
  78.2 1.1 far.1
  79.3 0.0 copy-done.6
  79.3 0.0 copy-start.5
  79.3 0.8 copy-done.5
  80.1 4.8 %all-to-all-start.1 = ((bf16[8,3,32,256]{3,2,1,0:T(8,128)(2,1)}), bf16[8,3,32,256]{3,2,1,0:T(8,128)(2,1)S(1)}, u32[]{:S(2)}, u32[]{:S(2)}) async-start(bf16[8,3,32,256]{3,2,1,0:T(8,128)(2,1)} %copy-done.5), calls=%async_computation.1 | async-start | bytes 786432 | tf_op jit(solution)/shard_map/all_to_all | solution.py:310
  84.9 0.0 collective-permute-done.7.n1_ref
  84.9 0.0 collective-permute-done.8.m0_ref
  84.9 2.8 %maximum_select_fusion = bf16[2944,256]{1,0:T(8,128)(2,1)} fusion(bf16[1472,256]{1,0:T(8,128)(2,1)} %collective-permute-done.7.n1_ref, bf16[1472,256]{1,0:T(8,128)(2,1)S(1)} %collective-permute-done.n_ref.n0_ref, bf16[1472,256]{1,0:T(8,128)(2,1)S(1)} %collective-permute-done.1.m_ref.m1_ref, bf16[1472,256]{1,0:T(8,128)(2,1)} %collective-permute-done.8.m0_ref, ...), kind=kLoop, calls=%fused_computation | loop fusion | flops 6782976 | bytes 4521985 | tf_op jit(solution)/shard_map/jit(_where)/select_n | solution.py:334
  87.7 1.9 %collective-permute-start.9 = (bf16[2944,256]{1,0:T(8,128)(2,1)}, bf16[2944,256]{1,0:T(8,128)(2,1)}, u32[]{:S(2)}, u32[]{:S(2)}) collective-permute-start(bf16[2944,256]{1,0:T(8,128)(2,1)} %maximum_select_fusion), channel_id=1, source_target_pairs={{0,8},{8,0},{16,24},{24,16},{32,40},{40,32},{48,56},{56,48},{64,72... | collective-permute-start | bytes 4521992 | tf_op jit(solution)/shard_map/ppermute | solution.py:259
  89.6 8.8 %all-to-all-done.1.parts_ref = bf16[8,3,32,256]{3,2,1,0:T(8,128)(2,1)S(1)} async-done(((bf16[8,3,32,256]{3,2,1,0:T(8,128)(2,1)}), bf16[8,3,32,256]{3,2,1,0:T(8,128)(2,1)S(1)}, u32[]{:S(2)}, u32[]{:S(2)}) %all-to-all-start.1) | async-done | bytes 393248 | tf_op jit(solution)/shard_map/all_to_all | solution.py:310
  98.4 0.1 pack.1
  98.5 1.9 %collective-permute-start.4 = (bf16[80,256]{1,0:T(8,128)(2,1)S(1)}, bf16[80,256]{1,0:T(8,128)(2,1)S(1)}, u32[]{:S(2)}, u32[]{:S(2)}) collective-permute-start(bf16[80,256]{1,0:T(8,128)(2,1)S(1)} %get-tuple-element.36), channel_id=1, source_target_pairs={{0,752},{8,760},{16,0},{24,8},{32,16},{40,24},{48,32},{56,40},{64,... | collective-permute-start | bytes 122888 | tf_op jit(solution)/shard_map/ppermute | solution.py:256
  100.4 3.9 %collective-permute-start.5 = (bf16[80,256]{1,0:T(8,128)(2,1)S(1)}, bf16[80,256]{1,0:T(8,128)(2,1)S(1)}, u32[]{:S(2)}, u32[]{:S(2)}) collective-permute-start(bf16[80,256]{1,0:T(8,128)(2,1)S(1)} %get-tuple-element.37), channel_id=1, source_target_pairs={{0,16},{8,24},{16,32},{24,40},{32,48},{40,56},{48,64},{56,72},{64,... | collective-permute-start | bytes 122888 | tf_op jit(solution)/shard_map/ppermute | solution.py:256
  104.3 1.9 %collective-permute-start.6 = (bf16[32,256]{1,0:T(8,128)(2,1)S(1)}, bf16[32,256]{1,0:T(8,128)(2,1)S(1)}, u32[]{:S(2)}, u32[]{:S(2)}) collective-permute-start(bf16[32,256]{1,0:T(8,128)(2,1)S(1)} %get-tuple-element.38), channel_id=1, source_target_pairs={{0,8},{8,0},{16,24},{24,16},{32,40},{40,32},{48,56},{56,48},{64,72... | collective-permute-start | bytes 49160 | tf_op jit(solution)/shard_map/ppermute | solution.py:259
  106.3 1.1 collective-permute-done.6.refs_6_
  107.4 0.0 collective-permute-done.4.refs_4_
  107.4 1.0 collective-permute-done.5.refs_5_
  108.4 0.0 copy-done.16
  108.4 0.9 copy-done.7
  109.4 0.6 amplitude.1
  110.0 0.0 copy-start.4
  110.0 0.8 copy-done.4
  110.9 4.2 %all-to-all-start.2 = ((bf16[8,5,32,256]{3,2,1,0:T(8,128)(2,1)}), bf16[8,5,32,256]{3,2,1,0:T(8,128)(2,1)}, u32[]{:S(2)}, u32[]{:S(2)}) async-start(bf16[8,5,32,256]{3,2,1,0:T(8,128)(2,1)} %copy-done.4), calls=%async_computation.2 | async-start | bytes 1310720 | tf_op jit(solution)/shard_map/all_to_all | solution.py:333
  115.1 0.0 collective-permute-done.9.x_ref
  115.1 19.3 %all-to-all-done.2.amps_ref = bf16[8,5,32,256]{3,2,1,0:T(8,128)(2,1)} async-done(((bf16[8,5,32,256]{3,2,1,0:T(8,128)(2,1)}), bf16[8,5,32,256]{3,2,1,0:T(8,128)(2,1)}, u32[]{:S(2)}, u32[]{:S(2)}) %all-to-all-start.2) | async-done | bytes 655392 | tf_op jit(solution)/shard_map/all_to_all | solution.py:333
  134.4 1.4 copy-done.3
  135.8 8.1 %gamma.1 = bf16[2944,256]{1,0:T(8,128)(2,1)} custom-call(s32[8]{0:T(128)S(1)} %copy-done.15, bf16[8,5,32,256]{3,2,1,0:T(8,128)(2,1)} %all-to-all-done.2.amps_ref, bf16[2944,256]{1,0:T(8,128)(2,1)S(1)} %copy-done.1, bf16[2944,256]{1,0:T(8,128)(2,1)S(1)} %copy-done.3, bf16[1472,256]{1,0:T(8,128)(2,1)S(1)} %collective-permute-done.n_ref.n0_ref, ...), custom_call_target="tpu_custom_call" | custom-call | flops 1929379840 | bytes 10551296 | tf_op jit(solution)/shard_map/gamma/pallas_call | solution.py:339
  (6 shorter events, 0.0 us)
Async XLA Ops:
  0.0 24.0 %collective-permute-start.3 = (bf16[2944,256]{1,0:T(8,128)(2,1)}, bf16[2944,256]{1,0:T(8,128)(2,1)S(1)}, u32[]{:S(2)}, u32[]{:S(2)}) collective-permute-start(bf16[2944,256]{1,0:T(8,128)(2,1)} %o_ref.1), channel_id=1, source_target_pairs={{0,8},{8,0},{16,24},{24,16},{32,40},{40,32},{48,56},{56,48},{64,72... | collective-permute-start | bytes 4521992 | tf_op jit(solution)/shard_map/ppermute | solution.py:259
  1.9 22.0 %collective-permute-start.2 = (f32[4]{0:T(128)}, f32[4]{0:T(128)S(1)}, u32[]{:S(2)}, u32[]{:S(2)}) collective-permute-start(f32[4]{0:T(128)} %energy_ref.1), channel_id=1, source_target_pairs={{0,8},{8,0},{16,24},{24,16},{32,40},{40,32},{48,56},{56,48},{64,72... | collective-permute-start | bytes 56 | tf_op jit(solution)/shard_map/ppermute | solution.py:259
  4.3 1.4 copy-start
  5.7 18.3 %copy-start.14 = (f32[64]{0:T(128)S(1)}, f32[64]{0:T(128)}, u32[]{:S(2)}) copy-start(f32[64]{0:T(128)} %param.7) | copy-start | bytes 772
  5.7 18.4 %copy-start.1 = (bf16[2944,256]{1,0:T(8,128)(2,1)S(1)}, bf16[2944,256]{1,0:T(8,128)(2,1)}, u32[]{:S(2)}) copy-start(bf16[2944,256]{1,0:T(8,128)(2,1)} %o_ref.1) | copy-start | bytes 4521988
  5.7 18.4 %copy-start.15 = (s32[8]{0:T(128)S(1)}, s32[8]{0:T(128)}, u32[]{:S(2)}) copy-start(s32[8]{0:T(128)} %aux_ref.3) | copy-start | bytes 100
  5.7 18.4 %copy-start.17 = (f32[4]{0:T(128)S(1)}, f32[4]{0:T(128)}, u32[]{:S(2)}) copy-start(f32[4]{0:T(128)} %energy_ref.1) | copy-start | bytes 52
  7.5 39.8 %collective-permute-start = (bf16[1472,256]{1,0:T(8,128)(2,1)}, bf16[1472,256]{1,0:T(8,128)(2,1)S(1)}, u32[]{:S(2)}, u32[]{:S(2)}) collective-permute-start(bf16[1472,256]{1,0:T(8,128)(2,1)} %get-tuple-element.40), channel_id=1, source_target_pairs={{0,752},{8,760},{16,0},{24,8},{32,16},{40,24},{48,32},{56,40},{64,... | collective-permute-start | bytes 2261000 | tf_op jit(solution)/shard_map/ppermute | solution.py:256
  22.0 25.3 %collective-permute-start.1 = (bf16[1472,256]{1,0:T(8,128)(2,1)}, bf16[1472,256]{1,0:T(8,128)(2,1)S(1)}, u32[]{:S(2)}, u32[]{:S(2)}) collective-permute-start(bf16[1472,256]{1,0:T(8,128)(2,1)} %get-tuple-element.39), channel_id=1, source_target_pairs={{0,16},{8,24},{16,32},{24,40},{32,48},{40,56},{48,64},{56,72},{64,... | collective-permute-start | bytes 2261000 | tf_op jit(solution)/shard_map/ppermute | solution.py:256
  24.0 3.1 %copy-start.2 = (bf16[2944,256]{1,0:T(8,128)(2,1)}, bf16[2944,256]{1,0:T(8,128)(2,1)S(1)}, u32[]{:S(2)}) copy-start(bf16[2944,256]{1,0:T(8,128)(2,1)S(1)} %collective-permute-done.3.p_ref) | copy-start | bytes 4521988
  27.1 0.9 copy-start.8
  27.9 0.9 copy-start.10
  28.8 0.9 copy-start.12
  29.8 55.1 %collective-permute-start.7 = (bf16[1472,256]{1,0:T(8,128)(2,1)}, bf16[1472,256]{1,0:T(8,128)(2,1)}, u32[]{:S(2)}, u32[]{:S(2)}) collective-permute-start(bf16[1472,256]{1,0:T(8,128)(2,1)} %get-tuple-element.39), channel_id=1, source_target_pairs={{0,752},{8,760},{16,0},{24,8},{32,16},{40,24},{48,32},{56,40},{64,... | collective-permute-start | bytes 2261000 | tf_op jit(solution)/shard_map/ppermute | solution.py:256
  35.8 49.1 %collective-permute-start.8 = (bf16[1472,256]{1,0:T(8,128)(2,1)}, bf16[1472,256]{1,0:T(8,128)(2,1)}, u32[]{:S(2)}, u32[]{:S(2)}) collective-permute-start(bf16[1472,256]{1,0:T(8,128)(2,1)} %get-tuple-element.40), channel_id=1, source_target_pairs={{0,16},{8,24},{16,32},{24,40},{32,48},{40,56},{48,64},{56,72},{64,... | collective-permute-start | bytes 2261000 | tf_op jit(solution)/shard_map/ppermute | solution.py:256
  37.7 37.0 %all-to-all-start = ((bf16[8,2,32,256]{3,2,1,0:T(8,128)(2,1)}), bf16[8,2,32,256]{3,2,1,0:T(8,128)(2,1)S(1)}, u32[]{:S(2)}, u32[]{:S(2)}) async-start(bf16[8,2,32,256]{3,2,1,0:T(8,128)(2,1)} %get-tuple-element.26), calls=%async_computation | async-start | bytes 524288 | tf_op jit(solution)/shard_map/all_to_all | solution.py:298
  74.7 4.6 %copy-start.6 = (bf16[8,2,32,256]{3,2,1,0:T(8,128)(2,1)}, bf16[8,2,32,256]{3,2,1,0:T(8,128)(2,1)S(1)}, u32[]{:S(2)}) copy-start(bf16[8,2,32,256]{3,2,1,0:T(8,128)(2,1)S(1)} %all-to-all-done.refs_1_) | copy-start | bytes 786436
  74.7 1.2 copy-start.9
  76.0 1.1 copy-start.11
  77.1 1.1 copy-start.13
  79.3 0.8 copy-start.5
  80.1 18.3 %all-to-all-start.1 = ((bf16[8,3,32,256]{3,2,1,0:T(8,128)(2,1)}), bf16[8,3,32,256]{3,2,1,0:T(8,128)(2,1)S(1)}, u32[]{:S(2)}, u32[]{:S(2)}) async-start(bf16[8,3,32,256]{3,2,1,0:T(8,128)(2,1)} %copy-done.5), calls=%async_computation.1 | async-start | bytes 786432 | tf_op jit(solution)/shard_map/all_to_all | solution.py:310
  84.9 23.5 %copy-start.16 = (s32[96]{0:T(128)S(1)}, s32[96]{0:T(128)}, u32[]{:S(2)}) copy-start(s32[96]{0:T(128)} %refs_0_.1) | copy-start | bytes 1156
  87.7 27.4 %collective-permute-start.9 = (bf16[2944,256]{1,0:T(8,128)(2,1)}, bf16[2944,256]{1,0:T(8,128)(2,1)}, u32[]{:S(2)}, u32[]{:S(2)}) collective-permute-start(bf16[2944,256]{1,0:T(8,128)(2,1)} %maximum_select_fusion), channel_id=1, source_target_pairs={{0,8},{8,0},{16,24},{24,16},{32,40},{40,32},{48,56},{56,48},{64,72... | collective-permute-start | bytes 4521992 | tf_op jit(solution)/shard_map/ppermute | solution.py:259
  98.5 8.9 %collective-permute-start.4 = (bf16[80,256]{1,0:T(8,128)(2,1)S(1)}, bf16[80,256]{1,0:T(8,128)(2,1)S(1)}, u32[]{:S(2)}, u32[]{:S(2)}) collective-permute-start(bf16[80,256]{1,0:T(8,128)(2,1)S(1)} %get-tuple-element.36), channel_id=1, source_target_pairs={{0,752},{8,760},{16,0},{24,8},{32,16},{40,24},{48,32},{56,40},{64,... | collective-permute-start | bytes 122888 | tf_op jit(solution)/shard_map/ppermute | solution.py:256
  100.4 8.0 %collective-permute-start.5 = (bf16[80,256]{1,0:T(8,128)(2,1)S(1)}, bf16[80,256]{1,0:T(8,128)(2,1)S(1)}, u32[]{:S(2)}, u32[]{:S(2)}) collective-permute-start(bf16[80,256]{1,0:T(8,128)(2,1)S(1)} %get-tuple-element.37), channel_id=1, source_target_pairs={{0,16},{8,24},{16,32},{24,40},{32,48},{40,56},{48,64},{56,72},{64,... | collective-permute-start | bytes 122888 | tf_op jit(solution)/shard_map/ppermute | solution.py:256
  104.3 3.1 %collective-permute-start.6 = (bf16[32,256]{1,0:T(8,128)(2,1)S(1)}, bf16[32,256]{1,0:T(8,128)(2,1)S(1)}, u32[]{:S(2)}, u32[]{:S(2)}) collective-permute-start(bf16[32,256]{1,0:T(8,128)(2,1)S(1)} %get-tuple-element.38), channel_id=1, source_target_pairs={{0,8},{8,0},{16,24},{24,16},{32,40},{40,32},{48,56},{56,48},{64,72... | collective-permute-start | bytes 49160 | tf_op jit(solution)/shard_map/ppermute | solution.py:259
  108.4 1.0 copy-start.7
  110.0 0.9 copy-start.4
  110.9 23.5 %all-to-all-start.2 = ((bf16[8,5,32,256]{3,2,1,0:T(8,128)(2,1)}), bf16[8,5,32,256]{3,2,1,0:T(8,128)(2,1)}, u32[]{:S(2)}, u32[]{:S(2)}) async-start(bf16[8,5,32,256]{3,2,1,0:T(8,128)(2,1)} %copy-done.4), calls=%async_computation.2 | async-start | bytes 1310720 | tf_op jit(solution)/shard_map/all_to_all | solution.py:333
  134.4 1.4 copy-start.3

commit v5 on v4

v5 whole, which is shorter than its diff:
```python
import jax
import jax.numpy as jnp
from jax import lax
from jax.experimental import pallas as pl
from jax.experimental.pallas import tpu as pltpu
from jax.sharding import PartitionSpec as P


BF = jnp.bfloat16
F32 = jnp.float32
VM = pl.BlockSpec(memory_space=pltpu.VMEM)
SM = pl.BlockSpec(memory_space=pltpu.SMEM)
ANY = pl.BlockSpec(memory_space=pl.ANY)


def mm(a, b):
    return jnp.dot(a, b, preferred_element_type=F32)


def keep_rows(block, start, count):
    row = lax.broadcasted_iota(jnp.int32, block.shape, 0) + start
    return jnp.where(row < count, block, jnp.zeros((), block.dtype))


def place():
    r = lax.axis_index("blk")
    return r, lax.rem(r, 2), lax.axis_index("grp")


def at(count_ref, index):
    slabs = count_ref.shape[0]
    return count_ref[lax.rem(index + slabs, slabs)]


def three_terms(value):
    hi = value.astype(BF)
    rest = value - hi.astype(F32)
    mid = rest.astype(BF)
    low = (rest - mid.astype(F32)).astype(BF)
    return [hi.astype(F32), mid.astype(F32), low.astype(F32)]


def prep_kernel(
    aux_ref, energy_ref, other_ref, vir_ref, vir_rows_ref, own_ref, p_ref,
    o0t_ref, o1t_ref, pt_ref, near_ref, gaps_ref, head_ref,
):
    _, parity, g = place()
    rows, cols = own_ref.shape
    half = rows // 2
    owners = near_ref.shape[0]
    piece = cols // owners
    part = piece // 2
    nv = vir_ref.shape[1]
    count = aux_ref[g]
    o0t_ref[...] = keep_rows(own_ref[:half, :], 0, count).T
    o1t_ref[...] = keep_rows(own_ref[half:, :], half, count).T

    @pl.when(parity == 0)
    def _():
        pt_ref[...] = keep_rows(p_ref[:half, :], 0, count).T

    @pl.when(parity == 1)
    def _():
        pt_ref[...] = keep_rows(p_ref[half:, :], half, count).T

    def put(rows_of, pair):
        near_ref[:, rows_of] = pair.reshape(owners, pair.shape[0] // owners, cols).astype(BF)

    put(slice(0, piece), mm(o0t_ref[...], own_ref[:half, :]) + mm(o1t_ref[...], own_ref[half:, :]))
    middle = cols // 2

    @pl.when(parity == 0)
    def _():
        put(
            slice(piece, piece + part),
            mm(o0t_ref[:middle, :], p_ref[:half, :]) + mm(o1t_ref[:middle, :], p_ref[half:, :]),
        )

    @pl.when(parity == 1)
    def _():
        low = keep_rows(p_ref[:half, middle:], 0, count).T
        put(
            slice(piece, piece + part),
            mm(low, own_ref[:half, :]) + mm(pt_ref[middle:, :], own_ref[half:, :]),
        )

    slots = cols // nv
    slot = (g * piece) // nv
    lane = lax.broadcasted_iota(jnp.int32, (1, cols), 1)
    vir = jnp.concatenate([vir_ref[...]] * slots, axis=1)
    rows_out = []
    for ref in (energy_ref, other_ref):
        level = jnp.zeros((1, cols), F32)
        for k in range(slots):
            level = jnp.where(lane // nv == k, ref[k], level)
        rows_out.append(level - vir)
    for ref in (energy_ref, other_ref):
        rows_out.append(jnp.broadcast_to(ref[slot], (1, cols)))
    terms = []
    for row in rows_out:
        terms += three_terms(row)
    zero = jnp.zeros((4, cols), F32)
    head_ref[...] = jnp.concatenate(terms + [zero], axis=0).astype(BF)
    for upper_half in range(2):
        k = (g * part) // nv + upper_half * (slots // 2)
        level = jnp.where(parity == 0, energy_ref[k], other_ref[k])
        rows_out.append(jnp.broadcast_to(level, (1, cols)))
    gaps_ref[0:8, :] = jnp.concatenate(rows_out + [zero[:2]], axis=0)
    start = pl.multiple_of(lax.rem(g * piece, nv), piece)
    gaps_ref[8:8 + piece, :] = vir_rows_ref[pl.ds(start, piece), :]
    start = pl.multiple_of(lax.rem(g * part, nv), part)
    gaps_ref[8 + piece:, :] = vir_rows_ref[pl.ds(start, part), :]


def far_kernel(n_ref, m_ref, o0t_ref, o1t_ref, pt_ref, near_ref, out_ref):
    _, parity, _ = place()
    owners, _, cols = out_ref.shape
    piece = cols // owners
    near = near_ref.shape[1]

    def put(j, pair):
        out_ref[:, near + j * piece:near + (j + 1) * piece] = pair.reshape(owners, piece, cols).astype(BF)

    out_ref[:, 0:near] = near_ref[...]
    put(0, mm(o0t_ref[...], n_ref[...]).T)
    put(1, mm(o1t_ref[...], m_ref[...]))

    @pl.when(parity == 0)
    def _():
        put(2, mm(pt_ref[...], n_ref[...]).T)

    @pl.when(parity == 1)
    def _():
        put(2, mm(pt_ref[...], m_ref[...]))


def pack_kernel(parts_ref, head_ref, sum_ref, up_ref, down_ref, swap_ref):
    total = jnp.sum(parts_ref[...].astype(F32), axis=0)
    size = parts_ref.shape[2] // parts_ref.shape[0]
    part = size // 2
    near = size + part
    sum_ref[0:size, :] = total[0:size]
    sum_ref[size:3 * size, :] = total[near:near + 2 * size]
    sum_ref[3 * size:, :] = total[size:near]
    extra = total[near + 2 * size:].astype(BF)
    swap_ref[0:size, :] = extra
    swap_ref[size:, :] = total[size:near].astype(BF)
    for j, ref in ((0, up_ref), (1, down_ref)):
        ref[0:size, :] = total[near + j * size:near + (j + 1) * size].astype(BF)
        ref[size:2 * size, :] = extra
        ref[2 * size:, :] = head_ref[...]


def amplitude_kernel(nv, count_ref, sum_ref, gaps_ref, above_ref, below_ref, swap_ref, out_ref):
    r, parity, g = place()
    owners, _, size, cols = out_ref.shape
    part = size // 2
    slot = (g * size) // nv
    vir = gaps_ref[8:8 + size, :]
    own_gap = gaps_ref[0:1, :]
    own_rows = gaps_ref[2:3, :] - vir
    own_count = count_ref[r]
    lane = lax.broadcasted_iota(jnp.int32, (size, cols), 1)

    def put(j, pair, gap_rows, gap_cols, row_count, col_count):
        keep = (lane < col_count * nv) & (slot < row_count)
        amp = jnp.where(keep, pair / (gap_rows + gap_cols), 0.0).astype(BF)
        for owner in range(out_ref.shape[0]):
            out_ref[owner, j] = amp

    def head(ref, row):
        block = ref[2 * size:, :].astype(F32)
        return block[3 * row:3 * row + 1] + block[3 * row + 1:3 * row + 2] + block[3 * row + 2:3 * row + 3]

    put(0, sum_ref[0:size, :], own_rows, own_gap, own_count, own_count)
    even_count, odd_count = count_ref[r - parity], count_ref[r - parity + 1]
    odd_gap = jnp.where(parity == 0, gaps_ref[1:2, :], own_gap)
    mine = sum_ref[3 * size:, :]
    theirs = swap_ref[size:, :].astype(F32)
    for upper_half in range(2):
        k = (g * part) // nv + upper_half * (cols // nv // 2)
        pair = jnp.where(parity == upper_half, mine, theirs)
        gap_rows = gaps_ref[4 + upper_half:5 + upper_half, :] - gaps_ref[8 + size:, :]
        keep = (lane[:part] < odd_count * nv) & (k < even_count)
        amp = jnp.where(keep, pair / (gap_rows + odd_gap), 0.0).astype(BF)
        for owner in range(owners):
            out_ref[owner, 1, upper_half * part:(upper_half + 1) * part] = amp

    put(
        2, sum_ref[size:2 * size, :] + above_ref[0:size, :].astype(F32), head(above_ref, 2) - vir, own_gap,
        at(count_ref, r + 2), own_count,
    )
    put(
        3, sum_ref[2 * size:3 * size, :] + below_ref[0:size, :].astype(F32), own_rows, head(below_ref, 0),
        own_count, at(count_ref, r - 2),
    )
    other = swap_ref[0:size, :].astype(F32)

    @pl.when(parity == 0)
    def _():
        put(
            4, other + below_ref[size:2 * size, :].astype(F32), own_rows, head(below_ref, 1),
            own_count, at(count_ref, r - 1),
        )

    @pl.when(parity == 1)
    def _():
        put(
            4, other + above_ref[size:2 * size, :].astype(F32), head(above_ref, 3) - vir, own_gap,
            at(count_ref, r + 1), own_count,
        )


def gamma_kernel(
    aux_ref, amps_ref, o_ref, p_ref, n0_ref, n1_ref, m0_ref, m1_ref, x_ref, out_ref, result, weights, sems
):
    rows, cols = o_ref.shape
    half = rows // 2
    _, parity, g = place()

    def put(j, matrix):
        weights[j * cols:(j + 1) * cols, :] = matrix

    def whole(j):
        return amps_ref[:, j].reshape(cols, cols)

    part = amps_ref.shape[2] // 2
    both = jnp.concatenate(
        [amps_ref[:, 1, k * part:(k + 1) * part].reshape(cols // 2, cols) for k in range(2)], axis=0
    )
    put(0, whole(0))
    put(2, whole(2))
    put(3, whole(3).T)

    @pl.when(parity == 0)
    def _():
        put(1, both.T)
        put(4, whole(4).T)

    @pl.when(parity == 1)
    def _():
        put(1, both)
        put(4, whole(4))

    tile = rows // sems.shape[0]
    copies = []
    for j in range(sems.shape[0]):
        start = j * tile
        n_ref, m_ref, low = (n0_ref, m0_ref, start) if start < half else (n1_ref, m1_ref, start - half)
        here, there = pl.ds(start, tile), pl.ds(low, tile)
        blocks = jnp.concatenate(
            [o_ref[here, :], p_ref[here, :], n_ref[there, :], m_ref[there, :], x_ref[here, :]], axis=1
        )
        result[here, :] = keep_rows(mm(blocks, weights[...]), start, aux_ref[g]).astype(result.dtype)
        copy = pltpu.make_async_copy(result.at[here, :], out_ref.at[here, :], sems.at[j])
        copy.start()
        copies.append(copy)
    for copy in copies:
        copy.wait()


def cost(flops, size):
    return pl.CostEstimate(flops=flops, bytes_accessed=size, transcendentals=0)


def memory(mebibytes):
    return pltpu.CompilerParams(vmem_limit_bytes=mebibytes << 20)


def per_device(three_index, occ_energy, vir_energy, aux_count, occ_count):
    rows, cols = three_index.shape
    half = rows // 2
    nv = vir_energy.shape[0]
    slabs = lax.axis_size("blk")
    owners = lax.axis_size("grp")
    piece = cols // owners
    part = piece // 2

    def shift(value, steps):
        return lax.ppermute(value, "blk", [(i, (i + steps) % slabs) for i in range(slabs)])

    def swap(value):
        return lax.ppermute(value, "blk", [(i, i ^ 1) for i in range(slabs)])

    def shape(*dims, dtype=BF):
        return jax.ShapeDtypeStruct(dims, dtype)

    own = three_index
    lower, upper = own[:half], own[half:]
    n0 = shift(lower, -2)
    m1 = shift(upper, 2)
    partner = swap(own)
    partner_energy = swap(occ_energy)

    o0t, o1t, pt, near, gaps, head = pl.pallas_call(
        prep_kernel,
        in_specs=[SM, SM, SM, VM, VM, VM, VM],
        out_specs=[VM] * 6,
        out_shape=[
            shape(cols, half), shape(cols, half), shape(cols, half), shape(owners, piece + part, cols),
            shape(8 + piece + part, cols, dtype=F32), shape(16, cols),
        ],
        cost_estimate=cost(4 * rows * cols * cols, 8 * rows * cols),
        compiler_params=memory(16),
        name="prep",
    )(
        aux_count, occ_energy, partner_energy, vir_energy[None, :],
        jnp.broadcast_to(vir_energy[:, None], (nv, cols)), own, partner,
    )
    upper, lower, near = lax.optimization_barrier((upper, lower, near))
    n1 = shift(upper, -2)
    m0 = shift(lower, 2)
    parts = shape(owners, 4 * piece + part, cols)
    partial_sums = pl.pallas_call(
        far_kernel,
        in_specs=[VM] * 6,
        out_specs=VM,
        out_shape=parts,
        cost_estimate=cost(3 * rows * cols * cols, 5 * rows * cols),
        compiler_params=memory(12),
        name="far",
    )(n0, m1, o0t, o1t, pt, near)
    pieces = lax.all_to_all(partial_sums, "grp", 0, 0)
    message = shape(2 * piece + 16, cols)
    sums, up, down, extra = pl.pallas_call(
        pack_kernel,
        in_specs=[VM, VM],
        out_specs=[VM] * 4,
        out_shape=[shape(3 * piece + part, cols, dtype=F32), message, message, shape(piece + part, cols)],
        cost_estimate=cost(cols * cols, 4 * cols * cols),
        compiler_params=memory(6),
        name="pack",
    )(pieces, head)
    below = shift(up, 2)
    above = shift(down, -2)
    extra = swap(extra)
    amps = pl.pallas_call(
        lambda *refs: amplitude_kernel(nv, *refs),
        in_specs=[SM] + [VM] * 5,
        out_specs=VM,
        out_shape=shape(owners, 5, piece, cols),
        cost_estimate=cost(cols * cols, 8 * cols * cols),
        compiler_params=memory(6),
        name="amplitude",
    )(occ_count, sums, gaps, above, below, extra)
    amps = lax.all_to_all(amps, "grp", 0, 0)
    fifth = swap(jnp.where(
        lax.axis_index("blk") % 2 == 0, jnp.concatenate([n0, n1], axis=0), jnp.concatenate([m0, m1], axis=0)
    ))

    tiles = 8
    return pl.pallas_call(
        gamma_kernel,
        in_specs=[SM] + [VM] * 8,
        out_specs=ANY,
        out_shape=jax.ShapeDtypeStruct((rows, cols), three_index.dtype),
        scratch_shapes=[
            pltpu.VMEM((rows, cols), three_index.dtype), pltpu.VMEM((5 * cols, cols), BF),
            pltpu.SemaphoreType.DMA((tiles,)),
        ],
        cost_estimate=cost(10 * rows * cols * cols, 14 * rows * cols),
        compiler_params=memory(20),
        name="gamma",
    )(aux_count, amps, own, partner, n0, n1, m0, m1, fifth)


def solution(mesh):
    in_specs = (P("grp", "blk"), P("blk"), P(), P(), P())
    out_specs = P("grp", "blk")
    return jax.shard_map(
        per_device, mesh=mesh, in_specs=in_specs, out_specs=out_specs, check_vma=False
    )
```

time: 145 us -> 118 us (0.81)
  the two profiles are of different devices: /device:TPU:8 before, /device:TPU:56 now
where the time goes in v5:
time: 118 us
  starting transfers between devices  56.2 us (48%)
  blocking collectives  24.2 us (21%)
  waiting for transfers between devices  20.4 us (17%)
  Pallas kernels  10.3 us (9%)
  local copies, waits for them, and re-layouts  3.53 us (3%)
  other arithmetic  2.81 us (2%)
    ppermute x6, starting transfers between devices, shift(): lax.ppermute(value, 'blk', [(i, (i + steps) % slabs) for i in range(slabs)])  38.5 us
    all_to_all x1, blocking collectives, per_device(): amps = lax.all_to_all(amps, 'grp', 0, 0)  24.2 us
    ppermute x6, waiting for transfers between devices, shift(): lax.ppermute(value, 'blk', [(i, (i + steps) % slabs) for i in range(slabs)])  13.3 us
    all_to_all x1, starting transfers between devices, per_device(): pieces = lax.all_to_all(partial_sums, 'grp', 0, 0)  9.67 us
    ppermute x4, starting transfers between devices, swap(): return lax.ppermute(value, 'blk', [(i, i ^ 1) for i in range(slabs)])  8.01 us
    all_to_all x1, waiting for transfers between devices, per_device(): pieces = lax.all_to_all(partial_sums, 'grp', 0, 0)  5.05 us
    pallas_call x1, Pallas kernels, per_device(): pl.pallas_call(gamma_kernel, in_specs=[SM] + [VM] * 8, out_specs=ANY, out...  5 us
    select_n x1, other arithmetic, per_device(): jnp.where(lax.axis_index('blk') % 2 == 0, jnp.concatenate([n0, n1], axis=...  2.81 us
  transfers between devices with their start and end apart: 11, of which 7 were waited for; matrix products, arithmetic and copies ran while one was open for 5% of the time, Pallas kernels for 4%

profile of v5, /device:TPU:56, one launch (start us, length us, event | category | flops | bytes accessed | tf_op | source)
XLA Modules:
  0.0 117.6 jit_solution(8232230326154573927)
XLA Ops:
  0.0 0.0 copy-start
  0.0 0.0 copy-start.7
  0.0 0.0 copy-start.5
  0.0 0.0 copy-start.4
  0.0 2.1 %collective-permute-start.3 = (bf16[2944,256]{1,0:T(8,128)(2,1)}, bf16[2944,256]{1,0:T(8,128)(2,1)S(1)}, u32[]{:S(2)}, u32[]{:S(2)}) collective-permute-start(bf16[2944,256]{1,0:T(8,128)(2,1)} %o_ref.1), channel_id=1, source_target_pairs={{0,8},{8,0},{16,24},{24,16},{32,40},{40,32},{48,56},{56,48},{64,72... | collective-permute-start | bytes 4521992 | tf_op jit(solution)/shard_map/ppermute | solution.py:283
  2.1 2.6 %fusion = (bf16[1472,256]{1,0:T(8,128)(2,1)}, bf16[1472,256]{1,0:T(8,128)(2,1)}) fusion(bf16[2944,256]{1,0:T(8,128)(2,1)} %o_ref.1), kind=kLoop, calls=%fused_computation.1 | loop fusion | bytes 3014656 | tf_op jit(solution)/shard_map/slice | solution.py:289
  4.7 4.3 %collective-permute-start.1 = (bf16[1472,256]{1,0:T(8,128)(2,1)}, bf16[1472,256]{1,0:T(8,128)(2,1)S(1)}, u32[]{:S(2)}, u32[]{:S(2)}) collective-permute-start(bf16[1472,256]{1,0:T(8,128)(2,1)} %get-tuple-element.29), channel_id=1, source_target_pairs={{0,16},{8,24},{16,32},{24,40},{32,48},{40,56},{48,64},{56,72},{64,... | collective-permute-start | bytes 2261000 | tf_op jit(solution)/shard_map/ppermute | solution.py:280
  8.9 13.0 %collective-permute-start = (bf16[1472,256]{1,0:T(8,128)(2,1)}, bf16[1472,256]{1,0:T(8,128)(2,1)S(1)}, u32[]{:S(2)}, u32[]{:S(2)}) collective-permute-start(bf16[1472,256]{1,0:T(8,128)(2,1)} %get-tuple-element.30), channel_id=1, source_target_pairs={{0,752},{8,760},{16,0},{24,8},{32,16},{40,24},{48,32},{56,40},{64,... | collective-permute-start | bytes 2261000 | tf_op jit(solution)/shard_map/ppermute | solution.py:280
  22.0 0.0 copy-done.7
  22.0 2.1 %collective-permute-start.2 = (f32[4]{0:T(128)S(1)}, f32[4]{0:T(128)S(1)}, u32[]{:S(2)}, u32[]{:S(2)}) collective-permute-start(f32[4]{0:T(128)S(1)} %copy-done.7), channel_id=1, source_target_pairs={{0,8},{8,0},{16,24},{24,16},{32,40},{40,32},{48,56},{56,48},{64,72... | collective-permute-start | bytes 56 | tf_op jit(solution)/shard_map/ppermute | solution.py:283
  24.1 0.9 collective-permute-done.2.other_ref
  25.0 0.0 collective-permute-done.3.p_ref
  25.0 0.0 copy-start.1
  25.0 0.0 copy-done.4
  25.0 0.1 broadcast_in_dim.10.vir_rows_ref
  25.1 0.0 copy-done
  25.1 0.0 copy-done.5
  25.1 2.3 %prep.1 = (bf16[256,1472]{1,0:T(8,128)(2,1)S(1)}, bf16[256,1472]{1,0:T(8,128)(2,1)S(1)}, bf16[256,1472]{1,0:T(8,128)(2,1)S(1)}, bf16[8,48,256]{2,1,0:T(8,128)(2,...) custom-call(s32[8]{0:T(128)S(1)} %copy-done.5, f32[4]{0:T(128)S(1)} %copy-done.7, ...), custom_call_target="tpu_custom_call" | custom-call | flops 771751936 | bytes 6029312 | tf_op jit(solution)/shard_map/prep/pallas_call | solution.py:295
  27.4 0.0 copy-done.1
  27.4 3.9 %collective-permute-start.7 = (bf16[1472,256]{1,0:T(8,128)(2,1)}, bf16[1472,256]{1,0:T(8,128)(2,1)}, u32[]{:S(2)}, u32[]{:S(2)}) collective-permute-start(bf16[1472,256]{1,0:T(8,128)(2,1)} %get-tuple-element.29), channel_id=1, source_target_pairs={{0,752},{8,760},{16,0},{24,8},{32,16},{40,24},{48,32},{56,40},{64,... | collective-permute-start | bytes 2261000 | tf_op jit(solution)/shard_map/ppermute | solution.py:280
  31.3 1.9 %collective-permute-start.8 = (bf16[1472,256]{1,0:T(8,128)(2,1)}, bf16[1472,256]{1,0:T(8,128)(2,1)}, u32[]{:S(2)}, u32[]{:S(2)}) collective-permute-start(bf16[1472,256]{1,0:T(8,128)(2,1)} %get-tuple-element.30), channel_id=1, source_target_pairs={{0,16},{8,24},{16,32},{24,40},{32,48},{40,56},{48,64},{56,72},{64,... | collective-permute-start | bytes 2261000 | tf_op jit(solution)/shard_map/ppermute | solution.py:280
  33.3 4.5 %collective-permute-done.1.m_ref.m1_ref = bf16[1472,256]{1,0:T(8,128)(2,1)S(1)} collective-permute-done((bf16[1472,256]{1,0:T(8,128)(2,1)}, bf16[1472,256]{1,0:T(8,128)(2,1)S(1)}, u32[]{:S(2)}, u32[]{:S(2)}) %collective-permute-start.1) | collective-permute-done | bytes 753696 | tf_op jit(solution)/shard_map/ppermute | solution.py:280
  37.7 1.7 %collective-permute-done.n_ref.n0_ref = bf16[1472,256]{1,0:T(8,128)(2,1)S(1)} collective-permute-done((bf16[1472,256]{1,0:T(8,128)(2,1)}, bf16[1472,256]{1,0:T(8,128)(2,1)S(1)}, u32[]{:S(2)}, u32[]{:S(2)}) %collective-permute-start) | collective-permute-done | bytes 753696 | tf_op jit(solution)/shard_map/ppermute | solution.py:280
  39.4 1.1 far.1
  40.5 0.0 copy-start.3
  40.5 0.8 copy-done.3
  41.3 9.7 %all-to-all-start = ((bf16[8,144,256]{2,1,0:T(8,128)(2,1)}), bf16[8,144,256]{2,1,0:T(8,128)(2,1)}, u32[]{:S(2)}, u32[]{:S(2)}) async-start(bf16[8,144,256]{2,1,0:T(8,128)(2,1)} %copy-done.3), calls=%async_computation | async-start | bytes 1179648 | tf_op jit(solution)/shard_map/all_to_all | solution.py:323
  51.0 0.0 copy-start.6
  51.0 4.2 %collective-permute-done.7.n1_ref = bf16[1472,256]{1,0:T(8,128)(2,1)} collective-permute-done((bf16[1472,256]{1,0:T(8,128)(2,1)}, bf16[1472,256]{1,0:T(8,128)(2,1)}, u32[]{:S(2)}, u32[]{:S(2)}) %collective-permute-start.7) | collective-permute-done | bytes 753696 | tf_op jit(solution)/shard_map/ppermute | solution.py:280
  55.2 0.0 collective-permute-done.8.m0_ref
  55.2 2.8 %maximum_select_fusion = bf16[2944,256]{1,0:T(8,128)(2,1)} fusion(bf16[1472,256]{1,0:T(8,128)(2,1)} %collective-permute-done.7.n1_ref, bf16[1472,256]{1,0:T(8,128)(2,1)S(1)} %collective-permute-done.n_ref.n0_ref, bf16[1472,256]{1,0:T(8,128)(2,1)S(1)} %collective-permute-done.1.m_ref.m1_ref, bf16[1472,256]{1,0:T(8,128)(2,1)} %collective-permute-done.8.m0_ref, ...), kind=kLoop, calls=%fused_computation | loop fusion | flops 6782976 | bytes 4521985 | tf_op jit(solution)/shard_map/jit(_where)/select_n | solution.py:347
  58.0 1.9 %collective-permute-start.9 = (bf16[2944,256]{1,0:T(8,128)(2,1)}, bf16[2944,256]{1,0:T(8,128)(2,1)}, u32[]{:S(2)}, u32[]{:S(2)}) collective-permute-start(bf16[2944,256]{1,0:T(8,128)(2,1)} %maximum_select_fusion), channel_id=1, source_target_pairs={{0,8},{8,0},{16,24},{24,16},{32,40},{40,32},{48,56},{56,48},{64,72... | collective-permute-start | bytes 4521992 | tf_op jit(solution)/shard_map/ppermute | solution.py:283
  59.9 5.0 %all-to-all-done.parts_ref = bf16[8,144,256]{2,1,0:T(8,128)(2,1)} async-done(((bf16[8,144,256]{2,1,0:T(8,128)(2,1)}), bf16[8,144,256]{2,1,0:T(8,128)(2,1)}, u32[]{:S(2)}, u32[]{:S(2)}) %all-to-all-start) | async-done | bytes 589856 | tf_op jit(solution)/shard_map/all_to_all | solution.py:323
  65.0 0.0 copy-start.2
  65.0 1.3 %pack.1 = (f32[112,256]{1,0:T(8,128)S(1)}, bf16[80,256]{1,0:T(8,128)(2,1)S(1)}, bf16[80,256]{1,0:T(8,128)(2,1)S(1)}, bf16[48,256]{1,0:T(8,128)(2,1)S(1)}) custom-call(bf16[8,144,256]{2,1,0:T(8,128)(2,1)} %all-to-all-done.parts_ref, bf16[16,256]{1,0:T(8,128)(2,1)S(1)} %get-tuple-element.23.head_ref), custom_call_target="tpu_custom_call" | custom-call | flops 65536 | bytes 262144 | tf_op jit(solution)/shard_map/pack/pallas_call | solution.py:325
  66.3 13.5 %collective-permute-start.4 = (bf16[80,256]{1,0:T(8,128)(2,1)S(1)}, bf16[80,256]{1,0:T(8,128)(2,1)S(1)}, u32[]{:S(2)}, u32[]{:S(2)}) collective-permute-start(bf16[80,256]{1,0:T(8,128)(2,1)S(1)} %get-tuple-element.26), channel_id=1, source_target_pairs={{0,752},{8,760},{16,0},{24,8},{32,16},{40,24},{48,32},{56,40},{64,... | collective-permute-start | bytes 122888 | tf_op jit(solution)/shard_map/ppermute | solution.py:280
  79.8 1.9 %collective-permute-start.5 = (bf16[80,256]{1,0:T(8,128)(2,1)S(1)}, bf16[80,256]{1,0:T(8,128)(2,1)S(1)}, u32[]{:S(2)}, u32[]{:S(2)}) collective-permute-start(bf16[80,256]{1,0:T(8,128)(2,1)S(1)} %get-tuple-element.27), channel_id=1, source_target_pairs={{0,16},{8,24},{16,32},{24,40},{32,48},{40,56},{48,64},{56,72},{64,... | collective-permute-start | bytes 122888 | tf_op jit(solution)/shard_map/ppermute | solution.py:280
  81.7 1.9 %collective-permute-start.6 = (bf16[48,256]{1,0:T(8,128)(2,1)S(1)}, bf16[48,256]{1,0:T(8,128)(2,1)S(1)}, u32[]{:S(2)}, u32[]{:S(2)}) collective-permute-start(bf16[48,256]{1,0:T(8,128)(2,1)S(1)} %get-tuple-element.28), channel_id=1, source_target_pairs={{0,8},{8,0},{16,24},{24,16},{32,40},{40,32},{48,56},{56,48},{64,72... | collective-permute-start | bytes 73736 | tf_op jit(solution)/shard_map/ppermute | solution.py:283
  83.6 1.2 collective-permute-done.6.refs_5_
  84.8 0.0 collective-permute-done.4.refs_3_
  84.8 3.0 %collective-permute-done.5.refs_4_ = bf16[80,256]{1,0:T(8,128)(2,1)S(1)} collective-permute-done((bf16[80,256]{1,0:T(8,128)(2,1)S(1)}, bf16[80,256]{1,0:T(8,128)(2,1)S(1)}, u32[]{:S(2)}, u32[]{:S(2)}) %collective-permute-start.5) | collective-permute-done | bytes 40992 | tf_op jit(solution)/shard_map/ppermute | solution.py:280
  87.8 0.0 copy-done.6
  87.8 0.6 amplitude.1
  88.4 24.2 %all_to_all.10.amps_ref = bf16[8,5,32,256]{3,2,1,0:T(8,128)(2,1)S(1)} all-to-all(bf16[8,5,32,256]{3,2,1,0:T(8,128)(2,1)S(1)} %amplitude.1), channel_id=1, replica_groups=mesh['blk'=96,'grp'=8] {'grp'}, dimensions={0} | all-to-all | bytes 1310720 | tf_op jit(solution)/shard_map/all_to_all | solution.py:346
  112.6 0.0 collective-permute-done.9.x_ref
  112.6 0.0 copy-done.2
  112.6 5.0 %gamma.1 = bf16[2944,256]{1,0:T(8,128)(2,1)} custom-call(s32[8]{0:T(128)S(1)} %copy-done.5, bf16[8,5,32,256]{3,2,1,0:T(8,128)(2,1)S(1)} %all_to_all.10.amps_ref, bf16[2944,256]{1,0:T(8,128)(2,1)S(1)} %copy-done, bf16[2944,256]{1,0:T(8,128)(2,1)S(1)} %copy-done.2, bf16[1472,256]{1,0:T(8,128)(2,1)S(1)} %collective-permute-done.n_ref.n0_ref, ...), custom_call_target="tpu_custom_call" | custom-call | flops 1929379840 | bytes 10551296 | tf_op jit(solution)/shard_map/gamma/pallas_call | solution.py:352
Async XLA Ops:
  0.0 25.1 %copy-start = (bf16[2944,256]{1,0:T(8,128)(2,1)S(1)}, bf16[2944,256]{1,0:T(8,128)(2,1)}, u32[]{:S(2)}) copy-start(bf16[2944,256]{1,0:T(8,128)(2,1)} %o_ref.1) | copy-start | bytes 4521988
  0.0 22.0 %copy-start.7 = (f32[4]{0:T(128)S(1)}, f32[4]{0:T(128)}, u32[]{:S(2)}) copy-start(f32[4]{0:T(128)} %energy_ref.1) | copy-start | bytes 52
  0.0 25.1 %copy-start.5 = (s32[8]{0:T(128)S(1)}, s32[8]{0:T(128)}, u32[]{:S(2)}) copy-start(s32[8]{0:T(128)} %aux_ref.3) | copy-start | bytes 100
  0.0 25.0 %copy-start.4 = (f32[64]{0:T(128)S(1)}, f32[64]{0:T(128)}, u32[]{:S(2)}) copy-start(f32[64]{0:T(128)} %param.7) | copy-start | bytes 772
  0.0 25.0 %collective-permute-start.3 = (bf16[2944,256]{1,0:T(8,128)(2,1)}, bf16[2944,256]{1,0:T(8,128)(2,1)S(1)}, u32[]{:S(2)}, u32[]{:S(2)}) collective-permute-start(bf16[2944,256]{1,0:T(8,128)(2,1)} %o_ref.1), channel_id=1, source_target_pairs={{0,8},{8,0},{16,24},{24,16},{32,40},{40,32},{48,56},{56,48},{64,72... | collective-permute-start | bytes 4521992 | tf_op jit(solution)/shard_map/ppermute | solution.py:283
  4.7 33.1 %collective-permute-start.1 = (bf16[1472,256]{1,0:T(8,128)(2,1)}, bf16[1472,256]{1,0:T(8,128)(2,1)S(1)}, u32[]{:S(2)}, u32[]{:S(2)}) collective-permute-start(bf16[1472,256]{1,0:T(8,128)(2,1)} %get-tuple-element.29), channel_id=1, source_target_pairs={{0,16},{8,24},{16,32},{24,40},{32,48},{40,56},{48,64},{56,72},{64,... | collective-permute-start | bytes 2261000 | tf_op jit(solution)/shard_map/ppermute | solution.py:280
  8.9 30.5 %collective-permute-start = (bf16[1472,256]{1,0:T(8,128)(2,1)}, bf16[1472,256]{1,0:T(8,128)(2,1)S(1)}, u32[]{:S(2)}, u32[]{:S(2)}) collective-permute-start(bf16[1472,256]{1,0:T(8,128)(2,1)} %get-tuple-element.30), channel_id=1, source_target_pairs={{0,752},{8,760},{16,0},{24,8},{32,16},{40,24},{48,32},{56,40},{64,... | collective-permute-start | bytes 2261000 | tf_op jit(solution)/shard_map/ppermute | solution.py:280
  22.0 3.0 %collective-permute-start.2 = (f32[4]{0:T(128)S(1)}, f32[4]{0:T(128)S(1)}, u32[]{:S(2)}, u32[]{:S(2)}) collective-permute-start(f32[4]{0:T(128)S(1)} %copy-done.7), channel_id=1, source_target_pairs={{0,8},{8,0},{16,24},{24,16},{32,40},{40,32},{48,56},{56,48},{64,72... | collective-permute-start | bytes 56 | tf_op jit(solution)/shard_map/ppermute | solution.py:283
  25.0 2.4 %copy-start.1 = (bf16[2944,256]{1,0:T(8,128)(2,1)}, bf16[2944,256]{1,0:T(8,128)(2,1)S(1)}, u32[]{:S(2)}) copy-start(bf16[2944,256]{1,0:T(8,128)(2,1)S(1)} %collective-permute-done.3.p_ref) | copy-start | bytes 4521988
  27.4 27.8 %collective-permute-start.7 = (bf16[1472,256]{1,0:T(8,128)(2,1)}, bf16[1472,256]{1,0:T(8,128)(2,1)}, u32[]{:S(2)}, u32[]{:S(2)}) collective-permute-start(bf16[1472,256]{1,0:T(8,128)(2,1)} %get-tuple-element.29), channel_id=1, source_target_pairs={{0,752},{8,760},{16,0},{24,8},{32,16},{40,24},{48,32},{56,40},{64,... | collective-permute-start | bytes 2261000 | tf_op jit(solution)/shard_map/ppermute | solution.py:280
  31.3 23.9 %collective-permute-start.8 = (bf16[1472,256]{1,0:T(8,128)(2,1)}, bf16[1472,256]{1,0:T(8,128)(2,1)}, u32[]{:S(2)}, u32[]{:S(2)}) collective-permute-start(bf16[1472,256]{1,0:T(8,128)(2,1)} %get-tuple-element.30), channel_id=1, source_target_pairs={{0,16},{8,24},{16,32},{24,40},{32,48},{40,56},{48,64},{56,72},{64,... | collective-permute-start | bytes 2261000 | tf_op jit(solution)/shard_map/ppermute | solution.py:280
  40.5 0.8 copy-start.3
  41.3 23.7 %all-to-all-start = ((bf16[8,144,256]{2,1,0:T(8,128)(2,1)}), bf16[8,144,256]{2,1,0:T(8,128)(2,1)}, u32[]{:S(2)}, u32[]{:S(2)}) async-start(bf16[8,144,256]{2,1,0:T(8,128)(2,1)} %copy-done.3), calls=%async_computation | async-start | bytes 1179648 | tf_op jit(solution)/shard_map/all_to_all | solution.py:323
  51.0 36.8 %copy-start.6 = (s32[96]{0:T(128)S(1)}, s32[96]{0:T(128)}, u32[]{:S(2)}) copy-start(s32[96]{0:T(128)} %refs_0_.1) | copy-start | bytes 1156
  58.0 54.5 %collective-permute-start.9 = (bf16[2944,256]{1,0:T(8,128)(2,1)}, bf16[2944,256]{1,0:T(8,128)(2,1)}, u32[]{:S(2)}, u32[]{:S(2)}) collective-permute-start(bf16[2944,256]{1,0:T(8,128)(2,1)} %maximum_select_fusion), channel_id=1, source_target_pairs={{0,8},{8,0},{16,24},{24,16},{32,40},{40,32},{48,56},{56,48},{64,72... | collective-permute-start | bytes 4521992 | tf_op jit(solution)/shard_map/ppermute | solution.py:283
  65.0 47.6 %copy-start.2 = (bf16[2944,256]{1,0:T(8,128)(2,1)S(1)}, bf16[2944,256]{1,0:T(8,128)(2,1)}, u32[]{:S(2)}) copy-start(bf16[2944,256]{1,0:T(8,128)(2,1)} %copy-done.1) | copy-start | bytes 4521988
  66.3 18.5 %collective-permute-start.4 = (bf16[80,256]{1,0:T(8,128)(2,1)S(1)}, bf16[80,256]{1,0:T(8,128)(2,1)S(1)}, u32[]{:S(2)}, u32[]{:S(2)}) collective-permute-start(bf16[80,256]{1,0:T(8,128)(2,1)S(1)} %get-tuple-element.26), channel_id=1, source_target_pairs={{0,752},{8,760},{16,0},{24,8},{32,16},{40,24},{48,32},{56,40},{64,... | collective-permute-start | bytes 122888 | tf_op jit(solution)/shard_map/ppermute | solution.py:280
  79.8 8.0 %collective-permute-start.5 = (bf16[80,256]{1,0:T(8,128)(2,1)S(1)}, bf16[80,256]{1,0:T(8,128)(2,1)S(1)}, u32[]{:S(2)}, u32[]{:S(2)}) collective-permute-start(bf16[80,256]{1,0:T(8,128)(2,1)S(1)} %get-tuple-element.27), channel_id=1, source_target_pairs={{0,16},{8,24},{16,32},{24,40},{32,48},{40,56},{48,64},{56,72},{64,... | collective-permute-start | bytes 122888 | tf_op jit(solution)/shard_map/ppermute | solution.py:280
  81.7 3.1 %collective-permute-start.6 = (bf16[48,256]{1,0:T(8,128)(2,1)S(1)}, bf16[48,256]{1,0:T(8,128)(2,1)S(1)}, u32[]{:S(2)}, u32[]{:S(2)}) collective-permute-start(bf16[48,256]{1,0:T(8,128)(2,1)S(1)} %get-tuple-element.28), channel_id=1, source_target_pairs={{0,8},{8,0},{16,24},{24,16},{32,40},{40,32},{48,56},{56,48},{64,72... | collective-permute-start | bytes 73736 | tf_op jit(solution)/shard_map/ppermute | solution.py:283

commit v6 on v5

--- a/solution.py
+++ b/solution.py
@@ -212,10 +212,22 @@
 
 
 def gamma_kernel(
-    aux_ref, amps_ref, o_ref, p_ref, n0_ref, n1_ref, m0_ref, m1_ref, x_ref, out_ref, result, weights, sems
+    aux_ref, amps_ref, o_ref, p_ref, n0_ref, n1_ref, m0_ref, m1_ref, x_ref, out_ref,
+    n_buf, m_buf, x_buf, result, weights, sems,
 ):
     rows, cols = o_ref.shape
     half = rows // 2
+    tiles = sems.shape[1]
+    tile = rows // tiles
+    fetches = []
+    for j in range(tiles):
+        start = j * tile
+        here, low = pl.ds(start, tile), pl.ds(start % half, tile)
+        wanted = [(x_ref.at[here, :], x_buf.at[here, :])]
+        wanted.append((m0_ref.at[low, :], m_buf.at[low, :]) if start < half else (n1_ref.at[low, :], n_buf.at[low, :]))
+        fetches.append([pltpu.make_async_copy(src, dst, sems.at[k, j]) for k, (src, dst) in enumerate(wanted)])
+        for copy in fetches[j]:
+            copy.start()
     _, parity, g = place()
 
     def put(j, matrix):
@@ -242,17 +254,18 @@
         put(1, both)
         put(4, whole(4))
 
-    tile = rows // sems.shape[0]
     copies = []
-    for j in range(sems.shape[0]):
+    for j in range(tiles):
         start = j * tile
-        n_ref, m_ref, low = (n0_ref, m0_ref, start) if start < half else (n1_ref, m1_ref, start - half)
-        here, there = pl.ds(start, tile), pl.ds(low, tile)
+        n_ref, m_ref = (n0_ref, m_buf) if start < half else (n_buf, m1_ref)
+        here, low = pl.ds(start, tile), pl.ds(start % half, tile)
+        for copy in fetches[j]:
+            copy.wait()
         blocks = jnp.concatenate(
-            [o_ref[here, :], p_ref[here, :], n_ref[there, :], m_ref[there, :], x_ref[here, :]], axis=1
+            [o_ref[here, :], p_ref[here, :], n_ref[low, :], m_ref[low, :], x_buf[here, :]], axis=1
         )
         result[here, :] = keep_rows(mm(blocks, weights[...]), start, aux_ref[g]).astype(result.dtype)
-        copy = pltpu.make_async_copy(result.at[here, :], out_ref.at[here, :], sems.at[j])
+        copy = pltpu.make_async_copy(result.at[here, :], out_ref.at[here, :], sems.at[2, j])
         copy.start()
         copies.append(copy)
     for copy in copies:
@@ -351,12 +364,13 @@
     tiles = 8
     return pl.pallas_call(
         gamma_kernel,
-        in_specs=[SM] + [VM] * 8,
+        in_specs=[SM, VM, VM, VM, VM, ANY, ANY, VM, ANY],
         out_specs=ANY,
         out_shape=jax.ShapeDtypeStruct((rows, cols), three_index.dtype),
         scratch_shapes=[
+            pltpu.VMEM((half, cols), BF), pltpu.VMEM((half, cols), BF), pltpu.VMEM((rows, cols), BF),
             pltpu.VMEM((rows, cols), three_index.dtype), pltpu.VMEM((5 * cols, cols), BF),
-            pltpu.SemaphoreType.DMA((tiles,)),
+            pltpu.SemaphoreType.DMA((3, tiles)),
         ],
         cost_estimate=cost(10 * rows * cols * cols, 14 * rows * cols),
         compiler_params=memory(20),

time: 118 us -> 121 us (1.025)
  Pallas kernels: 10.3 us -> 12.8 us
    pallas_call x1, Pallas kernels: 5 us -> 7.54 us  [per_device(): pl.pallas_call(gamma_kernel, in_specs=[SM, VM, VM, VM, VM, ANY, ANY, VM,...]
where the time goes in v6:
time: 121 us; the launch traced here: 120 us
  starting transfers between devices  56.2 us (46%)
  blocking collectives  24.2 us (20%)
  waiting for transfers between devices  20.4 us (17%)
  Pallas kernels  12.8 us (11%)
  local copies, waits for them, and re-layouts  3.53 us (3%)
  other arithmetic  2.81 us (2%)
    ppermute x6, starting transfers between devices, shift(): lax.ppermute(value, 'blk', [(i, (i + steps) % slabs) for i in range(slabs)])  38.5 us
    all_to_all x1, blocking collectives, per_device(): amps = lax.all_to_all(amps, 'grp', 0, 0)  24.2 us
    ppermute x6, waiting for transfers between devices, shift(): lax.ppermute(value, 'blk', [(i, (i + steps) % slabs) for i in range(slabs)])  13.3 us
    all_to_all x1, starting transfers between devices, per_device(): pieces = lax.all_to_all(partial_sums, 'grp', 0, 0)  9.67 us
    ppermute x4, starting transfers between devices, swap(): return lax.ppermute(value, 'blk', [(i, i ^ 1) for i in range(slabs)])  8.01 us
    pallas_call x1, Pallas kernels, per_device(): pl.pallas_call(gamma_kernel, in_specs=[SM, VM, VM, VM, VM, ANY, ANY, VM,...  7.54 us
    all_to_all x1, waiting for transfers between devices, per_device(): pieces = lax.all_to_all(partial_sums, 'grp', 0, 0)  5.05 us
    select_n x1, other arithmetic, per_device(): jnp.where(lax.axis_index('blk') % 2 == 0, jnp.concatenate([n0, n1], axis=...  2.81 us
  transfers between devices with their start and end apart: 11, of which 7 were waited for; matrix products, arithmetic and copies ran while one was open for 5% of the time, Pallas kernels for 4%

profile of v6, /device:TPU:56, one launch (start us, length us, event | category | flops | bytes accessed | tf_op | source)
XLA Modules:
  0.0 120.1 jit_solution(2817890796202918046)
XLA Ops:
  0.0 0.0 copy-start
  0.0 0.0 copy-start.7
  0.0 0.0 copy-start.5
  0.0 0.0 copy-start.4
  0.0 2.1 %collective-permute-start.3 = (bf16[2944,256]{1,0:T(8,128)(2,1)}, bf16[2944,256]{1,0:T(8,128)(2,1)S(1)}, u32[]{:S(2)}, u32[]{:S(2)}) collective-permute-start(bf16[2944,256]{1,0:T(8,128)(2,1)} %o_ref.1), channel_id=1, source_target_pairs={{0,8},{8,0},{16,24},{24,16},{32,40},{40,32},{48,56},{56,48},{64,72... | collective-permute-start | bytes 4521992 | tf_op jit(solution)/shard_map/ppermute | solution.py:296
  2.1 2.6 %fusion = (bf16[1472,256]{1,0:T(8,128)(2,1)}, bf16[1472,256]{1,0:T(8,128)(2,1)}) fusion(bf16[2944,256]{1,0:T(8,128)(2,1)} %o_ref.1), kind=kLoop, calls=%fused_computation.1 | loop fusion | bytes 3014656 | tf_op jit(solution)/shard_map/slice | solution.py:302
  4.7 4.3 %collective-permute-start.1 = (bf16[1472,256]{1,0:T(8,128)(2,1)}, bf16[1472,256]{1,0:T(8,128)(2,1)S(1)}, u32[]{:S(2)}, u32[]{:S(2)}) collective-permute-start(bf16[1472,256]{1,0:T(8,128)(2,1)} %get-tuple-element.29), channel_id=1, source_target_pairs={{0,16},{8,24},{16,32},{24,40},{32,48},{40,56},{48,64},{56,72},{64,... | collective-permute-start | bytes 2261000 | tf_op jit(solution)/shard_map/ppermute | solution.py:293
  8.9 13.0 %collective-permute-start = (bf16[1472,256]{1,0:T(8,128)(2,1)}, bf16[1472,256]{1,0:T(8,128)(2,1)S(1)}, u32[]{:S(2)}, u32[]{:S(2)}) collective-permute-start(bf16[1472,256]{1,0:T(8,128)(2,1)} %get-tuple-element.30), channel_id=1, source_target_pairs={{0,752},{8,760},{16,0},{24,8},{32,16},{40,24},{48,32},{56,40},{64,... | collective-permute-start | bytes 2261000 | tf_op jit(solution)/shard_map/ppermute | solution.py:293
  22.0 0.0 copy-done.7
  22.0 2.1 %collective-permute-start.2 = (f32[4]{0:T(128)S(1)}, f32[4]{0:T(128)S(1)}, u32[]{:S(2)}, u32[]{:S(2)}) collective-permute-start(f32[4]{0:T(128)S(1)} %copy-done.7), channel_id=1, source_target_pairs={{0,8},{8,0},{16,24},{24,16},{32,40},{40,32},{48,56},{56,48},{64,72... | collective-permute-start | bytes 56 | tf_op jit(solution)/shard_map/ppermute | solution.py:296
  24.1 0.9 collective-permute-done.2.other_ref
  25.0 0.0 collective-permute-done.3.p_ref
  25.0 0.0 copy-start.1
  25.0 0.0 copy-done.4
  25.0 0.1 broadcast_in_dim.10.vir_rows_ref
  25.1 0.0 copy-done
  25.1 0.0 copy-done.5
  25.1 2.3 %prep.1 = (bf16[256,1472]{1,0:T(8,128)(2,1)S(1)}, bf16[256,1472]{1,0:T(8,128)(2,1)S(1)}, bf16[256,1472]{1,0:T(8,128)(2,1)S(1)}, bf16[8,48,256]{2,1,0:T(8,128)(2,...) custom-call(s32[8]{0:T(128)S(1)} %copy-done.5, f32[4]{0:T(128)S(1)} %copy-done.7, ...), custom_call_target="tpu_custom_call" | custom-call | flops 771751936 | bytes 6029312 | tf_op jit(solution)/shard_map/prep/pallas_call | solution.py:308
  27.4 0.0 copy-done.1
  27.4 3.9 %collective-permute-start.7 = (bf16[1472,256]{1,0:T(8,128)(2,1)}, bf16[1472,256]{1,0:T(8,128)(2,1)}, u32[]{:S(2)}, u32[]{:S(2)}) collective-permute-start(bf16[1472,256]{1,0:T(8,128)(2,1)} %get-tuple-element.29), channel_id=1, source_target_pairs={{0,752},{8,760},{16,0},{24,8},{32,16},{40,24},{48,32},{56,40},{64,... | collective-permute-start | bytes 2261000 | tf_op jit(solution)/shard_map/ppermute | solution.py:293
  31.3 1.9 %collective-permute-start.8 = (bf16[1472,256]{1,0:T(8,128)(2,1)}, bf16[1472,256]{1,0:T(8,128)(2,1)}, u32[]{:S(2)}, u32[]{:S(2)}) collective-permute-start(bf16[1472,256]{1,0:T(8,128)(2,1)} %get-tuple-element.30), channel_id=1, source_target_pairs={{0,16},{8,24},{16,32},{24,40},{32,48},{40,56},{48,64},{56,72},{64,... | collective-permute-start | bytes 2261000 | tf_op jit(solution)/shard_map/ppermute | solution.py:293
  33.3 4.5 %collective-permute-done.1.m_ref.m1_ref = bf16[1472,256]{1,0:T(8,128)(2,1)S(1)} collective-permute-done((bf16[1472,256]{1,0:T(8,128)(2,1)}, bf16[1472,256]{1,0:T(8,128)(2,1)S(1)}, u32[]{:S(2)}, u32[]{:S(2)}) %collective-permute-start.1) | collective-permute-done | bytes 753696 | tf_op jit(solution)/shard_map/ppermute | solution.py:293
  37.7 1.7 %collective-permute-done.n_ref.n0_ref = bf16[1472,256]{1,0:T(8,128)(2,1)S(1)} collective-permute-done((bf16[1472,256]{1,0:T(8,128)(2,1)}, bf16[1472,256]{1,0:T(8,128)(2,1)S(1)}, u32[]{:S(2)}, u32[]{:S(2)}) %collective-permute-start) | collective-permute-done | bytes 753696 | tf_op jit(solution)/shard_map/ppermute | solution.py:293
  39.4 1.1 far.1
  40.5 0.0 copy-start.3
  40.5 0.8 copy-done.3
  41.3 9.7 %all-to-all-start = ((bf16[8,144,256]{2,1,0:T(8,128)(2,1)}), bf16[8,144,256]{2,1,0:T(8,128)(2,1)}, u32[]{:S(2)}, u32[]{:S(2)}) async-start(bf16[8,144,256]{2,1,0:T(8,128)(2,1)} %copy-done.3), calls=%async_computation | async-start | bytes 1179648 | tf_op jit(solution)/shard_map/all_to_all | solution.py:336
  51.0 0.0 copy-start.6
  51.0 4.2 %collective-permute-done.7.n1_ref = bf16[1472,256]{1,0:T(8,128)(2,1)} collective-permute-done((bf16[1472,256]{1,0:T(8,128)(2,1)}, bf16[1472,256]{1,0:T(8,128)(2,1)}, u32[]{:S(2)}, u32[]{:S(2)}) %collective-permute-start.7) | collective-permute-done | bytes 753696 | tf_op jit(solution)/shard_map/ppermute | solution.py:293
  55.2 0.0 collective-permute-done.8.m0_ref
  55.2 2.8 %maximum_select_fusion = bf16[2944,256]{1,0:T(8,128)(2,1)} fusion(bf16[1472,256]{1,0:T(8,128)(2,1)} %collective-permute-done.7.n1_ref, bf16[1472,256]{1,0:T(8,128)(2,1)S(1)} %collective-permute-done.n_ref.n0_ref, bf16[1472,256]{1,0:T(8,128)(2,1)S(1)} %collective-permute-done.1.m_ref.m1_ref, bf16[1472,256]{1,0:T(8,128)(2,1)} %collective-permute-done.8.m0_ref, ...), kind=kLoop, calls=%fused_computation | loop fusion | flops 6782976 | bytes 4521985 | tf_op jit(solution)/shard_map/jit(_where)/select_n | solution.py:360
  58.0 1.9 %collective-permute-start.9 = (bf16[2944,256]{1,0:T(8,128)(2,1)}, bf16[2944,256]{1,0:T(8,128)(2,1)}, u32[]{:S(2)}, u32[]{:S(2)}) collective-permute-start(bf16[2944,256]{1,0:T(8,128)(2,1)} %maximum_select_fusion), channel_id=1, source_target_pairs={{0,8},{8,0},{16,24},{24,16},{32,40},{40,32},{48,56},{56,48},{64,72... | collective-permute-start | bytes 4521992 | tf_op jit(solution)/shard_map/ppermute | solution.py:296
  59.9 5.0 %all-to-all-done.parts_ref = bf16[8,144,256]{2,1,0:T(8,128)(2,1)} async-done(((bf16[8,144,256]{2,1,0:T(8,128)(2,1)}), bf16[8,144,256]{2,1,0:T(8,128)(2,1)}, u32[]{:S(2)}, u32[]{:S(2)}) %all-to-all-start) | async-done | bytes 589856 | tf_op jit(solution)/shard_map/all_to_all | solution.py:336
  65.0 0.0 copy-start.2
  65.0 1.3 %pack.1 = (f32[112,256]{1,0:T(8,128)S(1)}, bf16[80,256]{1,0:T(8,128)(2,1)S(1)}, bf16[80,256]{1,0:T(8,128)(2,1)S(1)}, bf16[48,256]{1,0:T(8,128)(2,1)S(1)}) custom-call(bf16[8,144,256]{2,1,0:T(8,128)(2,1)} %all-to-all-done.parts_ref, bf16[16,256]{1,0:T(8,128)(2,1)S(1)} %get-tuple-element.23.head_ref), custom_call_target="tpu_custom_call" | custom-call | flops 65536 | bytes 262144 | tf_op jit(solution)/shard_map/pack/pallas_call | solution.py:338
  66.3 13.5 %collective-permute-start.4 = (bf16[80,256]{1,0:T(8,128)(2,1)S(1)}, bf16[80,256]{1,0:T(8,128)(2,1)S(1)}, u32[]{:S(2)}, u32[]{:S(2)}) collective-permute-start(bf16[80,256]{1,0:T(8,128)(2,1)S(1)} %get-tuple-element.26), channel_id=1, source_target_pairs={{0,752},{8,760},{16,0},{24,8},{32,16},{40,24},{48,32},{56,40},{64,... | collective-permute-start | bytes 122888 | tf_op jit(solution)/shard_map/ppermute | solution.py:293
  79.8 1.9 %collective-permute-start.5 = (bf16[80,256]{1,0:T(8,128)(2,1)S(1)}, bf16[80,256]{1,0:T(8,128)(2,1)S(1)}, u32[]{:S(2)}, u32[]{:S(2)}) collective-permute-start(bf16[80,256]{1,0:T(8,128)(2,1)S(1)} %get-tuple-element.27), channel_id=1, source_target_pairs={{0,16},{8,24},{16,32},{24,40},{32,48},{40,56},{48,64},{56,72},{64,... | collective-permute-start | bytes 122888 | tf_op jit(solution)/shard_map/ppermute | solution.py:293
  81.7 1.9 %collective-permute-start.6 = (bf16[48,256]{1,0:T(8,128)(2,1)S(1)}, bf16[48,256]{1,0:T(8,128)(2,1)S(1)}, u32[]{:S(2)}, u32[]{:S(2)}) collective-permute-start(bf16[48,256]{1,0:T(8,128)(2,1)S(1)} %get-tuple-element.28), channel_id=1, source_target_pairs={{0,8},{8,0},{16,24},{24,16},{32,40},{40,32},{48,56},{56,48},{64,72... | collective-permute-start | bytes 73736 | tf_op jit(solution)/shard_map/ppermute | solution.py:296
  83.6 1.2 collective-permute-done.6.refs_5_
  84.8 0.0 collective-permute-done.4.refs_3_
  84.8 3.0 %collective-permute-done.5.refs_4_ = bf16[80,256]{1,0:T(8,128)(2,1)S(1)} collective-permute-done((bf16[80,256]{1,0:T(8,128)(2,1)S(1)}, bf16[80,256]{1,0:T(8,128)(2,1)S(1)}, u32[]{:S(2)}, u32[]{:S(2)}) %collective-permute-start.5) | collective-permute-done | bytes 40992 | tf_op jit(solution)/shard_map/ppermute | solution.py:293
  87.8 0.0 copy-done.6
  87.8 0.6 amplitude.1
  88.4 24.2 %all_to_all.10.amps_ref = bf16[8,5,32,256]{3,2,1,0:T(8,128)(2,1)S(1)} all-to-all(bf16[8,5,32,256]{3,2,1,0:T(8,128)(2,1)S(1)} %amplitude.1), channel_id=1, replica_groups=mesh['blk'=96,'grp'=8] {'grp'}, dimensions={0} | all-to-all | bytes 1310720 | tf_op jit(solution)/shard_map/all_to_all | solution.py:359
  112.6 0.0 collective-permute-done.9.x_ref
  112.6 0.0 copy-done.2
  112.6 7.5 %gamma.1 = bf16[2944,256]{1,0:T(8,128)(2,1)} custom-call(s32[8]{0:T(128)S(1)} %copy-done.5, bf16[8,5,32,256]{3,2,1,0:T(8,128)(2,1)S(1)} %all_to_all.10.amps_ref, bf16[2944,256]{1,0:T(8,128)(2,1)S(1)} %copy-done, bf16[2944,256]{1,0:T(8,128)(2,1)S(1)} %copy-done.2, bf16[1472,256]{1,0:T(8,128)(2,1)S(1)} %collective-permute-done.n_ref.n0_ref, ...), custom_call_target="tpu_custom_call" | custom-call | flops 1929379840 | bytes 10551296 | tf_op jit(solution)/shard_map/gamma/pallas_call | solution.py:365
Async XLA Ops:
  0.0 25.1 %copy-start = (bf16[2944,256]{1,0:T(8,128)(2,1)S(1)}, bf16[2944,256]{1,0:T(8,128)(2,1)}, u32[]{:S(2)}) copy-start(bf16[2944,256]{1,0:T(8,128)(2,1)} %o_ref.1) | copy-start | bytes 4521988
  0.0 22.0 %copy-start.7 = (f32[4]{0:T(128)S(1)}, f32[4]{0:T(128)}, u32[]{:S(2)}) copy-start(f32[4]{0:T(128)} %energy_ref.1) | copy-start | bytes 52
  0.0 25.1 %copy-start.5 = (s32[8]{0:T(128)S(1)}, s32[8]{0:T(128)}, u32[]{:S(2)}) copy-start(s32[8]{0:T(128)} %aux_ref.3) | copy-start | bytes 100
  0.0 25.0 %copy-start.4 = (f32[64]{0:T(128)S(1)}, f32[64]{0:T(128)}, u32[]{:S(2)}) copy-start(f32[64]{0:T(128)} %param.7) | copy-start | bytes 772
  0.0 25.0 %collective-permute-start.3 = (bf16[2944,256]{1,0:T(8,128)(2,1)}, bf16[2944,256]{1,0:T(8,128)(2,1)S(1)}, u32[]{:S(2)}, u32[]{:S(2)}) collective-permute-start(bf16[2944,256]{1,0:T(8,128)(2,1)} %o_ref.1), channel_id=1, source_target_pairs={{0,8},{8,0},{16,24},{24,16},{32,40},{40,32},{48,56},{56,48},{64,72... | collective-permute-start | bytes 4521992 | tf_op jit(solution)/shard_map/ppermute | solution.py:296
  4.7 33.1 %collective-permute-start.1 = (bf16[1472,256]{1,0:T(8,128)(2,1)}, bf16[1472,256]{1,0:T(8,128)(2,1)S(1)}, u32[]{:S(2)}, u32[]{:S(2)}) collective-permute-start(bf16[1472,256]{1,0:T(8,128)(2,1)} %get-tuple-element.29), channel_id=1, source_target_pairs={{0,16},{8,24},{16,32},{24,40},{32,48},{40,56},{48,64},{56,72},{64,... | collective-permute-start | bytes 2261000 | tf_op jit(solution)/shard_map/ppermute | solution.py:293
  8.9 30.5 %collective-permute-start = (bf16[1472,256]{1,0:T(8,128)(2,1)}, bf16[1472,256]{1,0:T(8,128)(2,1)S(1)}, u32[]{:S(2)}, u32[]{:S(2)}) collective-permute-start(bf16[1472,256]{1,0:T(8,128)(2,1)} %get-tuple-element.30), channel_id=1, source_target_pairs={{0,752},{8,760},{16,0},{24,8},{32,16},{40,24},{48,32},{56,40},{64,... | collective-permute-start | bytes 2261000 | tf_op jit(solution)/shard_map/ppermute | solution.py:293
  22.0 3.0 %collective-permute-start.2 = (f32[4]{0:T(128)S(1)}, f32[4]{0:T(128)S(1)}, u32[]{:S(2)}, u32[]{:S(2)}) collective-permute-start(f32[4]{0:T(128)S(1)} %copy-done.7), channel_id=1, source_target_pairs={{0,8},{8,0},{16,24},{24,16},{32,40},{40,32},{48,56},{56,48},{64,72... | collective-permute-start | bytes 56 | tf_op jit(solution)/shard_map/ppermute | solution.py:296
  25.0 2.4 %copy-start.1 = (bf16[2944,256]{1,0:T(8,128)(2,1)}, bf16[2944,256]{1,0:T(8,128)(2,1)S(1)}, u32[]{:S(2)}) copy-start(bf16[2944,256]{1,0:T(8,128)(2,1)S(1)} %collective-permute-done.3.p_ref) | copy-start | bytes 4521988
  27.4 27.8 %collective-permute-start.7 = (bf16[1472,256]{1,0:T(8,128)(2,1)}, bf16[1472,256]{1,0:T(8,128)(2,1)}, u32[]{:S(2)}, u32[]{:S(2)}) collective-permute-start(bf16[1472,256]{1,0:T(8,128)(2,1)} %get-tuple-element.29), channel_id=1, source_target_pairs={{0,752},{8,760},{16,0},{24,8},{32,16},{40,24},{48,32},{56,40},{64,... | collective-permute-start | bytes 2261000 | tf_op jit(solution)/shard_map/ppermute | solution.py:293
  31.3 23.9 %collective-permute-start.8 = (bf16[1472,256]{1,0:T(8,128)(2,1)}, bf16[1472,256]{1,0:T(8,128)(2,1)}, u32[]{:S(2)}, u32[]{:S(2)}) collective-permute-start(bf16[1472,256]{1,0:T(8,128)(2,1)} %get-tuple-element.30), channel_id=1, source_target_pairs={{0,16},{8,24},{16,32},{24,40},{32,48},{40,56},{48,64},{56,72},{64,... | collective-permute-start | bytes 2261000 | tf_op jit(solution)/shard_map/ppermute | solution.py:293
  40.5 0.8 copy-start.3
  41.3 23.7 %all-to-all-start = ((bf16[8,144,256]{2,1,0:T(8,128)(2,1)}), bf16[8,144,256]{2,1,0:T(8,128)(2,1)}, u32[]{:S(2)}, u32[]{:S(2)}) async-start(bf16[8,144,256]{2,1,0:T(8,128)(2,1)} %copy-done.3), calls=%async_computation | async-start | bytes 1179648 | tf_op jit(solution)/shard_map/all_to_all | solution.py:336
  51.0 36.8 %copy-start.6 = (s32[96]{0:T(128)S(1)}, s32[96]{0:T(128)}, u32[]{:S(2)}) copy-start(s32[96]{0:T(128)} %refs_0_.1) | copy-start | bytes 1156
  58.0 54.5 %collective-permute-start.9 = (bf16[2944,256]{1,0:T(8,128)(2,1)}, bf16[2944,256]{1,0:T(8,128)(2,1)}, u32[]{:S(2)}, u32[]{:S(2)}) collective-permute-start(bf16[2944,256]{1,0:T(8,128)(2,1)} %maximum_select_fusion), channel_id=1, source_target_pairs={{0,8},{8,0},{16,24},{24,16},{32,40},{40,32},{48,56},{56,48},{64,72... | collective-permute-start | bytes 4521992 | tf_op jit(solution)/shard_map/ppermute | solution.py:296
  65.0 47.6 %copy-start.2 = (bf16[2944,256]{1,0:T(8,128)(2,1)S(1)}, bf16[2944,256]{1,0:T(8,128)(2,1)}, u32[]{:S(2)}) copy-start(bf16[2944,256]{1,0:T(8,128)(2,1)} %copy-done.1) | copy-start | bytes 4521988
  66.3 18.5 %collective-permute-start.4 = (bf16[80,256]{1,0:T(8,128)(2,1)S(1)}, bf16[80,256]{1,0:T(8,128)(2,1)S(1)}, u32[]{:S(2)}, u32[]{:S(2)}) collective-permute-start(bf16[80,256]{1,0:T(8,128)(2,1)S(1)} %get-tuple-element.26), channel_id=1, source_target_pairs={{0,752},{8,760},{16,0},{24,8},{32,16},{40,24},{48,32},{56,40},{64,... | collective-permute-start | bytes 122888 | tf_op jit(solution)/shard_map/ppermute | solution.py:293
  79.8 8.0 %collective-permute-start.5 = (bf16[80,256]{1,0:T(8,128)(2,1)S(1)}, bf16[80,256]{1,0:T(8,128)(2,1)S(1)}, u32[]{:S(2)}, u32[]{:S(2)}) collective-permute-start(bf16[80,256]{1,0:T(8,128)(2,1)S(1)} %get-tuple-element.27), channel_id=1, source_target_pairs={{0,16},{8,24},{16,32},{24,40},{32,48},{40,56},{48,64},{56,72},{64,... | collective-permute-start | bytes 122888 | tf_op jit(solution)/shard_map/ppermute | solution.py:293
  81.7 3.1 %collective-permute-start.6 = (bf16[48,256]{1,0:T(8,128)(2,1)S(1)}, bf16[48,256]{1,0:T(8,128)(2,1)S(1)}, u32[]{:S(2)}, u32[]{:S(2)}) collective-permute-start(bf16[48,256]{1,0:T(8,128)(2,1)S(1)} %get-tuple-element.28), channel_id=1, source_target_pairs={{0,8},{8,0},{16,24},{24,16},{32,40},{40,32},{48,56},{56,48},{64,72... | collective-permute-start | bytes 73736 | tf_op jit(solution)/shard_map/ppermute | solution.py:296

commit v7 on v5

v7 whole, which is shorter than its diff:
```python
import jax
import jax.numpy as jnp
from jax import lax
from jax.experimental import pallas as pl
from jax.experimental.pallas import tpu as pltpu
from jax.sharding import PartitionSpec as P


BF = jnp.bfloat16
F32 = jnp.float32
VM = pl.BlockSpec(memory_space=pltpu.VMEM)
SM = pl.BlockSpec(memory_space=pltpu.SMEM)
ANY = pl.BlockSpec(memory_space=pl.ANY)


def mm(a, b):
    return jnp.dot(a, b, preferred_element_type=F32)


def keep_rows(block, start, count):
    row = lax.broadcasted_iota(jnp.int32, block.shape, 0) + start
    return jnp.where(row < count, block, jnp.zeros((), block.dtype))


def place():
    r = lax.axis_index("blk")
    return r, lax.rem(r, 2), lax.axis_index("grp")


def at(count_ref, index):
    slabs = count_ref.shape[0]
    return count_ref[lax.rem(index + slabs, slabs)]


def three_terms(value):
    hi = value.astype(BF)
    rest = value - hi.astype(F32)
    mid = rest.astype(BF)
    low = (rest - mid.astype(F32)).astype(BF)
    return [hi.astype(F32), mid.astype(F32), low.astype(F32)]


def prep_kernel(
    aux_ref, energy_ref, other_ref, vir_ref, vir_rows_ref, own_ref, p_ref,
    ot_ref, pt_ref, near_ref, gaps_ref, head_ref,
):
    _, parity, g = place()
    cols = own_ref.shape[1]
    middle = cols // 2
    owners = near_ref.shape[0]
    piece = cols // owners
    part = piece // 2
    nv = vir_ref.shape[1]
    count = aux_ref[g]
    ot_ref[...] = keep_rows(own_ref[...], 0, count).T
    pt_ref[...] = keep_rows(p_ref[...], 0, count).T

    def put(rows_of, pair):
        near_ref[:, rows_of] = pair.reshape(owners, pair.shape[0] // owners, cols).astype(BF)

    put(slice(0, piece), mm(ot_ref[...], own_ref[...]))

    @pl.when(parity == 0)
    def _():
        put(slice(piece, piece + part), mm(ot_ref[:middle, :], p_ref[...]))

    @pl.when(parity == 1)
    def _():
        put(slice(piece, piece + part), mm(pt_ref[middle:, :], own_ref[...]))

    slots = cols // nv
    slot = (g * piece) // nv
    k = (g * part) // nv
    vir = jnp.concatenate([vir_ref[...]] * slots, axis=1)

    def spread(value):
        return jnp.broadcast_to(value, (1, cols))

    own_gap = levels(energy_ref, nv, cols) - vir
    other_gap = levels(other_ref, nv, cols) - vir
    own_level = spread(energy_ref[slot])
    own_parts = [energy_ref[k], energy_ref[k + slots // 2]]
    other_parts = [other_ref[k], other_ref[k + slots // 2]]
    even_parts = [jnp.where(parity == 0, a, b) for a, b in zip(own_parts, other_parts)]
    terms = []
    for row in [own_gap, other_gap, own_level] + [spread(value) for value in other_parts]:
        terms += three_terms(row)
    head_ref[...] = jnp.concatenate(terms + [jnp.zeros((1, cols), F32)], axis=0).astype(BF)
    gaps_ref[0:8, :] = jnp.concatenate(
        [own_gap, other_gap, own_level, vir] + [spread(value) for value in even_parts + own_parts], axis=0
    )
    start = pl.multiple_of(lax.rem(g * piece, nv), piece)
    gaps_ref[8:8 + piece, :] = vir_rows_ref[pl.ds(start, piece), :]
    start = pl.multiple_of(lax.rem(g * part, nv), part)
    gaps_ref[8 + piece:, :] = vir_rows_ref[pl.ds(start, part), :]


def levels(energy_ref, nv, cols):
    lane = lax.broadcasted_iota(jnp.int32, (1, cols), 1)
    level = jnp.zeros((1, cols), F32)
    for k in range(cols // nv):
        level = jnp.where(lane // nv == k, energy_ref[k], level)
    return level


def far_kernel(f_ref, ot_ref, pt_ref, near_ref, out_ref):
    _, parity, _ = place()
    owners, _, cols = out_ref.shape
    middle = cols // 2
    near = near_ref.shape[1]
    piece = cols // owners
    out_ref[:, 0:near] = near_ref[...]
    out_ref[:, near:near + piece] = mm(ot_ref[...], f_ref[...]).reshape(owners, piece, cols).astype(BF)

    def put(pair):
        out_ref[:, near + piece:] = pair.reshape(owners, piece // 2, cols).astype(BF)

    @pl.when(parity == 0)
    def _():
        put(mm(pt_ref[:middle, :], f_ref[...]))

    @pl.when(parity == 1)
    def _():
        put(mm(pt_ref[...], f_ref[:, middle:]).T)


def pack_kernel(parts_ref, head_ref, sum_ref, message_ref, swap_ref):
    total = jnp.sum(parts_ref[...].astype(F32), axis=0)
    size = parts_ref.shape[2] // parts_ref.shape[0]
    part = size // 2
    near = size + part
    across = total[near + size:].astype(BF)
    sum_ref[...] = total[:near + size]
    message_ref[0:size, :] = total[near:near + size].astype(BF)
    message_ref[size:near, :] = across
    message_ref[near:, :] = head_ref[...]
    swap_ref[0:part, :] = across
    swap_ref[part:, :] = total[size:near].astype(BF)


def amplitude_kernel(nv, count_ref, energy_ref, sum_ref, gaps_ref, message_ref, swap_ref, out_ref):
    r, parity, g = place()
    owners, _, size, cols = out_ref.shape
    part = size // 2
    near = size + part
    slot = (g * size) // nv
    sign = 1 - 2 * parity
    vir = gaps_ref[8:8 + size, :]
    vir_part = gaps_ref[8 + size:, :]
    own_gap = gaps_ref[0:1, :]
    own_rows = gaps_ref[2:3, :] - vir
    own_count, p_count = count_ref[r], count_ref[r + sign]
    f_count, s_count, x_count = at(count_ref, r + 2 * sign), at(count_ref, r - 2 * sign), at(count_ref, r - sign)
    lane = lax.broadcasted_iota(jnp.int32, (size, cols), 1)

    def head(row):
        block = message_ref[near:, :].astype(F32)
        return block[3 * row:3 * row + 1] + block[3 * row + 1:3 * row + 2] + block[3 * row + 2:3 * row + 3]

    def put(j, rows, pair, gap_rows, gap_cols, row_live, col_count):
        keep = (lane[:pair.shape[0]] < col_count * nv) & row_live
        amp = jnp.where(keep, pair / (gap_rows + gap_cols), 0.0).astype(BF)
        for owner in range(owners):
            out_ref[owner, j, rows] = amp

    every = slice(0, size)
    put(0, every, sum_ref[0:size, :], own_rows, own_gap, slot < own_count, own_count)
    f_gap = levels(energy_ref, nv, cols) - gaps_ref[3:4, :]
    put(2, every, sum_ref[near:, :], own_rows, f_gap, slot < own_count, f_count)
    put(3, every, message_ref[0:size, :].astype(F32), head(2) - vir, own_gap, slot < s_count, own_count)

    even = parity == 0
    even_count, odd_count = jnp.where(even, own_count, p_count), jnp.where(even, p_count, own_count)
    odd_gap = jnp.where(even, gaps_ref[1:2, :], own_gap)
    row_count, col_count = jnp.where(even, x_count, own_count), jnp.where(even, own_count, x_count)
    col_gap = jnp.where(even, own_gap, head(1))
    for h in range(2):
        k = (g * part) // nv + h * (cols // nv // 2)
        rows = slice(h * part, (h + 1) * part)
        pair = jnp.where(parity == h, sum_ref[size:near, :], swap_ref[part:, :].astype(F32))
        put(1, rows, pair, gaps_ref[4 + h:5 + h, :] - vir_part, odd_gap, k < even_count, odd_count)
        pair = jnp.where(parity == h, message_ref[size:near, :].astype(F32), swap_ref[0:part, :].astype(F32))
        level = jnp.where(even, head(3 + h), gaps_ref[6 + h:7 + h, :])
        put(4, rows, pair, level - vir_part, col_gap, k < row_count, col_count)


def gamma_kernel(aux_ref, amps_ref, o_ref, p_ref, f_ref, s_ref, x_ref, out_ref, result, weights, sems):
    rows, cols = o_ref.shape
    _, parity, g = place()

    def put(j, matrix):
        weights[j * cols:(j + 1) * cols, :] = matrix

    def whole(j):
        return amps_ref[:, j].reshape(cols, cols)

    def halves(j):
        part = amps_ref.shape[2] // 2
        return jnp.concatenate(
            [amps_ref[:, j, h * part:(h + 1) * part].reshape(cols // 2, cols) for h in range(2)], axis=0
        )

    put(0, whole(0))
    put(2, whole(2).T)
    put(3, whole(3))

    @pl.when(parity == 0)
    def _():
        put(1, halves(1).T)
        put(4, halves(4))

    @pl.when(parity == 1)
    def _():
        put(1, halves(1))
        put(4, halves(4).T)

    tile = rows // sems.shape[0]
    copies = []
    for j in range(sems.shape[0]):
        here = pl.ds(j * tile, tile)
        blocks = jnp.concatenate([ref[here, :] for ref in (o_ref, p_ref, f_ref, s_ref, x_ref)], axis=1)
        result[here, :] = keep_rows(mm(blocks, weights[...]), j * tile, aux_ref[g]).astype(result.dtype)
        copy = pltpu.make_async_copy(result.at[here, :], out_ref.at[here, :], sems.at[j])
        copy.start()
        copies.append(copy)
    for copy in copies:
        copy.wait()


def cost(flops, size):
    return pl.CostEstimate(flops=flops, bytes_accessed=size, transcendentals=0)


def memory(mebibytes):
    return pltpu.CompilerParams(vmem_limit_bytes=mebibytes << 20)


def per_device(three_index, occ_energy, vir_energy, aux_count, occ_count):
    rows, cols = three_index.shape
    nv = vir_energy.shape[0]
    slabs = lax.axis_size("blk")
    owners = lax.axis_size("grp")
    piece = cols // owners
    part = piece // 2

    def across(value, steps):
        pairs = [(i, (i + (steps if i % 2 == 0 else -steps)) % slabs) for i in range(slabs)]
        return lax.ppermute(value, "blk", pairs)

    def swap(value):
        return lax.ppermute(value, "blk", [(i, i ^ 1) for i in range(slabs)])

    def shape(*dims, dtype=BF):
        return jax.ShapeDtypeStruct(dims, dtype)

    own = three_index
    f_block = across(own, -2)
    partner = swap(own)
    partner_energy = swap(occ_energy)
    f_energy = across(occ_energy, -2)

    ot, pt, near, gaps, head = pl.pallas_call(
        prep_kernel,
        in_specs=[SM, SM, SM, VM, VM, VM, VM],
        out_specs=[VM] * 5,
        out_shape=[
            shape(cols, rows), shape(cols, rows), shape(owners, piece + part, cols),
            shape(8 + piece + part, cols, dtype=F32), shape(16, cols),
        ],
        cost_estimate=cost(3 * rows * cols * cols, 8 * rows * cols),
        compiler_params=memory(20),
        name="prep",
    )(
        aux_count, occ_energy, partner_energy, vir_energy[None, :],
        jnp.broadcast_to(vir_energy[:, None], (nv, cols)), own, partner,
    )
    own_later, near, f_energy = lax.optimization_barrier((own, near, f_energy))
    s_block = across(own_later, 2)
    parts = shape(owners, 3 * piece, cols)
    partial_sums = pl.pallas_call(
        far_kernel,
        in_specs=[VM] * 4,
        out_specs=VM,
        out_shape=parts,
        cost_estimate=cost(3 * rows * cols * cols, 5 * rows * cols),
        compiler_params=memory(12),
        name="far",
    )(f_block, ot, pt, near)
    pieces = lax.all_to_all(partial_sums, "grp", 0, 0)
    sums, message, extra = pl.pallas_call(
        pack_kernel,
        in_specs=[VM, VM],
        out_specs=[VM] * 3,
        out_shape=[
            shape(2 * piece + part, cols, dtype=F32), shape(piece + part + 16, cols), shape(piece, cols),
        ],
        cost_estimate=cost(cols * cols, 4 * cols * cols),
        compiler_params=memory(6),
        name="pack",
    )(pieces, head)
    fifth = swap(f_block)
    message, s_block, fifth = lax.optimization_barrier((message, s_block, fifth))
    message = across(message, 2)
    extra = swap(extra)
    amps = pl.pallas_call(
        lambda *refs: amplitude_kernel(nv, *refs),
        in_specs=[SM, SM] + [VM] * 4,
        out_specs=VM,
        out_shape=shape(owners, 5, piece, cols),
        cost_estimate=cost(cols * cols, 8 * cols * cols),
        compiler_params=memory(6),
        name="amplitude",
    )(occ_count, f_energy, sums, gaps, message, extra)
    amps = lax.all_to_all(amps, "grp", 0, 0)

    tiles = 8
    return pl.pallas_call(
        gamma_kernel,
        in_specs=[SM] + [VM] * 6,
        out_specs=ANY,
        out_shape=jax.ShapeDtypeStruct((rows, cols), three_index.dtype),
        scratch_shapes=[
            pltpu.VMEM((rows, cols), three_index.dtype), pltpu.VMEM((5 * cols, cols), BF),
            pltpu.SemaphoreType.DMA((tiles,)),
        ],
        cost_estimate=cost(10 * rows * cols * cols, 14 * rows * cols),
        compiler_params=memory(20),
        name="gamma",
    )(aux_count, amps, own, partner, f_block, s_block, fifth)


def solution(mesh):
    in_specs = (P("grp", "blk"), P("blk"), P(), P(), P())
    out_specs = P("grp", "blk")
    return jax.shard_map(
        per_device, mesh=mesh, in_specs=in_specs, out_specs=out_specs, check_vma=False
    )
```

time: 118 us -> 113 us (0.958)
  the two profiles are of different devices: /device:TPU:56 before, /device:TPU:8 now
where the time goes in v7:
time: 113 us; the launch traced here: 112 us
  blocking collectives  58.9 us (52%)
  starting transfers between devices  30.2 us (27%)
  waiting for transfers between devices  11.7 us (10%)
  Pallas kernels  8.88 us (8%)
  local copies, waits for them, and re-layouts  2.7 us (2%)
    all_to_all x1, blocking collectives, per_device(): pieces = lax.all_to_all(partial_sums, 'grp', 0, 0)  34.8 us
    all_to_all x1, blocking collectives, per_device(): amps = lax.all_to_all(amps, 'grp', 0, 0)  24.1 us
    ppermute x4, starting transfers between devices, across(): return lax.ppermute(value, 'blk', pairs)  20.8 us
    ppermute x4, waiting for transfers between devices, across(): return lax.ppermute(value, 'blk', pairs)  10.6 us
    ppermute x4, starting transfers between devices, swap(): return lax.ppermute(value, 'blk', [(i, i ^ 1) for i in range(slabs)])  9.39 us
    pallas_call x1, Pallas kernels, per_device(): pl.pallas_call(gamma_kernel, in_specs=[SM] + [VM] * 6, out_specs=ANY, out...  4.5 us
    pallas_call x1, Pallas kernels, per_device(): pl.pallas_call(prep_kernel, in_specs=[SM, SM, SM, VM, VM, VM, VM], out_sp...  2.74 us
  transfers between devices with their start and end apart: 8, of which 3 were waited for; matrix products, arithmetic and copies ran while one was open for 1% of the time, Pallas kernels for 3%

profile of v7, /device:TPU:8, one launch (start us, length us, event | category | flops | bytes accessed | tf_op | source)
XLA Modules:
  0.0 112.5 jit_solution(2201339699128102392)
XLA Ops:
  0.0 1.9 %collective-permute-start.1 = (bf16[2944,256]{1,0:T(8,128)(2,1)}, bf16[2944,256]{1,0:T(8,128)(2,1)S(1)}, u32[]{:S(2)}, u32[]{:S(2)}) collective-permute-start(bf16[2944,256]{1,0:T(8,128)(2,1)} %o_ref.1), channel_id=1, source_target_pairs={{0,8},{8,0},{16,24},{24,16},{32,40},{40,32},{48,56},{56,48},{64,72... | collective-permute-start | bytes 4521992 | tf_op jit(solution)/shard_map/ppermute | solution.py:251
  1.9 14.5 %collective-permute-start.3 = (bf16[2944,256]{1,0:T(8,128)(2,1)}, bf16[2944,256]{1,0:T(8,128)(2,1)S(1)}, u32[]{:S(2)}, u32[]{:S(2)}) collective-permute-start(bf16[2944,256]{1,0:T(8,128)(2,1)} %o_ref.1), channel_id=1, source_target_pairs={{0,752},{8,24},{16,0},{24,40},{32,16},{40,56},{48,32},{56,72},{64,... | collective-permute-start | bytes 4521992 | tf_op jit(solution)/shard_map/ppermute | solution.py:248
  16.4 1.9 %collective-permute-start = (f32[4]{0:T(128)}, f32[4]{0:T(128)S(1)}, u32[]{:S(2)}, u32[]{:S(2)}) collective-permute-start(f32[4]{0:T(128)} %energy_ref.1), channel_id=1, source_target_pairs={{0,8},{8,0},{16,24},{24,16},{32,40},{40,32},{48,56},{56,48},{64,72... | collective-permute-start | bytes 56 | tf_op jit(solution)/shard_map/ppermute | solution.py:251
  18.3 2.5 %collective-permute-start.2 = (f32[4]{0:T(128)}, f32[4]{0:T(128)S(1)}, u32[]{:S(2)}, u32[]{:S(2)}) collective-permute-start(f32[4]{0:T(128)} %energy_ref.1), channel_id=1, source_target_pairs={{0,752},{8,24},{16,0},{24,40},{32,16},{40,56},{48,32},{56,72},{64,... | collective-permute-start | bytes 56 | tf_op jit(solution)/shard_map/ppermute | solution.py:248
  20.8 0.0 collective-permute-done.other_ref
  20.8 0.0 collective-permute-done.1.p_ref
  20.8 0.7 broadcast_in_dim.10.vir_rows_ref
  21.6 0.0 copy-start
  21.6 0.7 copy-done
  22.2 0.0 copy-start.1
  22.2 0.7 copy-done.1
  22.9 0.0 copy-start.3
  22.9 0.7 copy-done.3
  23.5 2.7 %prep.1 = (bf16[256,2944]{1,0:T(8,128)(2,1)S(1)}, bf16[256,2944]{1,0:T(8,128)(2,1)S(1)}, bf16[8,48,256]{2,1,0:T(8,128)(2,1)S(1)}, f32[56,256]{1,0:T(8,128)S(1)}, bf16[16,256]{1,0:T(8,128)(2,1)S(1)}) custom-call(s32[8]{0:T(128)S(1)} %copy-done.1, f32[4]{0:T(128)S(1)} %copy-done.3, f32[4]{0:T(128)S(1)} %collective-permute-done.other_ref, f32[1,64]{1,0:T(1,128)S(1)} %bitcast.1, ...), custom_call_target="tpu_custom_call" | custom-call | flops 578813952 | bytes 6029312 | tf_op jit(solution)/shard_map/prep/pallas_call | solution.py:262
  26.3 7.7 %collective-permute-done.2.refs_1_ = f32[4]{0:T(128)S(1)} collective-permute-done((f32[4]{0:T(128)}, f32[4]{0:T(128)S(1)}, u32[]{:S(2)}, u32[]{:S(2)}) %collective-permute-start.2) | collective-permute-done | bytes 48 | tf_op jit(solution)/shard_map/ppermute | solution.py:248
  33.9 1.9 %collective-permute-start.4 = (bf16[2944,256]{1,0:T(8,128)(2,1)}, bf16[2944,256]{1,0:T(8,128)(2,1)S(1)}, u32[]{:S(2)}, u32[]{:S(2)}) collective-permute-start(bf16[2944,256]{1,0:T(8,128)(2,1)} %o_ref.1), channel_id=1, source_target_pairs={{0,16},{8,760},{16,32},{24,8},{32,48},{40,24},{48,64},{56,40},{64,... | collective-permute-start | bytes 4521992 | tf_op jit(solution)/shard_map/ppermute | solution.py:248
  35.8 0.0 collective-permute-done.3.f_ref
  35.9 3.6 %collective-permute-start.5 = (bf16[2944,256]{1,0:T(8,128)(2,1)S(1)}, bf16[2944,256]{1,0:T(8,128)(2,1)S(1)}, u32[]{:S(2)}, u32[]{:S(2)}) collective-permute-start(bf16[2944,256]{1,0:T(8,128)(2,1)S(1)} %collective-permute-done.3.f_ref), channel_id=1, source_target_pairs={{0,8},{8,0},{16,24},{24,16},{32,40},{40,32},{48,56},{56,48},{64,72... | collective-permute-start | bytes 4521992 | tf_op jit(solution)/shard_map/ppermute | solution.py:251
  39.5 0.0 copy-start.2
  39.5 1.0 far.1
  40.5 34.8 %all_to_all.10.parts_ref = bf16[8,96,256]{2,1,0:T(8,128)(2,1)S(1)} all-to-all(bf16[8,96,256]{2,1,0:T(8,128)(2,1)S(1)} %far.1), channel_id=1, replica_groups=mesh['blk'=96,'grp'=8] {'grp'}, dimensions={0} | all-to-all | bytes 786432 | tf_op jit(solution)/shard_map/all_to_all | solution.py:289
  75.3 0.1 pack.1
  75.3 0.0 collective-permute-done.4.s_ref
  75.3 0.0 collective-permute-done.5.x_ref
  75.3 1.9 %collective-permute-start.6 = (bf16[64,256]{1,0:T(8,128)(2,1)S(1)}, bf16[64,256]{1,0:T(8,128)(2,1)S(1)}, u32[]{:S(2)}, u32[]{:S(2)}) collective-permute-start(bf16[64,256]{1,0:T(8,128)(2,1)S(1)} %get-tuple-element.29), channel_id=1, source_target_pairs={{0,16},{8,760},{16,32},{24,8},{32,48},{40,24},{48,64},{56,40},{64,... | collective-permute-start | bytes 98312 | tf_op jit(solution)/shard_map/ppermute | solution.py:248
  77.3 1.9 %collective-permute-start.7 = (bf16[32,256]{1,0:T(8,128)(2,1)S(1)}, bf16[32,256]{1,0:T(8,128)(2,1)S(1)}, u32[]{:S(2)}, u32[]{:S(2)}) collective-permute-start(bf16[32,256]{1,0:T(8,128)(2,1)S(1)} %get-tuple-element.30), channel_id=1, source_target_pairs={{0,8},{8,0},{16,24},{24,16},{32,40},{40,32},{48,56},{56,48},{64,72... | collective-permute-start | bytes 49160 | tf_op jit(solution)/shard_map/ppermute | solution.py:251
  79.2 1.1 %collective-permute-done.7.refs_5_ = bf16[32,256]{1,0:T(8,128)(2,1)S(1)} collective-permute-done((bf16[32,256]{1,0:T(8,128)(2,1)S(1)}, bf16[32,256]{1,0:T(8,128)(2,1)S(1)}, u32[]{:S(2)}, u32[]{:S(2)}) %collective-permute-start.7) | collective-permute-done | bytes 16416 | tf_op jit(solution)/shard_map/ppermute | solution.py:251
  80.3 2.9 %collective-permute-done.6.refs_4_ = bf16[64,256]{1,0:T(8,128)(2,1)S(1)} collective-permute-done((bf16[64,256]{1,0:T(8,128)(2,1)S(1)}, bf16[64,256]{1,0:T(8,128)(2,1)S(1)}, u32[]{:S(2)}, u32[]{:S(2)}) %collective-permute-start.6) | collective-permute-done | bytes 32800 | tf_op jit(solution)/shard_map/ppermute | solution.py:248
  83.3 0.0 copy-done.2
  83.3 0.6 amplitude.1
  83.9 24.1 %all_to_all.11.amps_ref = bf16[8,5,32,256]{3,2,1,0:T(8,128)(2,1)S(1)} all-to-all(bf16[8,5,32,256]{3,2,1,0:T(8,128)(2,1)S(1)} %amplitude.1), channel_id=1, replica_groups=mesh['blk'=96,'grp'=8] {'grp'}, dimensions={0} | all-to-all | bytes 1310720 | tf_op jit(solution)/shard_map/all_to_all | solution.py:314
  108.0 4.5 %gamma.1 = bf16[2944,256]{1,0:T(8,128)(2,1)} custom-call(s32[8]{0:T(128)S(1)} %copy-done.1, bf16[8,5,32,256]{3,2,1,0:T(8,128)(2,1)S(1)} %all_to_all.11.amps_ref, bf16[2944,256]{1,0:T(8,128)(2,1)} %o_ref.1, bf16[2944,256]{1,0:T(8,128)(2,1)S(1)} %collective-permute-done.1.p_ref, bf16[2944,256]{1,0:T(8,128)(2,1)S(1)} %collective-permute-done.3.f_ref, ...), custom_call_target="tpu_custom_call" | custom-call | flops 1929379840 | bytes 10551296 | tf_op jit(solution)/shard_map/gamma/pallas_call | solution.py:317
Async XLA Ops:
  0.0 20.8 %collective-permute-start.1 = (bf16[2944,256]{1,0:T(8,128)(2,1)}, bf16[2944,256]{1,0:T(8,128)(2,1)S(1)}, u32[]{:S(2)}, u32[]{:S(2)}) collective-permute-start(bf16[2944,256]{1,0:T(8,128)(2,1)} %o_ref.1), channel_id=1, source_target_pairs={{0,8},{8,0},{16,24},{24,16},{32,40},{40,32},{48,56},{56,48},{64,72... | collective-permute-start | bytes 4521992 | tf_op jit(solution)/shard_map/ppermute | solution.py:251
  1.9 33.9 %collective-permute-start.3 = (bf16[2944,256]{1,0:T(8,128)(2,1)}, bf16[2944,256]{1,0:T(8,128)(2,1)S(1)}, u32[]{:S(2)}, u32[]{:S(2)}) collective-permute-start(bf16[2944,256]{1,0:T(8,128)(2,1)} %o_ref.1), channel_id=1, source_target_pairs={{0,752},{8,24},{16,0},{24,40},{32,16},{40,56},{48,32},{56,72},{64,... | collective-permute-start | bytes 4521992 | tf_op jit(solution)/shard_map/ppermute | solution.py:248
  16.4 4.4 %collective-permute-start = (f32[4]{0:T(128)}, f32[4]{0:T(128)S(1)}, u32[]{:S(2)}, u32[]{:S(2)}) collective-permute-start(f32[4]{0:T(128)} %energy_ref.1), channel_id=1, source_target_pairs={{0,8},{8,0},{16,24},{24,16},{32,40},{40,32},{48,56},{56,48},{64,72... | collective-permute-start | bytes 56 | tf_op jit(solution)/shard_map/ppermute | solution.py:251
  18.3 15.6 %collective-permute-start.2 = (f32[4]{0:T(128)}, f32[4]{0:T(128)S(1)}, u32[]{:S(2)}, u32[]{:S(2)}) collective-permute-start(f32[4]{0:T(128)} %energy_ref.1), channel_id=1, source_target_pairs={{0,752},{8,24},{16,0},{24,40},{32,16},{40,56},{48,32},{56,72},{64,... | collective-permute-start | bytes 56 | tf_op jit(solution)/shard_map/ppermute | solution.py:248
  21.6 0.7 copy-start
  22.2 0.7 copy-start.1
  22.9 0.7 copy-start.3
  33.9 41.4 %collective-permute-start.4 = (bf16[2944,256]{1,0:T(8,128)(2,1)}, bf16[2944,256]{1,0:T(8,128)(2,1)S(1)}, u32[]{:S(2)}, u32[]{:S(2)}) collective-permute-start(bf16[2944,256]{1,0:T(8,128)(2,1)} %o_ref.1), channel_id=1, source_target_pairs={{0,16},{8,760},{16,32},{24,8},{32,48},{40,24},{48,64},{56,40},{64,... | collective-permute-start | bytes 4521992 | tf_op jit(solution)/shard_map/ppermute | solution.py:248
  35.9 39.5 %collective-permute-start.5 = (bf16[2944,256]{1,0:T(8,128)(2,1)S(1)}, bf16[2944,256]{1,0:T(8,128)(2,1)S(1)}, u32[]{:S(2)}, u32[]{:S(2)}) collective-permute-start(bf16[2944,256]{1,0:T(8,128)(2,1)S(1)} %collective-permute-done.3.f_ref), channel_id=1, source_target_pairs={{0,8},{8,0},{16,24},{24,16},{32,40},{40,32},{48,56},{56,48},{64,72... | collective-permute-start | bytes 4521992 | tf_op jit(solution)/shard_map/ppermute | solution.py:251
  39.5 43.8 %copy-start.2 = (s32[96]{0:T(128)S(1)}, s32[96]{0:T(128)}, u32[]{:S(2)}) copy-start(s32[96]{0:T(128)} %refs_0_.1) | copy-start | bytes 1156
  75.3 7.9 %collective-permute-start.6 = (bf16[64,256]{1,0:T(8,128)(2,1)S(1)}, bf16[64,256]{1,0:T(8,128)(2,1)S(1)}, u32[]{:S(2)}, u32[]{:S(2)}) collective-permute-start(bf16[64,256]{1,0:T(8,128)(2,1)S(1)} %get-tuple-element.29), channel_id=1, source_target_pairs={{0,16},{8,760},{16,32},{24,8},{32,48},{40,24},{48,64},{56,40},{64,... | collective-permute-start | bytes 98312 | tf_op jit(solution)/shard_map/ppermute | solution.py:248
  77.3 3.1 %collective-permute-start.7 = (bf16[32,256]{1,0:T(8,128)(2,1)S(1)}, bf16[32,256]{1,0:T(8,128)(2,1)S(1)}, u32[]{:S(2)}, u32[]{:S(2)}) collective-permute-start(bf16[32,256]{1,0:T(8,128)(2,1)S(1)} %get-tuple-element.30), channel_id=1, source_target_pairs={{0,8},{8,0},{16,24},{24,16},{32,40},{40,32},{48,56},{56,48},{64,72... | collective-permute-start | bytes 49160 | tf_op jit(solution)/shard_map/ppermute | solution.py:251

commit v8 on v7

--- a/solution.py
+++ b/solution.py
@@ -257,7 +257,6 @@
     f_block = across(own, -2)
     partner = swap(own)
     partner_energy = swap(occ_energy)
-    f_energy = across(occ_energy, -2)
 
     ot, pt, near, gaps, head = pl.pallas_call(
         prep_kernel,
@@ -274,7 +273,7 @@
         aux_count, occ_energy, partner_energy, vir_energy[None, :],
         jnp.broadcast_to(vir_energy[:, None], (nv, cols)), own, partner,
     )
-    own_later, near, f_energy = lax.optimization_barrier((own, near, f_energy))
+    own_later, near = lax.optimization_barrier((own, near))
     s_block = across(own_later, 2)
     parts = shape(owners, 3 * piece, cols)
     partial_sums = pl.pallas_call(
@@ -287,6 +286,7 @@
         name="far",
     )(f_block, ot, pt, near)
     pieces = lax.all_to_all(partial_sums, "grp", 0, 0)
+    pieces, s_block = lax.optimization_barrier((pieces, s_block))
     sums, message, extra = pl.pallas_call(
         pack_kernel,
         in_specs=[VM, VM],
@@ -298,8 +298,9 @@
         compiler_params=memory(6),
         name="pack",
     )(pieces, head)
+    message, energy = lax.optimization_barrier((message, occ_energy))
+    f_energy = across(energy, -2)
     fifth = swap(f_block)
-    message, s_block, fifth = lax.optimization_barrier((message, s_block, fifth))
     message = across(message, 2)
     extra = swap(extra)
     amps = pl.pallas_call(
@@ -311,6 +312,7 @@
         compiler_params=memory(6),
         name="amplitude",
     )(occ_count, f_energy, sums, gaps, message, extra)
+    amps, fifth = lax.optimization_barrier((amps, fifth))
     amps = lax.all_to_all(amps, "grp", 0, 0)
 
     tiles = 8

time: 113 us -> 113 us (level)
  the two profiles are of different devices: /device:TPU:8 before, /device:TPU:1 now
where the time goes in v8:
time: 113 us
  starting transfers between devices  47.1 us (42%)
  blocking collectives  39.8 us (35%)
  waiting for transfers between devices  13.7 us (12%)
  Pallas kernels  9.17 us (8%)
  local copies, waits for them, and re-layouts  2.7 us (2%)
    ppermute x4, starting transfers between devices, swap(): return lax.ppermute(value, 'blk', [(i, i ^ 1) for i in range(slabs)])  31.1 us
    all_to_all x1, blocking collectives, per_device(): amps = lax.all_to_all(amps, 'grp', 0, 0)  21.1 us
    all_to_all x1, blocking collectives, per_device(): pieces = lax.all_to_all(partial_sums, 'grp', 0, 0)  18.7 us
    ppermute x4, starting transfers between devices, across(): return lax.ppermute(value, 'blk', pairs)  16 us
    ppermute x4, waiting for transfers between devices, across(): return lax.ppermute(value, 'blk', pairs)  12.8 us
    pallas_call x1, Pallas kernels, per_device(): pl.pallas_call(gamma_kernel, in_specs=[SM] + [VM] * 6, out_specs=ANY, out...  4.52 us
    pallas_call x1, Pallas kernels, per_device(): pl.pallas_call(prep_kernel, in_specs=[SM, SM, SM, VM, VM, VM, VM], out_sp...  2.77 us
  transfers between devices with their start and end apart: 8, of which 3 were waited for; matrix products, arithmetic and copies ran while one was open for 1% of the time, Pallas kernels for 4%

profile of v8, /device:TPU:1, one launch (start us, length us, event | category | flops | bytes accessed | tf_op | source)
XLA Modules:
  0.0 112.6 jit_solution(12792379282362546699)
XLA Ops:
  0.0 12.4 %collective-permute-start.2 = (bf16[2944,256]{1,0:T(8,128)(2,1)}, bf16[2944,256]{1,0:T(8,128)(2,1)S(1)}, u32[]{:S(2)}, u32[]{:S(2)}) collective-permute-start(bf16[2944,256]{1,0:T(8,128)(2,1)} %o_ref.1), channel_id=1, source_target_pairs={{0,8},{8,0},{16,24},{24,16},{32,40},{40,32},{48,56},{56,48},{64,72... | collective-permute-start | bytes 4521992 | tf_op jit(solution)/shard_map/ppermute | solution.py:251
  12.4 1.9 %collective-permute-start = (bf16[2944,256]{1,0:T(8,128)(2,1)}, bf16[2944,256]{1,0:T(8,128)(2,1)S(1)}, u32[]{:S(2)}, u32[]{:S(2)}) collective-permute-start(bf16[2944,256]{1,0:T(8,128)(2,1)} %o_ref.1), channel_id=1, source_target_pairs={{0,752},{8,24},{16,0},{24,40},{32,16},{40,56},{48,32},{56,72},{64,... | collective-permute-start | bytes 4521992 | tf_op jit(solution)/shard_map/ppermute | solution.py:248
  14.4 8.6 %collective-permute-start.1 = (f32[4]{0:T(128)}, f32[4]{0:T(128)S(1)}, u32[]{:S(2)}, u32[]{:S(2)}) collective-permute-start(f32[4]{0:T(128)} %energy_ref.1), channel_id=1, source_target_pairs={{0,8},{8,0},{16,24},{24,16},{32,40},{40,32},{48,56},{56,48},{64,72... | collective-permute-start | bytes 56 | tf_op jit(solution)/shard_map/ppermute | solution.py:251
  23.0 0.9 collective-permute-done.1.other_ref
  23.9 0.0 collective-permute-done.2.p_ref
  23.9 0.7 broadcast_in_dim.10.vir_rows_ref
  24.6 0.0 copy-start
  24.6 0.7 copy-done
  25.3 0.0 copy-start.1
  25.3 0.7 copy-done.1
  26.0 0.0 copy-start.3
  26.0 0.7 copy-done.3
  26.6 2.8 %prep.1 = (bf16[256,2944]{1,0:T(8,128)(2,1)S(1)}, bf16[256,2944]{1,0:T(8,128)(2,1)S(1)}, bf16[8,48,256]{2,1,0:T(8,128)(2,1)S(1)}, f32[56,256]{1,0:T(8,128)S(1)}, bf16[16,256]{1,0:T(8,128)(2,1)S(1)}) custom-call(s32[8]{0:T(128)S(1)} %copy-done.1, f32[4]{0:T(128)S(1)} %copy-done.3, f32[4]{0:T(128)S(1)} %collective-permute-done.1.other_ref, ...), custom_call_target="tpu_custom_call" | custom-call | flops 578813952 | bytes 6029312 | tf_op jit(solution)/shard_map/prep/pallas_call | solution.py:261
  29.4 2.2 %collective-permute-start.3 = (bf16[2944,256]{1,0:T(8,128)(2,1)}, bf16[2944,256]{1,0:T(8,128)(2,1)S(1)}, u32[]{:S(2)}, u32[]{:S(2)}) collective-permute-start(bf16[2944,256]{1,0:T(8,128)(2,1)} %o_ref.1), channel_id=1, source_target_pairs={{0,16},{8,760},{16,32},{24,8},{32,48},{40,24},{48,64},{56,40},{64,... | collective-permute-start | bytes 4521992 | tf_op jit(solution)/shard_map/ppermute | solution.py:248
  31.6 6.5 %collective-permute-done.f_ref = bf16[2944,256]{1,0:T(8,128)(2,1)S(1)} collective-permute-done((bf16[2944,256]{1,0:T(8,128)(2,1)}, bf16[2944,256]{1,0:T(8,128)(2,1)S(1)}, u32[]{:S(2)}, u32[]{:S(2)}) %collective-permute-start) | collective-permute-done | bytes 1507360 | tf_op jit(solution)/shard_map/ppermute | solution.py:248
  38.1 8.2 %collective-permute-start.7 = (bf16[2944,256]{1,0:T(8,128)(2,1)S(1)}, bf16[2944,256]{1,0:T(8,128)(2,1)S(1)}, u32[]{:S(2)}, u32[]{:S(2)}) collective-permute-start(bf16[2944,256]{1,0:T(8,128)(2,1)S(1)} %collective-permute-done.f_ref), channel_id=1, source_target_pairs={{0,8},{8,0},{16,24},{24,16},{32,40},{40,32},{48,56},{56,48},{64,72... | collective-permute-start | bytes 4521992 | tf_op jit(solution)/shard_map/ppermute | solution.py:251
  46.2 0.0 copy-start.2
  46.2 1.2 %far.1 = bf16[8,96,256]{2,1,0:T(8,128)(2,1)S(1)} custom-call(bf16[2944,256]{1,0:T(8,128)(2,1)S(1)} %collective-permute-done.f_ref, bf16[256,2944]{1,0:T(8,128)(2,1)S(1)} %get-tuple-element.21.ot_ref, bf16[256,2944]{1,0:T(8,128)(2,1)S(1)} %get-tuple-element.22.pt_ref, bf16[8,48,256]{2,1,0:T(8,128)(2,1)S(1)} %get-tuple-element.24.near_ref), custom_call_target="tpu_custom_call" | custom-call | flops 578813952 | bytes 3768320 | tf_op jit(solution)/shard_map/far/pallas_call | solution.py:279
  47.5 18.7 %all_to_all.10.parts_ref = bf16[8,96,256]{2,1,0:T(8,128)(2,1)S(1)} all-to-all(bf16[8,96,256]{2,1,0:T(8,128)(2,1)S(1)} %far.1), channel_id=1, replica_groups=mesh['blk'=96,'grp'=8] {'grp'}, dimensions={0} | all-to-all | bytes 786432 | tf_op jit(solution)/shard_map/all_to_all | solution.py:288
  66.2 0.0 collective-permute-done.3.s_ref
  66.2 0.1 pack.1
  66.2 10.0 %collective-permute-start.5 = (bf16[64,256]{1,0:T(8,128)(2,1)S(1)}, bf16[64,256]{1,0:T(8,128)(2,1)S(1)}, u32[]{:S(2)}, u32[]{:S(2)}) collective-permute-start(bf16[64,256]{1,0:T(8,128)(2,1)S(1)} %get-tuple-element.32), channel_id=1, source_target_pairs={{0,16},{8,760},{16,32},{24,8},{32,48},{40,24},{48,64},{56,40},{64,... | collective-permute-start | bytes 98312 | tf_op jit(solution)/shard_map/ppermute | solution.py:248
  76.2 1.9 %collective-permute-start.6 = (bf16[32,256]{1,0:T(8,128)(2,1)S(1)}, bf16[32,256]{1,0:T(8,128)(2,1)S(1)}, u32[]{:S(2)}, u32[]{:S(2)}) collective-permute-start(bf16[32,256]{1,0:T(8,128)(2,1)S(1)} %get-tuple-element.33), channel_id=1, source_target_pairs={{0,8},{8,0},{16,24},{24,16},{32,40},{40,32},{48,56},{56,48},{64,72... | collective-permute-start | bytes 49160 | tf_op jit(solution)/shard_map/ppermute | solution.py:251
  78.2 1.9 %collective-permute-start.4 = (f32[4]{0:T(128)S(1)}, f32[4]{0:T(128)S(1)}, u32[]{:S(2)}, u32[]{:S(2)}) collective-permute-start(f32[4]{0:T(128)S(1)} %copy-done.3), channel_id=1, source_target_pairs={{0,752},{8,24},{16,0},{24,40},{32,16},{40,56},{48,32},{56,72},{64,... | collective-permute-start | bytes 56 | tf_op jit(solution)/shard_map/ppermute | solution.py:248
  80.1 6.3 %collective-permute-done.4.refs_1_ = f32[4]{0:T(128)S(1)} collective-permute-done((f32[4]{0:T(128)S(1)}, f32[4]{0:T(128)S(1)}, u32[]{:S(2)}, u32[]{:S(2)}) %collective-permute-start.4) | collective-permute-done | bytes 48 | tf_op jit(solution)/shard_map/ppermute | solution.py:248
  86.3 0.0 collective-permute-done.6.refs_5_
  86.3 0.0 collective-permute-done.5.refs_4_
  86.4 0.0 copy-done.2
  86.4 0.6 amplitude.1
  87.0 0.0 collective-permute-done.7.x_ref
  87.0 21.1 %all_to_all.11.amps_ref = bf16[8,5,32,256]{3,2,1,0:T(8,128)(2,1)S(1)} all-to-all(bf16[8,5,32,256]{3,2,1,0:T(8,128)(2,1)S(1)} %amplitude.1), channel_id=1, replica_groups=mesh['blk'=96,'grp'=8] {'grp'}, dimensions={0} | all-to-all | bytes 1310720 | tf_op jit(solution)/shard_map/all_to_all | solution.py:316
  108.1 4.5 %gamma.1 = bf16[2944,256]{1,0:T(8,128)(2,1)} custom-call(s32[8]{0:T(128)S(1)} %copy-done.1, bf16[8,5,32,256]{3,2,1,0:T(8,128)(2,1)S(1)} %all_to_all.11.amps_ref, bf16[2944,256]{1,0:T(8,128)(2,1)} %o_ref.1, bf16[2944,256]{1,0:T(8,128)(2,1)S(1)} %collective-permute-done.2.p_ref, bf16[2944,256]{1,0:T(8,128)(2,1)S(1)} %collective-permute-done.f_ref, ...), custom_call_target="tpu_custom_call" | custom-call | flops 1929379840 | bytes 10551296 | tf_op jit(solution)/shard_map/gamma/pallas_call | solution.py:319
Async XLA Ops:
  0.0 23.9 %collective-permute-start.2 = (bf16[2944,256]{1,0:T(8,128)(2,1)}, bf16[2944,256]{1,0:T(8,128)(2,1)S(1)}, u32[]{:S(2)}, u32[]{:S(2)}) collective-permute-start(bf16[2944,256]{1,0:T(8,128)(2,1)} %o_ref.1), channel_id=1, source_target_pairs={{0,8},{8,0},{16,24},{24,16},{32,40},{40,32},{48,56},{56,48},{64,72... | collective-permute-start | bytes 4521992 | tf_op jit(solution)/shard_map/ppermute | solution.py:251
  12.4 25.6 %collective-permute-start = (bf16[2944,256]{1,0:T(8,128)(2,1)}, bf16[2944,256]{1,0:T(8,128)(2,1)S(1)}, u32[]{:S(2)}, u32[]{:S(2)}) collective-permute-start(bf16[2944,256]{1,0:T(8,128)(2,1)} %o_ref.1), channel_id=1, source_target_pairs={{0,752},{8,24},{16,0},{24,40},{32,16},{40,56},{48,32},{56,72},{64,... | collective-permute-start | bytes 4521992 | tf_op jit(solution)/shard_map/ppermute | solution.py:248
  14.4 9.6 %collective-permute-start.1 = (f32[4]{0:T(128)}, f32[4]{0:T(128)S(1)}, u32[]{:S(2)}, u32[]{:S(2)}) collective-permute-start(f32[4]{0:T(128)} %energy_ref.1), channel_id=1, source_target_pairs={{0,8},{8,0},{16,24},{24,16},{32,40},{40,32},{48,56},{56,48},{64,72... | collective-permute-start | bytes 56 | tf_op jit(solution)/shard_map/ppermute | solution.py:251
  24.6 0.7 copy-start
  25.3 0.7 copy-start.1
  26.0 0.7 copy-start.3
  29.4 36.8 %collective-permute-start.3 = (bf16[2944,256]{1,0:T(8,128)(2,1)}, bf16[2944,256]{1,0:T(8,128)(2,1)S(1)}, u32[]{:S(2)}, u32[]{:S(2)}) collective-permute-start(bf16[2944,256]{1,0:T(8,128)(2,1)} %o_ref.1), channel_id=1, source_target_pairs={{0,16},{8,760},{16,32},{24,8},{32,48},{40,24},{48,64},{56,40},{64,... | collective-permute-start | bytes 4521992 | tf_op jit(solution)/shard_map/ppermute | solution.py:248
  38.1 48.9 %collective-permute-start.7 = (bf16[2944,256]{1,0:T(8,128)(2,1)S(1)}, bf16[2944,256]{1,0:T(8,128)(2,1)S(1)}, u32[]{:S(2)}, u32[]{:S(2)}) collective-permute-start(bf16[2944,256]{1,0:T(8,128)(2,1)S(1)} %collective-permute-done.f_ref), channel_id=1, source_target_pairs={{0,8},{8,0},{16,24},{24,16},{32,40},{40,32},{48,56},{56,48},{64,72... | collective-permute-start | bytes 4521992 | tf_op jit(solution)/shard_map/ppermute | solution.py:251
  46.2 40.1 %copy-start.2 = (s32[96]{0:T(128)S(1)}, s32[96]{0:T(128)}, u32[]{:S(2)}) copy-start(s32[96]{0:T(128)} %refs_0_.1) | copy-start | bytes 1156
  66.2 20.1 %collective-permute-start.5 = (bf16[64,256]{1,0:T(8,128)(2,1)S(1)}, bf16[64,256]{1,0:T(8,128)(2,1)S(1)}, u32[]{:S(2)}, u32[]{:S(2)}) collective-permute-start(bf16[64,256]{1,0:T(8,128)(2,1)S(1)} %get-tuple-element.32), channel_id=1, source_target_pairs={{0,16},{8,760},{16,32},{24,8},{32,48},{40,24},{48,64},{56,40},{64,... | collective-permute-start | bytes 98312 | tf_op jit(solution)/shard_map/ppermute | solution.py:248
  76.2 10.1 %collective-permute-start.6 = (bf16[32,256]{1,0:T(8,128)(2,1)S(1)}, bf16[32,256]{1,0:T(8,128)(2,1)S(1)}, u32[]{:S(2)}, u32[]{:S(2)}) collective-permute-start(bf16[32,256]{1,0:T(8,128)(2,1)S(1)} %get-tuple-element.33), channel_id=1, source_target_pairs={{0,8},{8,0},{16,24},{24,16},{32,40},{40,32},{48,56},{56,48},{64,72... | collective-permute-start | bytes 49160 | tf_op jit(solution)/shard_map/ppermute | solution.py:251
  78.2 8.2 %collective-permute-start.4 = (f32[4]{0:T(128)S(1)}, f32[4]{0:T(128)S(1)}, u32[]{:S(2)}, u32[]{:S(2)}) collective-permute-start(f32[4]{0:T(128)S(1)} %copy-done.3), channel_id=1, source_target_pairs={{0,752},{8,24},{16,0},{24,40},{32,16},{40,56},{48,32},{56,72},{64,... | collective-permute-start | bytes 56 | tf_op jit(solution)/shard_map/ppermute | solution.py:248

commit v9 on v7

--- a/solution.py
+++ b/solution.py
@@ -313,7 +313,7 @@
     )(occ_count, f_energy, sums, gaps, message, extra)
     amps = lax.all_to_all(amps, "grp", 0, 0)
 
-    tiles = 8
+    tiles = 4
     return pl.pallas_call(
         gamma_kernel,
         in_specs=[SM] + [VM] * 6,

time: 113 us -> 113 us (level)
  no operation moved by 1% of the time
where the time goes in v9:
time: 113 us
  blocking collectives  58.9 us (52%)
  starting transfers between devices  30.2 us (27%)
  waiting for transfers between devices  11.7 us (10%)
  Pallas kernels  8.98 us (8%)
  local copies, waits for them, and re-layouts  2.7 us (2%)
    all_to_all x1, blocking collectives, per_device(): pieces = lax.all_to_all(partial_sums, 'grp', 0, 0)  34.8 us
    all_to_all x1, blocking collectives, per_device(): amps = lax.all_to_all(amps, 'grp', 0, 0)  24.1 us
    ppermute x4, starting transfers between devices, across(): return lax.ppermute(value, 'blk', pairs)  20.8 us
    ppermute x4, waiting for transfers between devices, across(): return lax.ppermute(value, 'blk', pairs)  10.6 us
    ppermute x4, starting transfers between devices, swap(): return lax.ppermute(value, 'blk', [(i, i ^ 1) for i in range(slabs)])  9.39 us
    pallas_call x1, Pallas kernels, per_device(): pl.pallas_call(gamma_kernel, in_specs=[SM] + [VM] * 6, out_specs=ANY, out...  4.6 us
    pallas_call x1, Pallas kernels, per_device(): pl.pallas_call(prep_kernel, in_specs=[SM, SM, SM, VM, VM, VM, VM], out_sp...  2.74 us
  transfers between devices with their start and end apart: 8, of which 3 were waited for; matrix products, arithmetic and copies ran while one was open for 1% of the time, Pallas kernels for 3%

profile of v9, /device:TPU:8, one launch (start us, length us, event | category | flops | bytes accessed | tf_op | source)
XLA Modules:
  0.0 112.6 jit_solution(17867433335312880408)
XLA Ops:
  0.0 1.9 %collective-permute-start.1 = (bf16[2944,256]{1,0:T(8,128)(2,1)}, bf16[2944,256]{1,0:T(8,128)(2,1)S(1)}, u32[]{:S(2)}, u32[]{:S(2)}) collective-permute-start(bf16[2944,256]{1,0:T(8,128)(2,1)} %o_ref.1), channel_id=1, source_target_pairs={{0,8},{8,0},{16,24},{24,16},{32,40},{40,32},{48,56},{56,48},{64,72... | collective-permute-start | bytes 4521992 | tf_op jit(solution)/shard_map/ppermute | solution.py:251
  1.9 14.5 %collective-permute-start.3 = (bf16[2944,256]{1,0:T(8,128)(2,1)}, bf16[2944,256]{1,0:T(8,128)(2,1)S(1)}, u32[]{:S(2)}, u32[]{:S(2)}) collective-permute-start(bf16[2944,256]{1,0:T(8,128)(2,1)} %o_ref.1), channel_id=1, source_target_pairs={{0,752},{8,24},{16,0},{24,40},{32,16},{40,56},{48,32},{56,72},{64,... | collective-permute-start | bytes 4521992 | tf_op jit(solution)/shard_map/ppermute | solution.py:248
  16.4 1.9 %collective-permute-start = (f32[4]{0:T(128)}, f32[4]{0:T(128)S(1)}, u32[]{:S(2)}, u32[]{:S(2)}) collective-permute-start(f32[4]{0:T(128)} %energy_ref.1), channel_id=1, source_target_pairs={{0,8},{8,0},{16,24},{24,16},{32,40},{40,32},{48,56},{56,48},{64,72... | collective-permute-start | bytes 56 | tf_op jit(solution)/shard_map/ppermute | solution.py:251
  18.3 2.5 %collective-permute-start.2 = (f32[4]{0:T(128)}, f32[4]{0:T(128)S(1)}, u32[]{:S(2)}, u32[]{:S(2)}) collective-permute-start(f32[4]{0:T(128)} %energy_ref.1), channel_id=1, source_target_pairs={{0,752},{8,24},{16,0},{24,40},{32,16},{40,56},{48,32},{56,72},{64,... | collective-permute-start | bytes 56 | tf_op jit(solution)/shard_map/ppermute | solution.py:248
  20.8 0.0 collective-permute-done.other_ref
  20.8 0.0 collective-permute-done.1.p_ref
  20.8 0.7 broadcast_in_dim.10.vir_rows_ref
  21.6 0.0 copy-start
  21.6 0.7 copy-done
  22.2 0.0 copy-start.1
  22.2 0.7 copy-done.1
  22.9 0.0 copy-start.3
  22.9 0.7 copy-done.3
  23.5 2.7 %prep.1 = (bf16[256,2944]{1,0:T(8,128)(2,1)S(1)}, bf16[256,2944]{1,0:T(8,128)(2,1)S(1)}, bf16[8,48,256]{2,1,0:T(8,128)(2,1)S(1)}, f32[56,256]{1,0:T(8,128)S(1)}, bf16[16,256]{1,0:T(8,128)(2,1)S(1)}) custom-call(s32[8]{0:T(128)S(1)} %copy-done.1, f32[4]{0:T(128)S(1)} %copy-done.3, f32[4]{0:T(128)S(1)} %collective-permute-done.other_ref, f32[1,64]{1,0:T(1,128)S(1)} %bitcast.1, ...), custom_call_target="tpu_custom_call" | custom-call | flops 578813952 | bytes 6029312 | tf_op jit(solution)/shard_map/prep/pallas_call | solution.py:262
  26.3 7.7 %collective-permute-done.2.refs_1_ = f32[4]{0:T(128)S(1)} collective-permute-done((f32[4]{0:T(128)}, f32[4]{0:T(128)S(1)}, u32[]{:S(2)}, u32[]{:S(2)}) %collective-permute-start.2) | collective-permute-done | bytes 48 | tf_op jit(solution)/shard_map/ppermute | solution.py:248
  33.9 1.9 %collective-permute-start.4 = (bf16[2944,256]{1,0:T(8,128)(2,1)}, bf16[2944,256]{1,0:T(8,128)(2,1)S(1)}, u32[]{:S(2)}, u32[]{:S(2)}) collective-permute-start(bf16[2944,256]{1,0:T(8,128)(2,1)} %o_ref.1), channel_id=1, source_target_pairs={{0,16},{8,760},{16,32},{24,8},{32,48},{40,24},{48,64},{56,40},{64,... | collective-permute-start | bytes 4521992 | tf_op jit(solution)/shard_map/ppermute | solution.py:248
  35.8 0.0 collective-permute-done.3.f_ref
  35.9 3.6 %collective-permute-start.5 = (bf16[2944,256]{1,0:T(8,128)(2,1)S(1)}, bf16[2944,256]{1,0:T(8,128)(2,1)S(1)}, u32[]{:S(2)}, u32[]{:S(2)}) collective-permute-start(bf16[2944,256]{1,0:T(8,128)(2,1)S(1)} %collective-permute-done.3.f_ref), channel_id=1, source_target_pairs={{0,8},{8,0},{16,24},{24,16},{32,40},{40,32},{48,56},{56,48},{64,72... | collective-permute-start | bytes 4521992 | tf_op jit(solution)/shard_map/ppermute | solution.py:251
  39.5 0.0 copy-start.2
  39.5 1.0 far.1
  40.5 34.8 %all_to_all.10.parts_ref = bf16[8,96,256]{2,1,0:T(8,128)(2,1)S(1)} all-to-all(bf16[8,96,256]{2,1,0:T(8,128)(2,1)S(1)} %far.1), channel_id=1, replica_groups=mesh['blk'=96,'grp'=8] {'grp'}, dimensions={0} | all-to-all | bytes 786432 | tf_op jit(solution)/shard_map/all_to_all | solution.py:289
  75.3 0.1 pack.1
  75.3 0.0 collective-permute-done.4.s_ref
  75.3 0.0 collective-permute-done.5.x_ref
  75.3 1.9 %collective-permute-start.6 = (bf16[64,256]{1,0:T(8,128)(2,1)S(1)}, bf16[64,256]{1,0:T(8,128)(2,1)S(1)}, u32[]{:S(2)}, u32[]{:S(2)}) collective-permute-start(bf16[64,256]{1,0:T(8,128)(2,1)S(1)} %get-tuple-element.29), channel_id=1, source_target_pairs={{0,16},{8,760},{16,32},{24,8},{32,48},{40,24},{48,64},{56,40},{64,... | collective-permute-start | bytes 98312 | tf_op jit(solution)/shard_map/ppermute | solution.py:248
  77.3 1.9 %collective-permute-start.7 = (bf16[32,256]{1,0:T(8,128)(2,1)S(1)}, bf16[32,256]{1,0:T(8,128)(2,1)S(1)}, u32[]{:S(2)}, u32[]{:S(2)}) collective-permute-start(bf16[32,256]{1,0:T(8,128)(2,1)S(1)} %get-tuple-element.30), channel_id=1, source_target_pairs={{0,8},{8,0},{16,24},{24,16},{32,40},{40,32},{48,56},{56,48},{64,72... | collective-permute-start | bytes 49160 | tf_op jit(solution)/shard_map/ppermute | solution.py:251
  79.2 1.1 %collective-permute-done.7.refs_5_ = bf16[32,256]{1,0:T(8,128)(2,1)S(1)} collective-permute-done((bf16[32,256]{1,0:T(8,128)(2,1)S(1)}, bf16[32,256]{1,0:T(8,128)(2,1)S(1)}, u32[]{:S(2)}, u32[]{:S(2)}) %collective-permute-start.7) | collective-permute-done | bytes 16416 | tf_op jit(solution)/shard_map/ppermute | solution.py:251
  80.3 2.9 %collective-permute-done.6.refs_4_ = bf16[64,256]{1,0:T(8,128)(2,1)S(1)} collective-permute-done((bf16[64,256]{1,0:T(8,128)(2,1)S(1)}, bf16[64,256]{1,0:T(8,128)(2,1)S(1)}, u32[]{:S(2)}, u32[]{:S(2)}) %collective-permute-start.6) | collective-permute-done | bytes 32800 | tf_op jit(solution)/shard_map/ppermute | solution.py:248
  83.3 0.0 copy-done.2
  83.3 0.6 amplitude.1
  83.9 24.1 %all_to_all.11.amps_ref = bf16[8,5,32,256]{3,2,1,0:T(8,128)(2,1)S(1)} all-to-all(bf16[8,5,32,256]{3,2,1,0:T(8,128)(2,1)S(1)} %amplitude.1), channel_id=1, replica_groups=mesh['blk'=96,'grp'=8] {'grp'}, dimensions={0} | all-to-all | bytes 1310720 | tf_op jit(solution)/shard_map/all_to_all | solution.py:314
  108.0 4.6 %gamma.1 = bf16[2944,256]{1,0:T(8,128)(2,1)} custom-call(s32[8]{0:T(128)S(1)} %copy-done.1, bf16[8,5,32,256]{3,2,1,0:T(8,128)(2,1)S(1)} %all_to_all.11.amps_ref, bf16[2944,256]{1,0:T(8,128)(2,1)} %o_ref.1, bf16[2944,256]{1,0:T(8,128)(2,1)S(1)} %collective-permute-done.1.p_ref, bf16[2944,256]{1,0:T(8,128)(2,1)S(1)} %collective-permute-done.3.f_ref, ...), custom_call_target="tpu_custom_call" | custom-call | flops 1929379840 | bytes 10551296 | tf_op jit(solution)/shard_map/gamma/pallas_call | solution.py:317
Async XLA Ops:
  0.0 20.8 %collective-permute-start.1 = (bf16[2944,256]{1,0:T(8,128)(2,1)}, bf16[2944,256]{1,0:T(8,128)(2,1)S(1)}, u32[]{:S(2)}, u32[]{:S(2)}) collective-permute-start(bf16[2944,256]{1,0:T(8,128)(2,1)} %o_ref.1), channel_id=1, source_target_pairs={{0,8},{8,0},{16,24},{24,16},{32,40},{40,32},{48,56},{56,48},{64,72... | collective-permute-start | bytes 4521992 | tf_op jit(solution)/shard_map/ppermute | solution.py:251
  1.9 33.9 %collective-permute-start.3 = (bf16[2944,256]{1,0:T(8,128)(2,1)}, bf16[2944,256]{1,0:T(8,128)(2,1)S(1)}, u32[]{:S(2)}, u32[]{:S(2)}) collective-permute-start(bf16[2944,256]{1,0:T(8,128)(2,1)} %o_ref.1), channel_id=1, source_target_pairs={{0,752},{8,24},{16,0},{24,40},{32,16},{40,56},{48,32},{56,72},{64,... | collective-permute-start | bytes 4521992 | tf_op jit(solution)/shard_map/ppermute | solution.py:248
  16.4 4.4 %collective-permute-start = (f32[4]{0:T(128)}, f32[4]{0:T(128)S(1)}, u32[]{:S(2)}, u32[]{:S(2)}) collective-permute-start(f32[4]{0:T(128)} %energy_ref.1), channel_id=1, source_target_pairs={{0,8},{8,0},{16,24},{24,16},{32,40},{40,32},{48,56},{56,48},{64,72... | collective-permute-start | bytes 56 | tf_op jit(solution)/shard_map/ppermute | solution.py:251
  18.3 15.6 %collective-permute-start.2 = (f32[4]{0:T(128)}, f32[4]{0:T(128)S(1)}, u32[]{:S(2)}, u32[]{:S(2)}) collective-permute-start(f32[4]{0:T(128)} %energy_ref.1), channel_id=1, source_target_pairs={{0,752},{8,24},{16,0},{24,40},{32,16},{40,56},{48,32},{56,72},{64,... | collective-permute-start | bytes 56 | tf_op jit(solution)/shard_map/ppermute | solution.py:248
  21.6 0.7 copy-start
  22.2 0.7 copy-start.1
  22.9 0.7 copy-start.3
  33.9 41.4 %collective-permute-start.4 = (bf16[2944,256]{1,0:T(8,128)(2,1)}, bf16[2944,256]{1,0:T(8,128)(2,1)S(1)}, u32[]{:S(2)}, u32[]{:S(2)}) collective-permute-start(bf16[2944,256]{1,0:T(8,128)(2,1)} %o_ref.1), channel_id=1, source_target_pairs={{0,16},{8,760},{16,32},{24,8},{32,48},{40,24},{48,64},{56,40},{64,... | collective-permute-start | bytes 4521992 | tf_op jit(solution)/shard_map/ppermute | solution.py:248
  35.9 39.5 %collective-permute-start.5 = (bf16[2944,256]{1,0:T(8,128)(2,1)S(1)}, bf16[2944,256]{1,0:T(8,128)(2,1)S(1)}, u32[]{:S(2)}, u32[]{:S(2)}) collective-permute-start(bf16[2944,256]{1,0:T(8,128)(2,1)S(1)} %collective-permute-done.3.f_ref), channel_id=1, source_target_pairs={{0,8},{8,0},{16,24},{24,16},{32,40},{40,32},{48,56},{56,48},{64,72... | collective-permute-start | bytes 4521992 | tf_op jit(solution)/shard_map/ppermute | solution.py:251
  39.5 43.8 %copy-start.2 = (s32[96]{0:T(128)S(1)}, s32[96]{0:T(128)}, u32[]{:S(2)}) copy-start(s32[96]{0:T(128)} %refs_0_.1) | copy-start | bytes 1156
  75.3 7.9 %collective-permute-start.6 = (bf16[64,256]{1,0:T(8,128)(2,1)S(1)}, bf16[64,256]{1,0:T(8,128)(2,1)S(1)}, u32[]{:S(2)}, u32[]{:S(2)}) collective-permute-start(bf16[64,256]{1,0:T(8,128)(2,1)S(1)} %get-tuple-element.29), channel_id=1, source_target_pairs={{0,16},{8,760},{16,32},{24,8},{32,48},{40,24},{48,64},{56,40},{64,... | collective-permute-start | bytes 98312 | tf_op jit(solution)/shard_map/ppermute | solution.py:248
  77.3 3.1 %collective-permute-start.7 = (bf16[32,256]{1,0:T(8,128)(2,1)S(1)}, bf16[32,256]{1,0:T(8,128)(2,1)S(1)}, u32[]{:S(2)}, u32[]{:S(2)}) collective-permute-start(bf16[32,256]{1,0:T(8,128)(2,1)S(1)} %get-tuple-element.30), channel_id=1, source_target_pairs={{0,8},{8,0},{16,24},{24,16},{32,40},{40,32},{48,56},{56,48},{64,72... | collective-permute-start | bytes 49160 | tf_op jit(solution)/shard_map/ppermute | solution.py:251

commit v10 on v7

--- a/solution.py
+++ b/solution.py
@@ -298,10 +298,10 @@
         compiler_params=memory(6),
         name="pack",
     )(pieces, head)
-    fifth = swap(f_block)
-    message, s_block, fifth = lax.optimization_barrier((message, s_block, fifth))
+    message, s_block, f_later = lax.optimization_barrier((message, s_block, f_block))
     message = across(message, 2)
     extra = swap(extra)
+    fifth = swap(f_later)
     amps = pl.pallas_call(
         lambda *refs: amplitude_kernel(nv, *refs),
         in_specs=[SM, SM] + [VM] * 4,
@@ -311,6 +311,7 @@
         compiler_params=memory(6),
         name="amplitude",
     )(occ_count, f_energy, sums, gaps, message, extra)
+    amps, fifth = lax.optimization_barrier((amps, fifth))
     amps = lax.all_to_all(amps, "grp", 0, 0)
 
     tiles = 8

time: 113 us -> 115 us (1.018)
  blocking collectives: 58.9 us -> 62.8 us
  starting transfers between devices: 30.2 us -> 28.9 us
    all_to_all x1, blocking collectives: 34.8 us -> 38.4 us  [per_device(): pieces = lax.all_to_all(partial_sums, 'grp', 0, 0)]
    ppermute x4, starting transfers between devices: 9.39 us -> 8.16 us  [swap(): return lax.ppermute(value, 'blk', [(i, i ^ 1) for i in range(slabs)])]
  transfers between devices with their start and end apart: 8 -> 8, of which waited for: 3 -> 3; matrix products, arithmetic and copies ran while one was open for 1% -> 1% of each run, Pallas kernels for 3% -> 4%
where the time goes in v10:
time: 115 us
  blocking collectives  62.8 us (55%)
  starting transfers between devices  28.9 us (25%)
  waiting for transfers between devices  11.2 us (10%)
  Pallas kernels  8.87 us (8%)
  local copies, waits for them, and re-layouts  2.7 us (2%)
    all_to_all x1, blocking collectives, per_device(): pieces = lax.all_to_all(partial_sums, 'grp', 0, 0)  38.4 us
    all_to_all x1, blocking collectives, per_device(): amps = lax.all_to_all(amps, 'grp', 0, 0)  24.5 us
    ppermute x4, starting transfers between devices, across(): return lax.ppermute(value, 'blk', pairs)  20.8 us
    ppermute x4, waiting for transfers between devices, across(): return lax.ppermute(value, 'blk', pairs)  10.4 us
    ppermute x4, starting transfers between devices, swap(): return lax.ppermute(value, 'blk', [(i, i ^ 1) for i in range(slabs)])  8.16 us
    pallas_call x1, Pallas kernels, per_device(): pl.pallas_call(gamma_kernel, in_specs=[SM] + [VM] * 6, out_specs=ANY, out...  4.5 us
    pallas_call x1, Pallas kernels, per_device(): pl.pallas_call(prep_kernel, in_specs=[SM, SM, SM, VM, VM, VM, VM], out_sp...  2.74 us
  transfers between devices with their start and end apart: 8, of which 3 were waited for; matrix products, arithmetic and copies ran while one was open for 1% of the time, Pallas kernels for 4%

profile of v10, /device:TPU:8, one launch (start us, length us, event | category | flops | bytes accessed | tf_op | source)
XLA Modules:
  0.0 114.7 jit_solution(4831320746545261516)
XLA Ops:
  0.0 1.9 %collective-permute-start.1 = (bf16[2944,256]{1,0:T(8,128)(2,1)}, bf16[2944,256]{1,0:T(8,128)(2,1)S(1)}, u32[]{:S(2)}, u32[]{:S(2)}) collective-permute-start(bf16[2944,256]{1,0:T(8,128)(2,1)} %o_ref.1), channel_id=1, source_target_pairs={{0,8},{8,0},{16,24},{24,16},{32,40},{40,32},{48,56},{56,48},{64,72... | collective-permute-start | bytes 4521992 | tf_op jit(solution)/shard_map/ppermute | solution.py:251
  1.9 14.5 %collective-permute-start.3 = (bf16[2944,256]{1,0:T(8,128)(2,1)}, bf16[2944,256]{1,0:T(8,128)(2,1)S(1)}, u32[]{:S(2)}, u32[]{:S(2)}) collective-permute-start(bf16[2944,256]{1,0:T(8,128)(2,1)} %o_ref.1), channel_id=1, source_target_pairs={{0,752},{8,24},{16,0},{24,40},{32,16},{40,56},{48,32},{56,72},{64,... | collective-permute-start | bytes 4521992 | tf_op jit(solution)/shard_map/ppermute | solution.py:248
  16.4 1.9 %collective-permute-start = (f32[4]{0:T(128)}, f32[4]{0:T(128)S(1)}, u32[]{:S(2)}, u32[]{:S(2)}) collective-permute-start(f32[4]{0:T(128)} %energy_ref.1), channel_id=1, source_target_pairs={{0,8},{8,0},{16,24},{24,16},{32,40},{40,32},{48,56},{56,48},{64,72... | collective-permute-start | bytes 56 | tf_op jit(solution)/shard_map/ppermute | solution.py:251
  18.3 2.5 %collective-permute-start.2 = (f32[4]{0:T(128)}, f32[4]{0:T(128)S(1)}, u32[]{:S(2)}, u32[]{:S(2)}) collective-permute-start(f32[4]{0:T(128)} %energy_ref.1), channel_id=1, source_target_pairs={{0,752},{8,24},{16,0},{24,40},{32,16},{40,56},{48,32},{56,72},{64,... | collective-permute-start | bytes 56 | tf_op jit(solution)/shard_map/ppermute | solution.py:248
  20.8 0.0 collective-permute-done.other_ref
  20.8 0.0 collective-permute-done.1.p_ref
  20.8 0.7 broadcast_in_dim.10.vir_rows_ref
  21.6 0.0 copy-start
  21.6 0.7 copy-done
  22.2 0.0 copy-start.1
  22.2 0.7 copy-done.1
  22.9 0.0 copy-start.3
  22.9 0.7 copy-done.3
  23.5 2.7 %prep.1 = (bf16[256,2944]{1,0:T(8,128)(2,1)S(1)}, bf16[256,2944]{1,0:T(8,128)(2,1)S(1)}, bf16[8,48,256]{2,1,0:T(8,128)(2,1)S(1)}, f32[56,256]{1,0:T(8,128)S(1)}, bf16[16,256]{1,0:T(8,128)(2,1)S(1)}) custom-call(s32[8]{0:T(128)S(1)} %copy-done.1, f32[4]{0:T(128)S(1)} %copy-done.3, f32[4]{0:T(128)S(1)} %collective-permute-done.other_ref, f32[1,64]{1,0:T(1,128)S(1)} %bitcast.1, ...), custom_call_target="tpu_custom_call" | custom-call | flops 578813952 | bytes 6029312 | tf_op jit(solution)/shard_map/prep/pallas_call | solution.py:262
  26.3 7.7 %collective-permute-done.2.refs_1_ = f32[4]{0:T(128)S(1)} collective-permute-done((f32[4]{0:T(128)}, f32[4]{0:T(128)S(1)}, u32[]{:S(2)}, u32[]{:S(2)}) %collective-permute-start.2) | collective-permute-done | bytes 48 | tf_op jit(solution)/shard_map/ppermute | solution.py:248
  33.9 1.9 %collective-permute-start.4 = (bf16[2944,256]{1,0:T(8,128)(2,1)}, bf16[2944,256]{1,0:T(8,128)(2,1)S(1)}, u32[]{:S(2)}, u32[]{:S(2)}) collective-permute-start(bf16[2944,256]{1,0:T(8,128)(2,1)} %o_ref.1), channel_id=1, source_target_pairs={{0,16},{8,760},{16,32},{24,8},{32,48},{40,24},{48,64},{56,40},{64,... | collective-permute-start | bytes 4521992 | tf_op jit(solution)/shard_map/ppermute | solution.py:248
  35.8 0.0 collective-permute-done.3.f_ref
  35.9 0.0 copy-start.2
  35.9 0.9 far.1
  36.8 38.4 %all_to_all.10.parts_ref = bf16[8,96,256]{2,1,0:T(8,128)(2,1)S(1)} all-to-all(bf16[8,96,256]{2,1,0:T(8,128)(2,1)S(1)} %far.1), channel_id=1, replica_groups=mesh['blk'=96,'grp'=8] {'grp'}, dimensions={0} | all-to-all | bytes 786432 | tf_op jit(solution)/shard_map/all_to_all | solution.py:289
  75.2 0.1 pack.1
  75.2 0.0 collective-permute-done.4.s_ref
  75.3 1.9 %collective-permute-start.7 = (bf16[2944,256]{1,0:T(8,128)(2,1)S(1)}, bf16[2944,256]{1,0:T(8,128)(2,1)S(1)}, u32[]{:S(2)}, u32[]{:S(2)}) collective-permute-start(bf16[2944,256]{1,0:T(8,128)(2,1)S(1)} %collective-permute-done.3.f_ref), channel_id=1, source_target_pairs={{0,8},{8,0},{16,24},{24,16},{32,40},{40,32},{48,56},{56,48},{64,72... | collective-permute-start | bytes 4521992 | tf_op jit(solution)/shard_map/ppermute | solution.py:251
  77.2 1.9 %collective-permute-start.5 = (bf16[64,256]{1,0:T(8,128)(2,1)S(1)}, bf16[64,256]{1,0:T(8,128)(2,1)S(1)}, u32[]{:S(2)}, u32[]{:S(2)}) collective-permute-start(bf16[64,256]{1,0:T(8,128)(2,1)S(1)} %get-tuple-element.31), channel_id=1, source_target_pairs={{0,16},{8,760},{16,32},{24,8},{32,48},{40,24},{48,64},{56,40},{64,... | collective-permute-start | bytes 98312 | tf_op jit(solution)/shard_map/ppermute | solution.py:248
  79.1 2.4 %collective-permute-start.6 = (bf16[32,256]{1,0:T(8,128)(2,1)S(1)}, bf16[32,256]{1,0:T(8,128)(2,1)S(1)}, u32[]{:S(2)}, u32[]{:S(2)}) collective-permute-start(bf16[32,256]{1,0:T(8,128)(2,1)S(1)} %get-tuple-element.32), channel_id=1, source_target_pairs={{0,8},{8,0},{16,24},{24,16},{32,40},{40,32},{48,56},{56,48},{64,72... | collective-permute-start | bytes 49160 | tf_op jit(solution)/shard_map/ppermute | solution.py:251
  81.5 0.8 collective-permute-done.6.refs_5_
  82.3 2.8 %collective-permute-done.5.refs_4_ = bf16[64,256]{1,0:T(8,128)(2,1)S(1)} collective-permute-done((bf16[64,256]{1,0:T(8,128)(2,1)S(1)}, bf16[64,256]{1,0:T(8,128)(2,1)S(1)}, u32[]{:S(2)}, u32[]{:S(2)}) %collective-permute-start.5) | collective-permute-done | bytes 32800 | tf_op jit(solution)/shard_map/ppermute | solution.py:248
  85.1 0.0 copy-done.2
  85.1 0.6 amplitude.1
  85.7 0.0 collective-permute-done.7.x_ref
  85.7 24.5 %all_to_all.11.amps_ref = bf16[8,5,32,256]{3,2,1,0:T(8,128)(2,1)S(1)} all-to-all(bf16[8,5,32,256]{3,2,1,0:T(8,128)(2,1)S(1)} %amplitude.1), channel_id=1, replica_groups=mesh['blk'=96,'grp'=8] {'grp'}, dimensions={0} | all-to-all | bytes 1310720 | tf_op jit(solution)/shard_map/all_to_all | solution.py:315
  110.2 4.5 %gamma.1 = bf16[2944,256]{1,0:T(8,128)(2,1)} custom-call(s32[8]{0:T(128)S(1)} %copy-done.1, bf16[8,5,32,256]{3,2,1,0:T(8,128)(2,1)S(1)} %all_to_all.11.amps_ref, bf16[2944,256]{1,0:T(8,128)(2,1)} %o_ref.1, bf16[2944,256]{1,0:T(8,128)(2,1)S(1)} %collective-permute-done.1.p_ref, bf16[2944,256]{1,0:T(8,128)(2,1)S(1)} %collective-permute-done.3.f_ref, ...), custom_call_target="tpu_custom_call" | custom-call | flops 1929379840 | bytes 10551296 | tf_op jit(solution)/shard_map/gamma/pallas_call | solution.py:318
Async XLA Ops:
  0.0 20.8 %collective-permute-start.1 = (bf16[2944,256]{1,0:T(8,128)(2,1)}, bf16[2944,256]{1,0:T(8,128)(2,1)S(1)}, u32[]{:S(2)}, u32[]{:S(2)}) collective-permute-start(bf16[2944,256]{1,0:T(8,128)(2,1)} %o_ref.1), channel_id=1, source_target_pairs={{0,8},{8,0},{16,24},{24,16},{32,40},{40,32},{48,56},{56,48},{64,72... | collective-permute-start | bytes 4521992 | tf_op jit(solution)/shard_map/ppermute | solution.py:251
  1.9 33.9 %collective-permute-start.3 = (bf16[2944,256]{1,0:T(8,128)(2,1)}, bf16[2944,256]{1,0:T(8,128)(2,1)S(1)}, u32[]{:S(2)}, u32[]{:S(2)}) collective-permute-start(bf16[2944,256]{1,0:T(8,128)(2,1)} %o_ref.1), channel_id=1, source_target_pairs={{0,752},{8,24},{16,0},{24,40},{32,16},{40,56},{48,32},{56,72},{64,... | collective-permute-start | bytes 4521992 | tf_op jit(solution)/shard_map/ppermute | solution.py:248
  16.4 4.4 %collective-permute-start = (f32[4]{0:T(128)}, f32[4]{0:T(128)S(1)}, u32[]{:S(2)}, u32[]{:S(2)}) collective-permute-start(f32[4]{0:T(128)} %energy_ref.1), channel_id=1, source_target_pairs={{0,8},{8,0},{16,24},{24,16},{32,40},{40,32},{48,56},{56,48},{64,72... | collective-permute-start | bytes 56 | tf_op jit(solution)/shard_map/ppermute | solution.py:251
  18.3 15.6 %collective-permute-start.2 = (f32[4]{0:T(128)}, f32[4]{0:T(128)S(1)}, u32[]{:S(2)}, u32[]{:S(2)}) collective-permute-start(f32[4]{0:T(128)} %energy_ref.1), channel_id=1, source_target_pairs={{0,752},{8,24},{16,0},{24,40},{32,16},{40,56},{48,32},{56,72},{64,... | collective-permute-start | bytes 56 | tf_op jit(solution)/shard_map/ppermute | solution.py:248
  21.6 0.7 copy-start
  22.2 0.7 copy-start.1
  22.9 0.7 copy-start.3
  33.9 41.3 %collective-permute-start.4 = (bf16[2944,256]{1,0:T(8,128)(2,1)}, bf16[2944,256]{1,0:T(8,128)(2,1)S(1)}, u32[]{:S(2)}, u32[]{:S(2)}) collective-permute-start(bf16[2944,256]{1,0:T(8,128)(2,1)} %o_ref.1), channel_id=1, source_target_pairs={{0,16},{8,760},{16,32},{24,8},{32,48},{40,24},{48,64},{56,40},{64,... | collective-permute-start | bytes 4521992 | tf_op jit(solution)/shard_map/ppermute | solution.py:248
  35.9 49.2 %copy-start.2 = (s32[96]{0:T(128)S(1)}, s32[96]{0:T(128)}, u32[]{:S(2)}) copy-start(s32[96]{0:T(128)} %refs_0_.1) | copy-start | bytes 1156
  75.3 10.5 %collective-permute-start.7 = (bf16[2944,256]{1,0:T(8,128)(2,1)S(1)}, bf16[2944,256]{1,0:T(8,128)(2,1)S(1)}, u32[]{:S(2)}, u32[]{:S(2)}) collective-permute-start(bf16[2944,256]{1,0:T(8,128)(2,1)S(1)} %collective-permute-done.3.f_ref), channel_id=1, source_target_pairs={{0,8},{8,0},{16,24},{24,16},{32,40},{40,32},{48,56},{56,48},{64,72... | collective-permute-start | bytes 4521992 | tf_op jit(solution)/shard_map/ppermute | solution.py:251
  77.2 7.9 %collective-permute-start.5 = (bf16[64,256]{1,0:T(8,128)(2,1)S(1)}, bf16[64,256]{1,0:T(8,128)(2,1)S(1)}, u32[]{:S(2)}, u32[]{:S(2)}) collective-permute-start(bf16[64,256]{1,0:T(8,128)(2,1)S(1)} %get-tuple-element.31), channel_id=1, source_target_pairs={{0,16},{8,760},{16,32},{24,8},{32,48},{40,24},{48,64},{56,40},{64,... | collective-permute-start | bytes 98312 | tf_op jit(solution)/shard_map/ppermute | solution.py:248
  79.1 3.2 %collective-permute-start.6 = (bf16[32,256]{1,0:T(8,128)(2,1)S(1)}, bf16[32,256]{1,0:T(8,128)(2,1)S(1)}, u32[]{:S(2)}, u32[]{:S(2)}) collective-permute-start(bf16[32,256]{1,0:T(8,128)(2,1)S(1)} %get-tuple-element.32), channel_id=1, source_target_pairs={{0,8},{8,0},{16,24},{24,16},{32,40},{40,32},{48,56},{56,48},{64,72... | collective-permute-start | bytes 49160 | tf_op jit(solution)/shard_map/ppermute | solution.py:251
